TPU v7x, 32 devices: a whole 2x2x4 slice. The times are simulated.
32 devices in a mesh: dp: 16 (over z, y, x), mp: 2 (over core).
Axes of the slice: x: 2, y: 2, z: 4, core: 2. Of those that a mesh axis runs over, the one named last changes fastest.
Arguments:
- x_short: bfloat16 [64, 256, 768], P('dp'), may hold values from -6 to 6
- x_long: bfloat16 [32, 512, 768], P('dp'), may hold values from -6 to 6
- len_short: int32 [64], P('dp'), may hold values from 64 to 256, as said below
- len_long: int32 [32], P('dp'), may hold values from 128 to 512, as said below
- boundaries: int32 [15], replicated, may hold values from 1 to 128, as said below
- q_weight: bfloat16 [768, 768], P('dp', 'mp'), may hold values from -0.109375 to 0.109375
- k_weight: bfloat16 [768, 768], P('dp', 'mp'), may hold values from -0.109375 to 0.109375
- v_weight: bfloat16 [768, 768], P('dp', 'mp'), may hold values from -0.21875 to 0.21875
- out_weight: bfloat16 [768, 768], P('dp', 'mp'), may hold values from -0.625 to 0.625
- in_weight: bfloat16 [768, 3072], P('dp', 'mp'), may hold values from -0.21875 to 0.21875
- ff_out_weight: bfloat16 [768, 3072], P('dp', 'mp'), may hold values from -0.15625 to 0.15625
- attn_gain: bfloat16 [768], P('dp'), may hold values from 0.5 to 1.5
- ffn_gain: bfloat16 [768], P('dp'), may hold values from 0.5 to 1.5
- bias_table: bfloat16 [32, 12], P(None, 'mp'), may hold values from -4 to 4
- cot_short: bfloat16 [64, 256, 768], P('dp'), may hold values from -6 to 6
- cot_long: bfloat16 [32, 512, 768], P('dp'), may hold values from -6 to 6
Outputs:
- out_short: bfloat16 [64, 256, 768], P('dp')
- out_long: bfloat16 [32, 512, 768], P('dp')
- grad_short: bfloat16 [64, 256, 768], P('dp')
- grad_long: bfloat16 [32, 512, 768], P('dp')
- grad_q_weight: float32 [768, 768], P('dp', 'mp')
- grad_k_weight: float32 [768, 768], P('dp', 'mp')
- grad_v_weight: float32 [768, 768], P('dp', 'mp')
- grad_out_weight: float32 [768, 768], P('dp', 'mp')
- grad_in_weight: float32 [768, 3072], P('dp', 'mp')
- grad_ff_out_weight: float32 [768, 3072], P('dp', 'mp')
- grad_attn_gain: float32 [768], P('dp')
- grad_ffn_gain: float32 [768], P('dp')
- grad_bias_table: float32 [32, 12], P(None, 'mp')
Inputs may be any that keep to these rules, and one draw needn't show every extreme that they name: `len_short`: valid positions at the head of each slot of 256; the rest is padding. `len_long`: valid positions at the head of each slot of 512; the rest is padding. `boundaries`: strictly increasing thresholds on the distance; the first is 1 and the last 128.
All inputs are finite; a program needn't handle non-finite values.
Results may differ from a plain program's by a relative error of at most 0.02.
Values may be sent and summed in bfloat16 or wider, within the bound.
No kernel may reach another device: no remote copies, remote signals or barrier semaphores. Data moves between devices by JAX's collectives and lax.ppermute only.
A program may use at most 192 MiB of HBM per device.

v0:
```python
import math

import jax
import jax.numpy as jnp
from jax import lax
from jax.sharding import PartitionSpec as P

DH = 64


EPS = 1e-06
NEG = -1000000000.0


def matmul(left, right):
    return jnp.dot(left, right, preferred_element_type=jnp.float32)


def contract_rows(left, right):
    return lax.dot_general(
        left, right, (((0,), (0,)), ((), ())), preferred_element_type=jnp.float32
    )


def contract_cols(left, right):
    return lax.dot_general(
        left, right, (((1,), (1,)), ((), ())), preferred_element_type=jnp.float32
    )


def rms_parts(field):
    scale = lax.rsqrt(jnp.mean(field * field, -1, keepdims=True) + EPS)
    return (scale, field * scale)


def norm_back(grad_unit, unit, scale):
    return scale * (grad_unit - unit * jnp.mean(grad_unit * unit, -1, keepdims=True))


def bucket_table(length, boundaries, buckets):
    places = jnp.arange(length, dtype=jnp.int32)
    dist = places[None, :] - places[:, None]
    half = jnp.sum((jnp.abs(dist)[..., None] >= boundaries).astype(jnp.int32), -1)
    marks = half + buckets // 2 * (dist > 0).astype(jnp.int32)
    labels = jnp.arange(buckets, dtype=jnp.int32)
    return (marks[..., None] == labels).astype(jnp.bfloat16)


def bias_field(table01, table):
    return jnp.einsum("ijb,bh->hij", table01, table, preferred_element_type=jnp.float32)


def bucket_sums(grads, table01):
    return jnp.einsum("ghij,ijb->bh", grads, table01, preferred_element_type=jnp.float32)


def group_count(slots, length):
    return math.gcd(slots, max(1, 512 // length))


def split_groups(array, group):
    return array.reshape((array.shape[0] // group, group) + array.shape[1:])


def project(normed, weight, slots, length):
    return matmul(normed, weight).astype(jnp.bfloat16).reshape(slots, length, -1, DH)


def masked_scores(queries, keys, bias, mask):
    scores = jnp.einsum("gihd,gjhd->ghij", queries, keys, preferred_element_type=jnp.float32) + bias
    return jnp.where(mask[:, None, None, :], scores, NEG)


def forward(x, lengths, weights, table, boundaries):
    q_w, k_w, v_w, o_w, ffn_in_matrix, ffn_out_matrix, gain_a, gain_f = weights
    slots, length, width = x.shape
    rows = slots * length
    field = x.reshape(rows, width).astype(jnp.float32)
    scale_a, unit_a = rms_parts(field)
    normed = (unit_a * gain_a.astype(jnp.float32)).astype(jnp.bfloat16)
    queries = project(normed, q_w, slots, length)
    keys = project(normed, k_w, slots, length)
    values = project(normed, v_w, slots, length)
    bias = bias_field(bucket_table(length, boundaries, table.shape[0]), table)
    valid = jnp.arange(length, dtype=jnp.int32)[None, :] < lengths[:, None]
    group = group_count(slots, length)

    def forward_one(item):
        q_g, k_g, v_g, mask = item
        scores = masked_scores(q_g, k_g, bias, mask)
        top = jnp.max(scores, -1, keepdims=True)
        expo = jnp.exp(scores - top)
        total = jnp.sum(expo, -1, keepdims=True)
        probs = (expo / total).astype(jnp.bfloat16)
        mixed = jnp.einsum("ghij,gjhd->gihd", probs, v_g, preferred_element_type=jnp.float32)
        return (mixed.astype(jnp.bfloat16), (top + jnp.log(total))[..., 0])

    mixed, logsum = lax.map(
        forward_one,
        (
            split_groups(queries, group),
            split_groups(keys, group),
            split_groups(values, group),
            split_groups(valid, group),
        ),
    )
    mixed = mixed.reshape(rows, -1)
    attn_term = contract_cols(mixed, o_w)
    attn = lax.psum(attn_term.astype(jnp.bfloat16), "mp").astype(jnp.float32)
    hidden_activation = field + attn
    scale_f, unit_f = rms_parts(hidden_activation)
    ffn_normed_input = (unit_f * gain_f.astype(jnp.float32)).astype(jnp.bfloat16)
    active_rows = jax.nn.gelu(matmul(ffn_normed_input, ffn_in_matrix), approximate=True).astype(
        jnp.bfloat16
    )
    ffn = lax.psum(contract_cols(active_rows, ffn_out_matrix).astype(jnp.bfloat16), "mp").astype(
        jnp.float32
    )
    out = (hidden_activation + ffn).astype(jnp.bfloat16).reshape(slots, length, width)
    return (out, hidden_activation, None, logsum)


def backward(x, lengths, cotangent, hidden_activation, logsum, weights, table, boundaries):
    q_w, k_w, v_w, o_w, ffn_in_matrix, ffn_out_matrix, gain_a, gain_f = weights
    slots, length, width = x.shape
    rows = slots * length
    grad_out = cotangent.reshape(rows, width)
    scale_f, unit_f = rms_parts(hidden_activation)
    ffn_normed_input = (unit_f * gain_f.astype(jnp.float32)).astype(jnp.bfloat16)
    preactivation = matmul(ffn_normed_input, ffn_in_matrix)
    active_rows, gelu_back = jax.vjp(lambda t: jax.nn.gelu(t, approximate=True), preactivation)
    active_rows = active_rows.astype(jnp.bfloat16)
    grad_f_w = contract_rows(grad_out, active_rows)
    grad_pre = gelu_back(matmul(grad_out, ffn_out_matrix))[0].astype(jnp.bfloat16)
    grad_i_w = contract_rows(ffn_normed_input, grad_pre)
    partial_f = contract_cols(grad_pre, ffn_in_matrix)
    grad_norm_f = lax.psum(partial_f.astype(jnp.bfloat16), "mp").astype(jnp.float32)
    grad_gain_f = jnp.sum(grad_norm_f * unit_f, 0)
    grad_mid = grad_out.astype(jnp.float32) + norm_back(
        grad_norm_f * gain_f.astype(jnp.float32), unit_f, scale_f
    )
    grad_attn = grad_mid.astype(jnp.bfloat16)
    field = x.reshape(rows, width).astype(jnp.float32)
    scale_a, unit_a = rms_parts(field)
    normed = (unit_a * gain_a.astype(jnp.float32)).astype(jnp.bfloat16)
    queries = project(normed, q_w, slots, length)
    keys = project(normed, k_w, slots, length)
    values = project(normed, v_w, slots, length)
    grad_mixed = matmul(grad_attn, o_w).astype(jnp.bfloat16).reshape(slots, length, -1, DH)
    table01 = bucket_table(length, boundaries, table.shape[0])
    bias = bias_field(table01, table)
    valid = jnp.arange(length, dtype=jnp.int32)[None, :] < lengths[:, None]
    group = group_count(slots, length)

    def backward_one(item):
        q_g, k_g, v_g, d_g, mask, lse = item
        scores = masked_scores(q_g, k_g, bias, mask)
        probs = jnp.exp(scores - lse[..., None])
        low_probs = probs.astype(jnp.bfloat16)
        mixed = jnp.einsum(
            "ghij,gjhd->gihd", low_probs, v_g, preferred_element_type=jnp.float32
        ).astype(jnp.bfloat16)
        grad_probs = jnp.einsum("gihd,gjhd->ghij", d_g, v_g, preferred_element_type=jnp.float32)
        grad_v = jnp.einsum(
            "ghij,gihd->gjhd", low_probs, d_g, preferred_element_type=jnp.float32
        ).astype(jnp.bfloat16)
        grad_s = probs * (grad_probs - jnp.sum(probs * grad_probs, -1, keepdims=True))
        grad_s = grad_s.astype(jnp.bfloat16)
        grad_q = jnp.einsum(
            "ghij,gjhd->gihd", grad_s, k_g, preferred_element_type=jnp.float32
        ).astype(jnp.bfloat16)
        grad_k = jnp.einsum(
            "ghij,gihd->gjhd", grad_s, q_g, preferred_element_type=jnp.float32
        ).astype(jnp.bfloat16)
        return (mixed, grad_q, grad_k, grad_v, bucket_sums(grad_s, table01))

    mixed, grad_q, grad_k, grad_v, grad_table = lax.map(
        backward_one,
        (
            split_groups(queries, group),
            split_groups(keys, group),
            split_groups(values, group),
            split_groups(grad_mixed, group),
            split_groups(valid, group),
            logsum,
        ),
    )
    mixed = mixed.reshape(rows, -1)
    grad_q = grad_q.reshape(rows, -1)
    grad_k = grad_k.reshape(rows, -1)
    grad_v = grad_v.reshape(rows, -1)
    grad_o_w = contract_rows(grad_attn, mixed)
    grad_q_w = contract_rows(normed, grad_q)
    grad_k_w = contract_rows(normed, grad_k)
    grad_v_w = contract_rows(normed, grad_v)
    partial_norm = (
        contract_cols(grad_q, q_w) + contract_cols(grad_k, k_w) + contract_cols(grad_v, v_w)
    )
    grad_norm_a = lax.psum(partial_norm.astype(jnp.bfloat16), "mp").astype(jnp.float32)
    grad_gain_a = jnp.sum(grad_norm_a * unit_a, 0)
    grad_x = (
        grad_mid + norm_back(grad_norm_a * gain_a.astype(jnp.float32), unit_a, scale_a)
    ).astype(jnp.bfloat16)
    grads = (grad_q_w, grad_k_w, grad_v_w, grad_o_w, grad_i_w, grad_f_w, grad_gain_a, grad_gain_f)
    return (grad_x.reshape(slots, length, width), grads, jnp.sum(grad_table, 0))


def on_device(
    x_short,
    x_long,
    len_short,
    len_long,
    boundaries,
    q_weight,
    k_weight,
    v_weight,
    out_weight,
    in_weight,
    ff_out_weight,
    attn_gain,
    ffn_gain,
    bias_table,
    cot_short,
    cot_long,
):
    whole = (
        lax.all_gather(q_weight, "dp", axis=0, tiled=True),
        lax.all_gather(k_weight, "dp", axis=0, tiled=True),
        lax.all_gather(v_weight, "dp", axis=0, tiled=True),
        lax.all_gather(out_weight, "dp", axis=0, tiled=True),
        lax.all_gather(in_weight, "dp", axis=0, tiled=True),
        lax.all_gather(ff_out_weight, "dp", axis=0, tiled=True),
        lax.all_gather(attn_gain, "dp", axis=0, tiled=True),
        lax.all_gather(ffn_gain, "dp", axis=0, tiled=True),
    )
    out_short, middle_short, normed_short, logsum_short = forward(
        x_short, len_short, whole, bias_table, boundaries
    )
    out_long, middle_long, normed_long, logsum_long = forward(
        x_long, len_long, whole, bias_table, boundaries
    )
    again = (
        lax.all_gather(q_weight, "dp", axis=0, tiled=True),
        lax.all_gather(k_weight, "dp", axis=0, tiled=True),
        lax.all_gather(v_weight, "dp", axis=0, tiled=True),
        lax.all_gather(out_weight, "dp", axis=0, tiled=True),
        lax.all_gather(in_weight, "dp", axis=0, tiled=True),
        lax.all_gather(ff_out_weight, "dp", axis=0, tiled=True),
        lax.all_gather(attn_gain, "dp", axis=0, tiled=True),
        lax.all_gather(ffn_gain, "dp", axis=0, tiled=True),
    )
    grad_short, grads_s, table_s = backward(
        x_short, len_short, cot_short, middle_short, logsum_short, again, bias_table, boundaries
    )
    grad_long, grads_l, table_l = backward(
        x_long, len_long, cot_long, middle_long, logsum_long, again, bias_table, boundaries
    )
    total = jax.tree.map(lambda a, b: a + b, grads_s, grads_l)
    shares = (
        lax.psum_scatter(total[0], "dp", scatter_dimension=0, tiled=True),
        lax.psum_scatter(total[1], "dp", scatter_dimension=0, tiled=True),
        lax.psum_scatter(total[2], "dp", scatter_dimension=0, tiled=True),
        lax.psum_scatter(total[3], "dp", scatter_dimension=0, tiled=True),
        lax.psum_scatter(total[4], "dp", scatter_dimension=0, tiled=True),
        lax.psum_scatter(total[5], "dp", scatter_dimension=0, tiled=True),
        lax.psum_scatter(total[6], "dp", scatter_dimension=0, tiled=True),
        lax.psum_scatter(total[7], "dp", scatter_dimension=0, tiled=True),
    )
    gain_a_grad, gain_f_grad = (shares[6], shares[7])
    table_grad = lax.psum(table_s + table_l, "dp")
    return (
        out_short,
        out_long,
        grad_short,
        grad_long,
        shares[0],
        shares[1],
        shares[2],
        shares[3],
        shares[4],
        shares[5],
        gain_a_grad,
        gain_f_grad,
        table_grad,
    )


def solution(mesh):
    return jax.shard_map(
        on_device,
        mesh=mesh,
        in_specs=(
            P("dp", None, None),
            P("dp", None, None),
            P("dp"),
            P("dp"),
            P(),
            P("dp", "mp"),
            P("dp", "mp"),
            P("dp", "mp"),
            P("dp", "mp"),
            P("dp", "mp"),
            P("dp", "mp"),
            P("dp"),
            P("dp"),
            P(None, "mp"),
            P("dp", None, None),
            P("dp", None, None),
        ),
        out_specs=(
            P("dp", None, None),
            P("dp", None, None),
            P("dp", None, None),
            P("dp", None, None),
            P("dp", "mp"),
            P("dp", "mp"),
            P("dp", "mp"),
            P("dp", "mp"),
            P("dp", "mp"),
            P("dp", "mp"),
            P("dp"),
            P("dp"),
            P(None, "mp"),
        ),
        check_vma=False,
    )
```

profile of v0, /device:TPU:0, one launch (start us, length us, event | category | flops | bytes accessed | tf_op | source)
XLA Modules:
  0.0 1477.1 jit_solution(6637561046153170051)
XLA Ops:
  13.1 43.5 %all-reduce.5 = (bf16[768]{0:T(1024)(128)(2,1)S(1)}, bf16[768]{0:T(1024)(128)(2,1)S(1)}) all-reduce(bf16[768]{0:T(1024)(128)(2,1)S(1)} %dynamic-update-slice, bf16[768]{0:T(1024)(128)(2,1)S(1)} %dynamic-update-slice.1), channel_id=1, replica_groups=mesh['dp'=16,'mp'=2] {'dp'}, use_global_device_ids=true, to_apply=%add | all-reduce | flops 1536 | bytes 6144
  60.0 38.7 %all_gather.34 = bf16[768,384]{1,0:T(8,128)(2,1)S(1)} all-gather(bf16[48,384]{1,0:T(8,128)(2,1)S(1)} %copy-done.93), channel_id=1, replica_groups=mesh['dp'=16,'mp'=2] {'dp'}, dimensions={0}, use_global_device_ids=true | all-gather | bytes 626688 | tf_op jit(solution)/shard_map/all_gather | solution.py:227
  98.7 41.2 %all_gather.35 = bf16[768,384]{1,0:T(8,128)(2,1)S(1)} all-gather(bf16[48,384]{1,0:T(8,128)(2,1)S(1)} %copy-done.94), channel_id=1, replica_groups=mesh['dp'=16,'mp'=2] {'dp'}, dimensions={0}, use_global_device_ids=true | all-gather | bytes 626688 | tf_op jit(solution)/shard_map/all_gather | solution.py:228
  148.2 39.2 %all_gather.33 = bf16[768,384]{1,0:T(8,128)(2,1)S(1)} all-gather(bf16[48,384]{1,0:T(8,128)(2,1)S(1)} %copy-done.95), channel_id=1, replica_groups=mesh['dp'=16,'mp'=2] {'dp'}, dimensions={0}, use_global_device_ids=true | all-gather | bytes 626688 | tf_op jit(solution)/shard_map/all_gather | solution.py:229
  191.9 42.5 %all_gather.36 = bf16[768,384]{1,0:T(8,128)(2,1)} all-gather(bf16[48,384]{1,0:T(8,128)(2,1)S(1)} %copy-done.96), channel_id=1, replica_groups=mesh['dp'=16,'mp'=2] {'dp'}, dimensions={0}, use_global_device_ids=true | all-gather | bytes 626688 | tf_op jit(solution)/shard_map/all_gather | solution.py:230
  289.6 12.2 while.62
  305.3 7.8 fusion.151
  313.1 9.1 copy.182
  322.3 14.1 while.63
  343.3 18.4 %all-reduce.17.cloned.1.call-done = (bf16[1024,768]{1,0:T(8,128)(2,1)}, bf16[1024,768]{1,0:T(8,128)(2,1)}) async-done(((bf16[1024,768]{1,0:T(8,128)(2,1)}, bf16[1024,768]{1,0:T(8,128)(2,1)}), (bf16[1024,768]{1,0:T(8,128)(2,1)}, bf16[1024,768]{1,0:T(8,128)(2,1)})) %all-reduce.17.cloned.1.call-update) | async-done | bytes 3145744 | tf_op jit(solution)/shard_map/psum | solution.py:109
  367.5 37.0 %all-gather.5.cloned.1.call-done = bf16[768,1536]{1,0:T(8,128)(2,1)} async-done(((bf16[48,1536]{1,0:T(8,128)(2,1)}), bf16[768,1536]{1,0:T(8,128)(2,1)}) %all-gather.5.cloned.1.call-update) | async-done | bytes 2359312 | tf_op jit(solution)/shard_map/all_gather | solution.py:232
  416.6 51.7 %all-gather.3.cloned.1.call-done = bf16[768,1536]{1,0:T(8,128)(2,1)} async-done(((bf16[48,1536]{1,0:T(8,128)(2,1)}), bf16[768,1536]{1,0:T(8,128)(2,1)}) %all-gather.3.cloned.1.call-update) | async-done | bytes 2359312 | tf_op jit(solution)/shard_map/all_gather | solution.py:231
  468.3 10.3 fusion.141
  483.6 7.7 fusion.134
  497.3 8.6 convolution_convert_fusion.10
  534.8 56.1 %while.65 = (s32[]{:T(128)}, bf16[2,1,512,6,64]{2,4,3,1,0:T(8,128)(2,1)}, bf16[2,1,512,6,64]{2,4,3,1,0:T(8,128)(2,1)}, bf16[2,1,512,6,64]{2,4,3,1,0:T(8,128)(2,1...) while((s32[]{:T(128)}, ...), condition=%wide.region_30.31_spmd.clone, body=%wide.region_28.30_spmd.clone.sunk | while | flops 1341912064 | bytes 128524232 | solution.py:177
  609.0 36.5 %while.64 = (s32[]{:T(128)}, bf16[2,2,256,6,64]{2,1,0,4,3:T(2,128)(2,1)}, bf16[2,2,256,6,64]{2,1,0,4,3:T(2,128)(2,1)}, bf16[2,2,256,6,64]{2,1,0,4,3:T(2,128)(2,1...) while((s32[]{:T(128)}, ...), condition=%wide.region_23.24_spmd.clone, body=%wide.region_20.23_spmd.clone.sunk | while | flops 643167232 | bytes 82906184 | solution.py:177
  707.6 8.7 add_bitcast_fusion
  731.9 77.1 %all-reduce.4 = (f32[768]{0:T(1024)S(1)}, f32[768]{0:T(1024)S(1)}, f32[32,6]{0,1:T(8,128)}) all-reduce(f32[768]{0:T(1024)S(1)} %add.269, f32[768]{0:T(1024)S(1)} %add.270, f32[32,6]{0,1:T(8,128)S(1)} %add.271), channel_id=8, replica_groups=mesh['dp'=16,'mp'=2] {'dp'}, use_global_device_ids=true, to_apply=%region_41.42.clone | all-reduce | flops 1728 | bytes 13824
  815.4 112.5 %reduce-scatter.13.cloned.1.call-done = f32[48,384]{1,0:T(8,128)} async-done(((f32[768,384]{1,0:T(8,128)}), f32[48,384]{1,0:T(8,128)}) %reduce-scatter.13.cloned.1.call-update) | async-done | bytes 73744 | tf_op jit(solution)/shard_map/reduce_scatter | solution.py:262
  927.9 128.7 %reduce-scatter.11.cloned.1.call-done = f32[48,384]{1,0:T(8,128)} async-done(((f32[768,384]{1,0:T(8,128)}), f32[48,384]{1,0:T(8,128)}) %reduce-scatter.11.cloned.1.call-update) | async-done | bytes 73744 | tf_op jit(solution)/shard_map/reduce_scatter | solution.py:261
  1056.6 128.9 %reduce-scatter.9.cloned.1.call-done = f32[48,384]{1,0:T(8,128)} async-done(((f32[768,384]{1,0:T(8,128)}), f32[48,384]{1,0:T(8,128)}) %reduce-scatter.9.cloned.1.call-update) | async-done | bytes 73744 | tf_op jit(solution)/shard_map/reduce_scatter | solution.py:260
  1185.6 142.4 %reduce-scatter.17.cloned.1.call-done = f32[48,1536]{1,0:T(8,128)} async-done(((f32[768,1536]{1,0:T(8,128)}), f32[48,1536]{1,0:T(8,128)}) %reduce-scatter.17.cloned.1.call-update) | async-done | bytes 294928 | tf_op jit(solution)/shard_map/reduce_scatter | solution.py:264
  1327.9 141.6 %reduce-scatter.19.cloned.1.call-done = f32[48,1536]{1,0:T(8,128)} async-done(((f32[768,1536]{1,0:T(8,128)}), f32[48,1536]{1,0:T(8,128)}) %reduce-scatter.19.cloned.1.call-update) | async-done | bytes 294928
  (510 shorter events, 361.7 us)
Async XLA Ops:
  8.0 229.2 %copy-start = (bf16[32,6]{0,1:T(8,128)(2,1)S(1)}, bf16[32,6]{0,1:T(8,128)(2,1)}, u32[]{:S(2)}) copy-start(bf16[32,6]{0,1:T(8,128)(2,1)} %param.37) | copy-start | bytes 1156
  8.0 50.3 %copy-start.5 = (bf16[2,512,768]{2,1,0:T(8,128)(2,1)S(1)}, bf16[2,512,768]{2,1,0:T(8,128)(2,1)}, u32[]{:S(2)}) copy-start(bf16[2,512,768]{2,1,0:T(8,128)(2,1)} %param.25) | copy-start | bytes 4718596
  8.0 131.9 %copy-start.7 = (bf16[4,256,768]{2,1,0:T(8,128)(2,1)S(1)}, bf16[4,256,768]{2,1,0:T(8,128)(2,1)}, u32[]{:S(2)}) copy-start(bf16[4,256,768]{2,1,0:T(8,128)(2,1)} %param.24) | copy-start | bytes 4718596
  8.1 51.9 %copy-start.93 = (bf16[48,384]{1,0:T(8,128)(2,1)S(1)}, bf16[48,384]{1,0:T(8,128)(2,1)}, u32[]{:S(2)}) copy-start(bf16[48,384]{1,0:T(8,128)(2,1)} %param.29) | copy-start | bytes 110596
  8.1 90.6 %copy-start.94 = (bf16[48,384]{1,0:T(8,128)(2,1)S(1)}, bf16[48,384]{1,0:T(8,128)(2,1)}, u32[]{:S(2)}) copy-start(bf16[48,384]{1,0:T(8,128)(2,1)} %param.30) | copy-start | bytes 110596
  8.1 353.6 %all-reduce.17.cloned.1.call-start = ((), (), s32[]{:S(2)}) async-start(), calls=%async_computation.16 | async-start | bytes 6291456 | tf_op jit(solution)/shard_map/psum | solution.py:109
  56.6 84.1 %copy-start.85 = (f32[768]{0:T(1024)}, f32[768]{0:T(1024)S(1)}, u32[]{:S(2)}) copy-start(f32[768]{0:T(1024)S(1)} %convert_element_type.311) | copy-start | bytes 9220
  59.4 81.3 %copy-start.91 = (f32[1,4,2,128]{3,1,2,0:T(4,128)}, f32[1,4,2,128]{3,1,2,0:T(4,128)S(1)}, u32[]{:S(2)}) copy-start(f32[1,4,2,128]{3,1,2,0:T(4,128)S(1)} %copy.229) | copy-start | bytes 12292
  60.0 80.7 %copy-start.89 = (f32[1,2,4,128]{3,1,2,0:T(2,128)}, f32[1,2,4,128]{3,1,2,0:T(2,128)S(1)}, u32[]{:S(2)}) copy-start(f32[1,2,4,128]{3,1,2,0:T(2,128)S(1)} %copy.228) | copy-start | bytes 12292
  98.7 47.6 %copy-start.46 = (bf16[768,384]{1,0:T(8,128)(2,1)}, bf16[768,384]{1,0:T(8,128)(2,1)S(1)}, u32[]{:S(2)}) copy-start(bf16[768,384]{1,0:T(8,128)(2,1)S(1)} %all_gather.34) | copy-start | bytes 1769476
  189.3 45.2 %copy-start.55 = (s32[512,512]{1,0:T(8,128)S(1)}, s32[512,512]{1,0:T(8,128)}, u32[]{:S(2)}) copy-start(s32[512,512]{1,0:T(8,128)} %fusion.186) | copy-start | bytes 3145732
  191.9 45.3 %copy-start.83 = (s32[256,256]{1,0:T(8,128)}, s32[256,256]{1,0:T(8,128)S(1)}, u32[]{:S(2)}) copy-start(s32[256,256]{1,0:T(8,128)S(1)} %select_add_fusion.1) | copy-start | bytes 786436
  339.9 21.8 %copy-start.8 = (bf16[4,256,768]{2,1,0:T(8,128)(2,1)S(1)}, bf16[4,256,768]{2,1,0:T(8,128)(2,1)}, u32[]{:S(2)}) copy-start(bf16[4,256,768]{2,1,0:T(8,128)(2,1)} %param.24) | copy-start | bytes 4718596
  342.1 62.4 %all-gather.5.cloned.1.call-start = ((), (), s32[]{:S(2)}) async-start(), calls=%async_computation.7 | async-start | bytes 2506752 | tf_op jit(solution)/shard_map/all_gather | solution.py:232
  342.7 125.7 %all-gather.3.cloned.1.call-start = ((), (), s32[]{:S(2)}) async-start(), calls=%async_computation.6 | async-start | bytes 2506752 | tf_op jit(solution)/shard_map/all_gather | solution.py:231
  343.2 175.2 %all-reduce.15.cloned.1.call-start = ((), (), s32[]{:S(2)}) async-start(), calls=%async_computation.15 | async-start | bytes 6291456 | tf_op jit(solution)/shard_map/psum | solution.py:137
  496.8 226.5 %all-reduce.13.cloned.1.call-start = ((), (), s32[]{:S(2)}) async-start(), calls=%async_computation.14 | async-start | bytes 12582912 | tf_op jit(solution)/shard_map/psum | solution.py:116
  662.2 153.2 %reduce-scatter.15.cloned.1.call-start = ((), (), s32[]{:S(2)}) async-start(), calls=%async_computation.11 | async-start | bytes 1253376 | tf_op jit(solution)/shard_map/reduce_scatter | solution.py:263
  673.9 254.1 %reduce-scatter.13.cloned.1.call-start = ((), (), s32[]{:S(2)}) async-start(), calls=%async_computation.10 | async-start | bytes 1253376 | tf_op jit(solution)/shard_map/reduce_scatter | solution.py:262
  680.1 376.6 %reduce-scatter.11.cloned.1.call-start = ((), (), s32[]{:S(2)}) async-start(), calls=%async_computation.9 | async-start | bytes 1253376 | tf_op jit(solution)/shard_map/reduce_scatter | solution.py:261
  685.1 500.4 %reduce-scatter.9.cloned.1.call-start = ((), (), s32[]{:S(2)}) async-start(), calls=%async_computation.8 | async-start | bytes 1253376 | tf_op jit(solution)/shard_map/reduce_scatter | solution.py:260
  690.5 637.5 %reduce-scatter.17.cloned.1.call-start = ((), (), s32[]{:S(2)}) async-start(), calls=%async_computation.12 | async-start | bytes 5013504 | tf_op jit(solution)/shard_map/reduce_scatter | solution.py:264
  701.1 768.5 %reduce-scatter.19.cloned.1.call-start = ((), (), s32[]{:S(2)}) async-start(), calls=%async_computation.13 | async-start | bytes 5013504
  810.1 659.5 %copy-start.1 = (bf16[32,6]{0,1:T(8,128)(2,1)S(1)}, bf16[32,6]{0,1:T(8,128)(2,1)}, u32[]{:S(2)}) copy-start(bf16[32,6]{0,1:T(8,128)(2,1)} %param.37) | copy-start | bytes 1156
  (127 other events, 411.0 us)
Sparse Core Ops, SparseCore 0:
  342.2 19.4 all-reduce.16
  496.9 21.5 all-reduce.14
  662.3 33.3 all-reduce.12
Sparse Core Ops, SparseCore 1:
  345.7 58.7 all-gather.4
  407.5 60.7 all-gather.2
  673.9 124.9 reduce-scatter.14
  805.0 122.9 reduce-scatter.12
  934.0 122.6 reduce-scatter.10
  1062.7 122.8 reduce-scatter.8
  1192.0 135.9 reduce-scatter.16
  1333.6 136.0 reduce-scatter.18
where the time goes:
time: 1490 us; the launch traced here: 1480 us
  waiting for transfers between devices  767 us (51%)
  blocking collectives  282 us (19%)
  matrix products  208 us (14%)
  local copies, waits for them, and re-layouts  148 us (10%)
  other arithmetic  50.7 us (3%)
  between operations  18 us (1%)
    unnamed x12, waiting for transfers between devices  143 us
    reduce_scatter x1, waiting for transfers between devices, on_device(): lax.psum_scatter(total[4], 'dp', scatter_dimension=0, tiled=True)  142 us
    reduce_scatter x1, waiting for transfers between devices, on_device(): lax.psum_scatter(total[0], 'dp', scatter_dimension=0, tiled=True)  129 us
    reduce_scatter x1, waiting for transfers between devices, on_device(): lax.psum_scatter(total[1], 'dp', scatter_dimension=0, tiled=True)  129 us
    unnamed x2, blocking collectives  121 us
    reduce_scatter x1, waiting for transfers between devices, on_device(): lax.psum_scatter(total[2], 'dp', scatter_dimension=0, tiled=True)  113 us
    all_gather x1, waiting for transfers between devices, on_device(): lax.all_gather(in_weight, 'dp', axis=0, tiled=True)  51.7 us
    dot_general x12, matrix products, contract_rows(): lax.dot_general(left, right, (((0,), (0,)), ((), ())), preferred_element_...  43.3 us
  transfers between devices with their start and end apart: 11, of which 9 were waited for; matrix products, arithmetic and copies ran while one was open for 7% of the time, Pallas kernels for 0%

commit v1 on v0

v1 whole, which is shorter than its diff:
```python
import functools

import jax
import jax.numpy as jnp
from jax import lax
from jax.experimental import pallas as pl
from jax.experimental.pallas import tpu as pltpu
from jax.sharding import PartitionSpec as P

DH = 64
LANES = 128
EPS = 1e-06
NEG = -1000000000.0
VMEM_LIMIT = 56 * 1024 * 1024
BF = jnp.bfloat16
F32 = jnp.float32


def dot(left, right):
    return jnp.dot(left, right, preferred_element_type=F32)


def dot_rows(left, right):
    return lax.dot_general(left, right, (((0,), (0,)), ((), ())), preferred_element_type=F32)


def dot_cols(left, right):
    return lax.dot_general(left, right, (((1,), (1,)), ((), ())), preferred_element_type=F32)


def whole(array):
    zeros = (0,) * array.ndim
    return pl.BlockSpec(array.shape, lambda *_: zeros)


def rows_of(array, rows):
    return pl.BlockSpec((rows,) + array.shape[1:], lambda i, *_: (i,) + (0,) * (array.ndim - 1))


def params():
    return pltpu.CompilerParams(vmem_limit_bytes=VMEM_LIMIT)


def out_of(shape, kind):
    return jax.ShapeDtypeStruct(shape, kind)


def distance_buckets(bounds_ref, dist, buckets):
    size = jnp.abs(dist)
    half = jnp.zeros(dist.shape, jnp.int32)
    for b in range(bounds_ref.shape[0]):
        half += (size >= bounds_ref[b]).astype(jnp.int32)
    return half + jnp.where(dist > 0, buckets // 2, 0)


def bases_kernel(bounds_ref, table_ref, near_ref, far_ref):
    heads, _, width = near_ref.shape
    buckets = table_ref.shape[1]
    for ref, sign in ((near_ref, 1), (far_ref, -1)):
        dist = sign * (lax.broadcasted_iota(jnp.int32, (buckets, width), 1) - width // 2)
        marks = distance_buckets(bounds_ref, dist, buckets)
        onehot = (marks == lax.broadcasted_iota(jnp.int32, (buckets, width), 0)).astype(F32)
        line = dot(table_ref[...], onehot.astype(BF))
        row = lax.broadcasted_iota(jnp.int32, (8, width), 0)
        for h in range(heads):
            field = jnp.broadcast_to(line[h : h + 1], (8, width))
            for k in (1, 2, 4):
                field = jnp.where((row & k) != 0, pltpu.roll(field, k, 1), field)
            while field.shape[0] < LANES:
                field = jnp.concatenate([field, pltpu.roll(field, field.shape[0], 1)], 0)
            ref[h] = field


def bias_bases(boundaries, table, heads, width):
    rows = jnp.zeros((8, table.shape[0]), table.dtype).at[: table.shape[1]].set(table.T)
    shape = out_of((heads, LANES, width), F32)
    return pl.pallas_call(
        bases_kernel,
        in_specs=[pl.BlockSpec(memory_space=pltpu.SMEM), pl.BlockSpec(memory_space=pltpu.VMEM)],
        out_specs=[pl.BlockSpec(memory_space=pltpu.VMEM)] * 2,
        out_shape=[shape, shape],
        compiler_params=params(),
    )(boundaries, rows)


def bucket_kernel(bounds_ref, field_ref, sums_ref):
    heads, _, width = field_ref.shape
    buckets = sums_ref.shape[0]
    dist = width // 2 - lax.broadcasted_iota(jnp.int32, (8, width), 1)
    marks = distance_buckets(bounds_ref, dist, buckets)
    row = lax.broadcasted_iota(jnp.int32, (8, width), 0)
    line = jnp.zeros((8, width), F32)
    for h in range(heads):
        field = field_ref[h]
        while field.shape[0] > 8:
            half = field.shape[0] // 2
            field = field[:half] + pltpu.roll(field[half:], width - half, 1)
        for k in (4, 2, 1):
            field = jnp.where((row & k) != 0, pltpu.roll(field, width - k, 1), field)
        line = jnp.where(row == h, jnp.sum(field, 0, keepdims=True), line)
    for b in range(buckets):
        total = jnp.sum(jnp.where(marks == b, line, 0.0), 1, keepdims=True)
        sums_ref[b] = jnp.broadcast_to(total, (8, LANES))


def bucket_sums(boundaries, field, buckets):
    return pl.pallas_call(
        bucket_kernel,
        in_specs=[pl.BlockSpec(memory_space=pltpu.SMEM), pl.BlockSpec(memory_space=pltpu.VMEM)],
        out_specs=pl.BlockSpec(memory_space=pltpu.VMEM),
        out_shape=out_of((buckets, 8, LANES), F32),
        compiler_params=params(),
    )(boundaries, field)[:, :, 0]


def split_low(values, lane, off, rest):
    high = values.astype(BF).astype(F32)
    mid = (values - high).astype(BF).astype(F32)
    low = values - high - mid
    return jnp.where(
        lane == off,
        high,
        jnp.where(lane == off + 1, mid, jnp.where(lane == off + 2, low, rest)),
    )


def three_ones(lane, off):
    return jnp.where((lane >= off) & (lane < off + 3), 1.0, 0.0)


def attend_kernel(
    len_ref, normed_ref, qk_ref, vo_ref, near_ref, aug_ref, k_ref, v_ref, o_ref, attn_ref
):
    length = normed_ref.shape[0]
    width = near_ref.shape[-1]
    cols = k_ref.shape[1]
    valid = len_ref[pl.program_id(0)]
    lane = lax.broadcasted_iota(jnp.int32, (length, LANES), 1)
    place = lax.broadcasted_iota(jnp.int32, (length, LANES), 0)
    masked = jnp.where(place >= valid, NEG, 0.0)
    normed = normed_ref[...]
    for p in range(cols // LANES):
        at = slice(p * LANES, (p + 1) * LANES)
        keys_at = slice(cols + p * LANES, cols + (p + 1) * LANES)
        q = dot(normed, qk_ref[:, at])
        k = dot(normed, qk_ref[:, keys_at])
        v = dot(normed, vo_ref[:, at])
        k_ref[:, at] = k.astype(BF)
        v_ref[:, at] = v.astype(BF)
        mixed = []
        for e in range(2):
            own = (lane >= DH) == (e == 1)
            off = DH * (1 - e)
            h = 2 * p + e
            marker = jnp.where(lane == off + 3, 1.0, 0.0)
            q_own = jnp.where(own, q, marker).astype(BF)
            k_own = jnp.where(own, k, jnp.where(lane == off + 3, masked, 0.0)).astype(BF)
            v_own = jnp.where(own, v, 1.0).astype(BF)
            tops = []
            sums = []
            for a in range(length // LANES):
                rows = slice(a * LANES, (a + 1) * LANES)
                start = width // 2 - a * LANES
                scores = dot_cols(q_own[rows], k_own) + near_ref[h, :, start : start + length]
                top = jnp.max(scores, 1, keepdims=True)
                expo = jnp.exp(scores - top)
                tops.append(jnp.broadcast_to(top, (LANES, LANES)))
                sums.append(dot(expo.astype(BF), v_own))
            sums = jnp.concatenate(sums, 0)
            total = jnp.where(own, pltpu.roll(sums, DH, 1), sums)
            logsum = jnp.concatenate(tops, 0) + jnp.log(total)
            extra = split_low(-logsum, lane, off, marker)
            aug_ref[:, h * LANES : (h + 1) * LANES] = jnp.where(own, q, extra).astype(BF)
            mixed.append(sums / total)
        o_ref[:, at] = jnp.where(lane < DH, mixed[0], mixed[1]).astype(BF)
    attn_ref[...] = dot_cols(o_ref[...], vo_ref[:, cols:]).astype(BF)


def attend(lengths, normed, qk, vo, near, length):
    rows, width = normed.shape
    cols = vo.shape[1] // 2
    slots = rows // length
    shapes = [(rows, 2 * cols), (rows, cols), (rows, cols), (rows, cols), (rows, width)]
    shapes = [out_of(s, BF) for s in shapes]
    return pl.pallas_call(
        attend_kernel,
        grid_spec=pltpu.PrefetchScalarGridSpec(
            num_scalar_prefetch=1,
            grid=(slots,),
            in_specs=[rows_of(normed, length), whole(qk), whole(vo), whole(near)],
            out_specs=[rows_of(s, length) for s in shapes],
        ),
        out_shape=shapes,
        compiler_params=params(),
    )(lengths, normed, qk, vo, near)


def attend_back_kernel(
    len_ref,
    grad_ref,
    normed_ref,
    aug_ref,
    k_ref,
    v_ref,
    o_ref,
    qk_ref,
    vo_ref,
    far_ref,
    *refs,
):
    kept = refs[:-7]
    part_ref, gqk_ref, gvo_ref, gbase_ref, gq_scr, gkv_scr, ds_scr = refs[-7:]
    length = grad_ref.shape[0]
    width = far_ref.shape[-1]
    cols = k_ref.shape[1]
    slot = pl.program_id(0)
    valid = len_ref[slot]

    @pl.when(slot == 0)
    def _():
        for i, ref in enumerate((gqk_ref, gvo_ref, gbase_ref)):
            ref[...] = kept[i][...] if kept else jnp.zeros_like(ref)

    lane = lax.broadcasted_iota(jnp.int32, (length, LANES), 1)
    place = lax.broadcasted_iota(jnp.int32, (length, LANES), 0)
    masked = jnp.where(place >= valid, NEG, 0.0)
    grad = grad_ref[...]
    for p in range(cols // LANES):
        at = slice(p * LANES, (p + 1) * LANES)
        k = k_ref[:, at].astype(F32)
        v = v_ref[:, at].astype(F32)
        o = o_ref[:, at].astype(F32)
        go = dot(grad, vo_ref[:, cols + p * LANES : cols + (p + 1) * LANES]).astype(BF).astype(F32)
        both = go * o
        grads = []
        for e in range(2):
            own = (lane >= DH) == (e == 1)
            off = DH * (1 - e)
            h = 2 * p + e
            q_own = aug_ref[:, h * LANES : (h + 1) * LANES]
            ones = three_ones(lane, off)
            k_own = jnp.where(own, k, jnp.where(lane == off + 3, masked, ones)).astype(BF)
            v_own = jnp.where(own, v, ones).astype(BF)
            delta = jnp.sum(jnp.where(own, both, 0.0), 1, keepdims=True)
            extra = split_low(-delta, lane, off, 0.0)
            g_own = jnp.where(own, go, extra).astype(BF)
            gks = []
            gvs = []
            for a in range(length // LANES):
                rows = slice(a * LANES, (a + 1) * LANES)
                start = width // 2 - a * LANES
                span = slice(start, start + length)
                probs = jnp.exp(dot_cols(k_own[rows], q_own) + far_ref[h, :, span])
                ds = probs * dot_cols(v_own[rows], g_own)
                gbase_ref[h, :, span] += ds
                ds = ds.astype(BF)
                ds_scr[rows, :] = ds
                gvs.append(dot(probs.astype(BF), g_own))
                gks.append(dot(ds, q_own))
            gq = dot_rows(ds_scr[...], k_own)
            grads.append((gq, jnp.concatenate(gks, 0), jnp.concatenate(gvs, 0)))
        first = lane < DH
        gq, gk, gv = (jnp.where(first, a, b).astype(BF) for a, b in zip(*grads))
        gq_scr[:, at] = gq
        gq_scr[:, cols + p * LANES : cols + (p + 1) * LANES] = gk
        gkv_scr[:, at] = gv
    normed = normed_ref[...]
    gqk = gq_scr[...]
    gv = gkv_scr[...]
    part_ref[...] = (dot_cols(gqk, qk_ref[...]) + dot_cols(gv, vo_ref[:, :cols])).astype(BF)
    gqk_ref[...] += dot_rows(normed, gqk)
    gvo_ref[:, :cols] += dot_rows(normed, gv)
    gvo_ref[:, cols:] += dot_rows(grad, o_ref[...])


def attend_back(lengths, grad, normed, aug, k, v, o, qk, vo, far, kept, length):
    rows, width = normed.shape
    cols = vo.shape[1] // 2
    slots = rows // length
    part = out_of((rows, width), BF)
    totals = [out_of(qk.shape, F32), out_of(vo.shape, F32), out_of(far.shape, F32)]
    return pl.pallas_call(
        attend_back_kernel,
        grid_spec=pltpu.PrefetchScalarGridSpec(
            num_scalar_prefetch=1,
            grid=(slots,),
            in_specs=[rows_of(a, length) for a in (grad, normed, aug, k, v, o)]
            + [whole(a) for a in (qk, vo, far) + tuple(kept)],
            out_specs=[rows_of(part, length)] + [whole(t) for t in totals],
            scratch_shapes=[
                pltpu.VMEM((length, 2 * cols), BF),
                pltpu.VMEM((length, cols), BF),
                pltpu.VMEM((length, length), BF),
            ],
        ),
        out_shape=[part] + totals,
        compiler_params=params(),
    )(lengths, grad, normed, aug, k, v, o, qk, vo, far, *kept)


def gelu_parts(x):
    c = 0.7978845608028654
    d = c * 0.044715
    square = x * x
    t = jnp.tanh(x * (c + d * square))
    half = 0.5 + 0.5 * t
    slope = half + (0.5 * x) * (1.0 - t * t) * (c + 3.0 * d * square)
    return x * half, slope


def ffn_kernel(normed_ref, g_ref, win_ref, wout_ref, *refs):
    kept = refs[:-4]
    out_ref, gn_ref, gin_ref, gout_ref = refs[-4:]

    @pl.when(pl.program_id(0) == 0)
    def _():
        gin_ref[...] = jnp.zeros_like(gin_ref)
        gout_ref[...] = jnp.zeros_like(gout_ref)

    normed = normed_ref[...]
    g = g_ref[...]
    act, slope = gelu_parts(dot(normed, win_ref[...]))
    act = act.astype(BF)
    gpre = (dot(g, wout_ref[...]) * slope).astype(BF)
    out = dot_cols(act, wout_ref[...])
    gn = dot_cols(gpre, win_ref[...])
    if kept:
        out += kept[0][...]
        gn += kept[1][...]
    out_ref[...] = out.astype(out_ref.dtype)
    gn_ref[...] = gn.astype(gn_ref.dtype)
    gout_ref[...] += dot_rows(g, act)
    gin_ref[...] += dot_rows(normed, gpre)


def ffn(normed, g, win, wout, kept, kind, tile=512):
    rows, width = normed.shape
    field = out_of((rows, width), kind)
    weight = out_of(win.shape, F32)
    return pl.pallas_call(
        ffn_kernel,
        grid=(rows // tile,),
        in_specs=[rows_of(normed, tile), rows_of(g, tile), whole(win), whole(wout)]
        + [rows_of(a, tile) for a in kept],
        out_specs=[rows_of(field, tile), rows_of(field, tile), whole(weight), whole(weight)],
        out_shape=[field, field, weight, weight],
        compiler_params=params(),
    )(normed, g, win, wout, *kept)


def send_xor(array, mask, size):
    return lax.ppermute(array, "dp", [(i, i ^ mask) for i in range(size)])


def exchange(array, size):
    return [
        lax.ppermute(array, "mp", [(i, i ^ k) for i in range(size)]) for k in range(1, size)
    ]


def group_sum(array, size):
    total = array.astype(F32)
    for other in exchange(array, size):
        total = total + other.astype(F32)
    return total


def stages(size, swap):
    bits = [1 << b for b in range(size.bit_length() - 1)]
    low, high = bits[:2], bits[2:]
    groups = [high[i : i + 2] for i in range(0, len(high), 2)]
    return groups + [[b] for b in (low[::-1] if swap else low)]


def combos(bits):
    masks = [0]
    for b in bits:
        masks = masks + [m | b for m in masks]
    return masks


def gather(part, size, me, swap):
    held = part[(None,) * (size.bit_length() - 1)]
    axes = size.bit_length() - 1
    for bits in stages(size, swap):
        got = [held] + [send_xor(held, m, size) for m in combos(bits)[1:]]
        for b in bits:
            axis = axes - b.bit_length()
            mine = (me & b) == 0
            pairs = [(got[2 * i], got[2 * i + 1]) for i in range(len(got) // 2)]
            got = [
                jnp.concatenate([jnp.where(mine, p, q), jnp.where(mine, q, p)], axis)
                for p, q in pairs
            ]
        held = got[0]
    return held.reshape((size * part.shape[0],) + part.shape[1:])


def scatter(total, size, me, swap):
    axes = size.bit_length() - 1
    held = total.reshape((2,) * axes + (total.shape[0] // size,) + total.shape[1:])
    for bits in reversed(stages(size, swap)):
        got = []
        for m in combos(bits):
            piece = held
            for b in bits:
                at = jnp.where(((me ^ m) & b) == 0, 0, 1)
                piece = lax.dynamic_slice_in_dim(piece, at, 1, axes - b.bit_length())
            got.append(piece if m == 0 else send_xor(piece.astype(BF), m, size))
        held = got[0]
        for piece in got[1:]:
            held = held + piece.astype(F32)
    return held.reshape((total.shape[0] // size,) + total.shape[1:])


def scatter_both(total, size, me):
    half = total.shape[1] // 2
    return scatter(total[:, :half], size, me, False), scatter(total[:, half:], size, me, True)


def small_sum(array, size):
    bits = [1 << b for b in range(size.bit_length() - 1)]
    for i in range(0, len(bits), 2):
        total = array
        for m in combos(bits[i : i + 2])[1:]:
            total = total + send_xor(array, m, size)
        array = total
    return array


def rms_parts(field):
    scale = lax.rsqrt(jnp.mean(field * field, -1, keepdims=True) + EPS)
    return (scale, field * scale)


def norm_back(grad_unit, unit, scale):
    return scale * (grad_unit - unit * jnp.mean(grad_unit * unit, -1, keepdims=True))


def pad_cols(array, cols):
    return jnp.pad(array, ((0, 0), (0, cols - array.shape[1]))) if cols > array.shape[1] else array


def on_device(
    sizes,
    x_short,
    x_long,
    len_short,
    len_long,
    boundaries,
    q_weight,
    k_weight,
    v_weight,
    out_weight,
    in_weight,
    ff_out_weight,
    attn_gain,
    ffn_gain,
    bias_table,
    cot_short,
    cot_long,
):
    dp, mp = sizes
    me = lax.axis_index("dp")
    width = x_short.shape[2]
    heads = bias_table.shape[1]
    real = heads * DH
    cols = -(-real // LANES) * LANES
    chunks = 3
    units = in_weight.shape[1] // chunks
    span = 2 * max(x_short.shape[1], x_long.shape[1])

    gains = small_gather(jnp.stack([attn_gain, ffn_gain]).astype(F32), dp, me)
    gain_a, gain_f = gains[0], gains[1]
    padded = [pad_cols(w, cols) for w in (q_weight, k_weight, v_weight, out_weight)]
    qk = gather(jnp.concatenate(padded[:2], 1), dp, me, False)
    vo = gather(jnp.concatenate(padded[2:], 1), dp, me, True)
    ffn_weights = []
    for c in range(chunks):
        at = slice(c * units, (c + 1) * units)
        ffn_weights.append(
            (gather(in_weight[:, at], dp, me, False), gather(ff_out_weight[:, at], dp, me, True))
        )

    near, far = bias_bases(boundaries, bias_table, cols // DH, span)

    batches = []
    for x, lengths, cot in ((x_short, len_short, cot_short), (x_long, len_long, cot_long)):
        length = x.shape[1]
        field = x.reshape(-1, width).astype(F32)
        normed = (rms_parts(field)[1] * gain_a).astype(BF)
        aug, k, v, o, attn = attend(lengths, normed, qk, vo, near, length)
        batches.append((x, lengths, cot, length, normed, aug, k, v, o, attn))

    middles = []
    for x, lengths, cot, length, normed, aug, k, v, o, attn in batches:
        middle = x.reshape(-1, width).astype(F32) + group_sum(attn, mp)
        middles.append(middle)
    middle = jnp.concatenate(middles, 0)
    scale_f, unit_f = rms_parts(middle)
    normed_f = (unit_f * gain_f).astype(BF)
    g = jnp.concatenate([cot_short.reshape(-1, width), cot_long.reshape(-1, width)], 0)
    kept = ()
    grads_f = []
    for c in range(chunks):
        out, gn, gin, gout = ffn(
            normed_f, g, *ffn_weights[c], kept, BF if c == chunks - 1 else F32
        )
        kept = (out, gn)
        grads_f.append((scatter(gin, dp, me, False), scatter(gout, dp, me, True)))
    grad_in_weight = jnp.concatenate([a for a, _ in grads_f], 1)
    grad_ff_out_weight = jnp.concatenate([b for _, b in grads_f], 1)
    out = (middle + group_sum(out, mp)).astype(BF)
    grad_norm_f = group_sum(gn, mp)
    grad_gain_f = jnp.sum(grad_norm_f * unit_f, 0)
    grad_mid = g.astype(F32) + norm_back(grad_norm_f * gain_f, unit_f, scale_f)
    grad_attn = grad_mid.astype(BF)

    split = x_short.shape[0] * x_short.shape[1]
    kept = ()
    parts = []
    for i, (x, lengths, cot, length, normed, aug, k, v, o, attn) in enumerate(batches):
        rows = slice(0, split) if i == 0 else slice(split, None)
        part, *kept = attend_back(
            lengths, grad_attn[rows], normed, aug, k, v, o, qk, vo, far, kept, length
        )
        parts.append(part)
    gqk, gvo, gbase = kept
    shares_qk = scatter(gqk, dp, me, False)
    shares_vo = scatter(gvo, dp, me, True)
    table_grad = bucket_sums(boundaries, gbase, bias_table.shape[0])[:, :heads]

    grad_xs = []
    grad_gain_a = 0.0
    for i, (x, lengths, cot, length, normed, aug, k, v, o, attn) in enumerate(batches):
        rows = slice(0, split) if i == 0 else slice(split, None)
        scale_a, unit_a = rms_parts(x.reshape(-1, width).astype(F32))
        grad_norm_a = group_sum(parts[i], mp)
        grad_gain_a = grad_gain_a + jnp.sum(grad_norm_a * unit_a, 0)
        grad_x = grad_mid[rows] + norm_back(grad_norm_a * gain_a, unit_a, scale_a)
        grad_xs.append(grad_x.astype(BF).reshape(x.shape))

    small = jnp.concatenate([grad_gain_a, grad_gain_f, table_grad.reshape(-1)])
    small = small_sum(small, dp)
    share = width // dp
    gain_a_grad = lax.dynamic_slice_in_dim(small, me * share, share)
    gain_f_grad = lax.dynamic_slice_in_dim(small, width + me * share, share)
    table_grad = small[2 * width :].reshape(table_grad.shape)
    return (
        out[:split].reshape(x_short.shape),
        out[split:].reshape(x_long.shape),
        grad_xs[0],
        grad_xs[1],
        shares_qk[:, :real],
        shares_qk[:, cols : cols + real],
        shares_vo[:, :real],
        shares_vo[:, cols : cols + real],
        grad_in_weight,
        grad_ff_out_weight,
        gain_a_grad,
        gain_f_grad,
        table_grad,
    )


def small_gather(part, size, me):
    rows, share = part.shape
    wide = jnp.zeros((rows, share * size), part.dtype)
    return small_sum(lax.dynamic_update_slice_in_dim(wide, part, me * share, 1), size)


def solution(mesh):
    sizes = (mesh.shape["dp"], mesh.shape["mp"])
    return jax.shard_map(
        functools.partial(on_device, sizes),
        mesh=mesh,
        in_specs=(
            P("dp", None, None),
            P("dp", None, None),
            P("dp"),
            P("dp"),
            P(),
            P("dp", "mp"),
            P("dp", "mp"),
            P("dp", "mp"),
            P("dp", "mp"),
            P("dp", "mp"),
            P("dp", "mp"),
            P("dp"),
            P("dp"),
            P(None, "mp"),
            P("dp", None, None),
            P("dp", None, None),
        ),
        out_specs=(
            P("dp", None, None),
            P("dp", None, None),
            P("dp", None, None),
            P("dp", None, None),
            P("dp", "mp"),
            P("dp", "mp"),
            P("dp", "mp"),
            P("dp", "mp"),
            P("dp", "mp"),
            P("dp", "mp"),
            P("dp"),
            P("dp"),
            P(None, "mp"),
        ),
        check_vma=False,
    )
```

time: 1490 us -> 466 us (0.31)
  waiting for transfers between devices: 767 us -> 98.8 us
  blocking collectives: 282 us -> 0 us
  matrix products: 208 us -> 0 us
  Pallas kernels: 0 us -> 156 us
  local copies, waits for them, and re-layouts: 148 us -> 27.2 us
  starting transfers between devices: 1.34 us -> 115 us
  between operations: 18 us -> 2.45 us
    reduce_scatter x5 -> x0, waiting for transfers between devices: 513 us -> none  [the longest x1 142 us: on_device(): lax.psum_scatter(total[4], 'dp', scatter_dimension=0, tiled=True)]
    dot_general x74 -> x0, matrix products: 208 us -> none  [the longest x12 43.3 us: contract_rows(): lax.dot_general(left, right, (((0,), (0,)), ((), ())), preferred_element_...]
    all_gather x4 -> x0, blocking collectives: 162 us -> none  [the longest x1 42.5 us: on_device(): lax.all_gather(out_weight, 'dp', axis=0, tiled=True)]
    pallas_call x0 -> x9, Pallas kernels: none -> 156 us  [the longest x2 57.1 us: attend_back(): pl.pallas_call(attend_back_kernel, grid_spec=pltpu.PrefetchScalarGridSpec...]
    unnamed x12 -> x0, waiting for transfers between devices: 143 us -> none
    unnamed x2 -> x0, blocking collectives: 121 us -> none
    ppermute x0 -> x98, starting transfers between devices: none -> 115 us  [the longest x92 113 us: send_xor(): return lax.ppermute(array, 'dp', [(i, i ^ mask) for i in range(size)])]
    ppermute x0 -> x98, waiting for transfers between devices: none -> 98.8 us  [the longest x92 98.8 us: send_xor(): return lax.ppermute(array, 'dp', [(i, i ^ mask) for i in range(size)])]
  transfers between devices with their start and end apart: 11 -> 98, of which waited for: 9 -> 41; matrix products, arithmetic and copies ran while one was open for 7% -> 12% of each run, Pallas kernels for 0% -> 19%
where the time goes in v1:
time: 466 us; the launch traced here: 457 us
  Pallas kernels  156 us (33%)
  starting transfers between devices  115 us (25%)
  waiting for transfers between devices  98.8 us (21%)
  other arithmetic  57.9 us (12%)
  local copies, waits for them, and re-layouts  27.2 us (6%)
    ppermute x92, starting transfers between devices, send_xor(): return lax.ppermute(array, 'dp', [(i, i ^ mask) for i in range(size)])  113 us
    ppermute x92, waiting for transfers between devices, send_xor(): return lax.ppermute(array, 'dp', [(i, i ^ mask) for i in range(size)])  98.8 us
    pallas_call x2, Pallas kernels, attend_back(): pl.pallas_call(attend_back_kernel, grid_spec=pltpu.PrefetchScalarGridSpec...  57.1 us
    pallas_call x3, Pallas kernels, ffn(): pl.pallas_call(ffn_kernel, grid=(rows // tile,), in_specs=[rows_of(normed...  45.9 us
    pallas_call x2, Pallas kernels, attend(): pl.pallas_call(attend_kernel, grid_spec=pltpu.PrefetchScalarGridSpec(num_...  40.7 us
    convert_element_type x24, local copies, waits for them, and re-layouts, scatter(): got.append(piece if m == 0 else send_xor(piece.astype(BF), m, size))  13.9 us
    convert_element_type x1, other arithmetic, on_device(): grad_attn = grad_mid.astype(BF)  11.6 us
  transfers between devices with their start and end apart: 98, of which 41 were waited for; matrix products, arithmetic and copies ran while one was open for 12% of the time, Pallas kernels for 19%

profile of v1, /device:TPU:0, one launch (start us, length us, event | category | flops | bytes accessed | tf_op | source)
XLA Modules:
  0.0 457.3 jit_solution(5593855820779914809)
XLA Ops:
  1.6 4.0 collective-permute-start.2
  7.7 4.0 collective-permute-start.13
  25.1 7.8 %shard_map.255 = (f32[6,128,1024]{2,1,0:T(8,128)}, f32[6,128,1024]{2,1,0:T(8,128)}) custom-call(s32[15]{0:T(128)} %bounds_ref.3, bf16[8,32]{1,0:T(8,128)(2,1)} %scatter.4.table_ref), custom_call_target="tpu_custom_call" | custom-call | tf_op jit(solution)/shard_map/pallas_call | solution.py:77
  56.2 3.7 collective-permute-done.30
  61.9 4.1 collective-permute-done.35
  67.8 4.2 collective-permute-done.40
  89.7 5.0 %collective-permute-done.31 = bf16[2,2,1,1,48,512]{5,4,3,2,1,0:T(8,128)(2,1)S(1)} collective-permute-done((bf16[2,2,1,1,48,512]{5,4,3,2,1,0:T(8,128)(2,1)S(1)}, bf16[2,2,1,1,48,512]{5,4,3,2,1,0:T(8,128)(2,1)S(1)}, u32[]{:S(2)}, u32[]{:S(2)}) %collective-permute-start.31) | collective-permute-done | bytes 196640 | tf_op jit(solution)/shard_map/ppermute | solution.py:352
  110.6 6.7 %collective-permute-done.42 = bf16[2,2,1,2,48,512]{5,4,3,2,1,0:T(8,128)(2,1)S(1)} collective-permute-done((bf16[2,2,1,2,48,512]{5,4,3,2,1,0:T(8,128)(2,1)S(1)}, bf16[2,2,1,2,48,512]{5,4,3,2,1,0:T(8,128)(2,1)S(1)}, u32[]{:S(2)}, u32[]{:S(2)}) %collective-permute-start.42) | collective-permute-done | bytes 393248 | tf_op jit(solution)/shard_map/ppermute | solution.py:352
  121.5 11.1 %collective-permute-done.10 = bf16[2,2,1,2,48,768]{5,4,3,2,1,0:T(8,128)(2,1)S(1)} collective-permute-done((bf16[2,2,1,2,48,768]{5,4,3,2,1,0:T(8,128)(2,1)S(1)}, bf16[2,2,1,2,48,768]{5,4,3,2,1,0:T(8,128)(2,1)S(1)}, u32[]{:S(2)}, u32[]{:S(2)}) %collective-permute-start.10) | collective-permute-done | bytes 589856 | tf_op jit(solution)/shard_map/ppermute | solution.py:352
  135.6 25.0 %shard_map.257 = (bf16[1024,768]{1,0:T(8,128)(2,1)}, bf16[1024,384]{1,0:T(8,128)(2,1)}, bf16[1024,384]{1,0:T(8,128)(2,1)}, bf16[1024,384]{1,0:T(8,128)(2,1)}, bf16[1024,768]{1,0:T(8,128)(2,1)}) custom-call(s32[2]{0:T(128)} %len_ref.7, bf16[1024,768]{1,0:T(8,128)(2,1)} %get-tuple-element.246.normed_ref, bf16[768,768]{1,0:T(8,128)(2,1)} %bitcast.144, ...), custom_call_target="tpu_custom_call" | custom-call | tf_op jit(solution)/shard_map/pallas_call | solution.py:185
  162.6 15.8 %shard_map.256 = (bf16[1024,768]{1,0:T(8,128)(2,1)}, bf16[1024,384]{1,0:T(8,128)(2,1)}, bf16[1024,384]{1,0:T(8,128)(2,1)}, bf16[1024,384]{1,0:T(8,128)(2,1)}, bf16[1024,768]{1,0:T(8,128)(2,1)}) custom-call(s32[4]{0:T(128)} %len_ref.6, bf16[1024,768]{1,0:T(8,128)(2,1)} %get-tuple-element.245.normed_ref, bf16[768,768]{1,0:T(8,128)(2,1)} %bitcast.145, ...), custom_call_target="tpu_custom_call" | custom-call | tf_op jit(solution)/shard_map/pallas_call | solution.py:185
  188.8 14.6 %shard_map.258 = (f32[2048,768]{1,0:T(8,128)}, f32[2048,768]{1,0:T(8,128)}, f32[768,512]{1,0:T(8,128)}, f32[768,512]{1,0:T(8,128)}) custom-call(bf16[2048,768]{1,0:T(8,128)(2,1)} %multiply_convert_fusion.normed_ref, bf16[2048,768]{1,0:T(8,128)(2,1)} %pad_maximum_fusion.1.g_ref, bf16[768,512]{1,0:T(8,128)(2,1)} %bitcast.162, bf16[768,512]{1,0:T(8,128)(2,1)} %bitcast.163), custom_call_target="tpu_custom_call" | custom-call | tf_op jit(solution)/shard_map/pallas_call | solution.py:340
  209.3 15.7 %shard_map.259 = (f32[2048,768]{1,0:T(8,128)}, f32[2048,768]{1,0:T(8,128)}, f32[768,512]{1,0:T(8,128)}, f32[768,512]{1,0:T(8,128)}) custom-call(bf16[2048,768]{1,0:T(8,128)(2,1)} %multiply_convert_fusion.normed_ref, bf16[2048,768]{1,0:T(8,128)(2,1)} %pad_maximum_fusion.1.g_ref, bf16[768,512]{1,0:T(8,128)(2,1)} %bitcast.158, bf16[768,512]{1,0:T(8,128)(2,1)} %bitcast.159, ...), custom_call_target="tpu_custom_call" | custom-call | tf_op jit(solution)/shard_map/pallas_call | solution.py:340
  228.3 15.6 %shard_map.260 = (bf16[2048,768]{1,0:T(8,128)(2,1)}, bf16[2048,768]{1,0:T(8,128)(2,1)}, f32[768,512]{1,0:T(8,128)}, f32[768,512]{1,0:T(8,128)}) custom-call(bf16[2048,768]{1,0:T(8,128)(2,1)} %multiply_convert_fusion.normed_ref, bf16[2048,768]{1,0:T(8,128)(2,1)} %pad_maximum_fusion.1.g_ref, bf16[768,512]{1,0:T(8,128)(2,1)} %bitcast.160, ...), custom_call_target="tpu_custom_call" | custom-call | tf_op jit(solution)/shard_map/pallas_call | solution.py:340
  259.7 7.4 %collective-permute-done.72 = bf16[2,2,1,2,48,512]{5,4,3,2,1,0:T(8,128)(2,1)S(1)} collective-permute-done((bf16[2,2,1,2,48,512]{5,4,3,2,1,0:T(8,128)(2,1)S(1)}, bf16[2,2,1,2,48,512]{5,4,3,2,1,0:T(8,128)(2,1)S(1)}, u32[]{:S(2)}, u32[]{:S(2)}) %collective-permute-start.72) | collective-permute-done | bytes 393248 | tf_op jit(solution)/shard_map/ppermute | solution.py:352
  312.9 4.0 collective-permute-done.91
  322.0 11.6 %fusion.26 = (bf16[2048,768]{1,0:T(8,128)(2,1)S(1)}, f32[2048,768]{1,0:T(8,128)}, bf16[2048,768]{1,0:T(8,128)(2,1)}) fusion(f32[2048]{0:T(1024)S(1)} %broadcast_multiply_fusion, f32[1024,768]{1,0:T(8,128)S(1)} %bitcast_add_fusion, f32[1024,768]{1,0:T(8,128)S(1)} %bitcast_add_fusion.1, f32[768]{0:T(1024)S(1)} %get-tuple-element.109, ...), kind=kLoop, calls=%fused_computation.254 | loop fusion | flops 31457280 | bytes 34622464 | tf_op jit(solution)/shard_map/convert_element_type | solution.py:517
  335.4 26.6 %shard_map.261 = (bf16[1024,768]{1,0:T(8,128)(2,1)}, f32[768,768]{1,0:T(8,128)}, f32[768,768]{1,0:T(8,128)}, f32[6,128,1024]{2,1,0:T(8,128)}) custom-call(s32[4]{0:T(128)} %len_ref.6, bf16[1024,768]{1,0:T(8,128)(2,1)} %get-tuple-element.116.grad_ref, bf16[1024,768]{1,0:T(8,128)(2,1)} %get-tuple-element.245.normed_ref, ...), custom_call_target="tpu_custom_call" | custom-call | tf_op jit(solution)/shard_map/pallas_call | solution.py:282
  362.0 30.5 %shard_map.262 = (bf16[1024,768]{1,0:T(8,128)(2,1)}, f32[768,768]{1,0:T(8,128)}, f32[768,768]{1,0:T(8,128)}, f32[6,128,1024]{2,1,0:T(8,128)}) custom-call(s32[2]{0:T(128)} %len_ref.7, bf16[1024,768]{1,0:T(8,128)(2,1)} %get-tuple-element.115.grad_ref, bf16[1024,768]{1,0:T(8,128)(2,1)} %get-tuple-element.246.normed_ref, ...), custom_call_target="tpu_custom_call" | custom-call | tf_op jit(solution)/shard_map/pallas_call | solution.py:282
  396.2 4.8 %shard_map.263 = f32[32,8,128]{2,1,0:T(8,128)} custom-call(s32[15]{0:T(128)} %bounds_ref.3, f32[6,128,1024]{2,1,0:T(8,128)} %get-tuple-element.88.field_ref), custom_call_target="tpu_custom_call" | custom-call | tf_op jit(solution)/shard_map/pallas_call | solution.py:107
  405.8 3.9 fusion.28
  415.8 4.3 collective-permute-done.53
  433.7 3.7 collective-permute-done.60
  451.9 3.6 fusion.1
  (408 shorter events, 217.2 us)
Async XLA Ops:
  1.6 17.2 %collective-permute-start.2 = (f32[2,768]{1,0:T(2,128)S(1)}, f32[2,768]{1,0:T(2,128)S(1)}, u32[]{:S(2)}, u32[]{:S(2)}) collective-permute-start(f32[2,768]{1,0:T(2,128)S(1)} %dynamic_update_slice.5), channel_id=1, source_target_pairs={{0,6},{2,4},{4,2},{6,0},{8,14},{10,12},{12,10},{14,8},{16,22},{18,... | collective-permute-start | bytes 18440 | tf_op jit(solution)/shard_map/ppermute | solution.py:352
  7.7 72.6 %collective-permute-start.13 = (bf16[1,1,1,1,48,768]{5,4,3,2,1,0:T(8,128)(2,1)}, bf16[1,1,1,1,48,768]{5,4,3,2,1,0:T(8,128)(2,1)}, u32[]{:S(2)}, u32[]{:S(2)}) collective-permute-start(bf16[1,1,1,1,48,768]{5,4,3,2,1,0:T(8,128)(2,1)} %maximum_bitcast_fusion.1), channel_id=1, source_target_pairs={{0,24},{2,26},{4,28},{6,30},{8,16},{10,18},{12,20},{14,22},{16,8},... | collective-permute-start | bytes 221192 | tf_op jit(solution)/shard_map/ppermute | solution.py:352
  11.7 70.9 %collective-permute-start.12 = (bf16[1,1,1,1,48,768]{5,4,3,2,1,0:T(8,128)(2,1)}, bf16[1,1,1,1,48,768]{5,4,3,2,1,0:T(8,128)(2,1)}, u32[]{:S(2)}, u32[]{:S(2)}) collective-permute-start(bf16[1,1,1,1,48,768]{5,4,3,2,1,0:T(8,128)(2,1)} %maximum_bitcast_fusion.1), channel_id=1, source_target_pairs={{0,16},{2,18},{4,20},{6,22},{8,24},{10,26},{12,28},{14,30},{16,0},... | collective-permute-start | bytes 221192 | tf_op jit(solution)/shard_map/ppermute | solution.py:352
  52.6 32.6 %collective-permute-start.11 = (bf16[1,1,1,1,48,768]{5,4,3,2,1,0:T(8,128)(2,1)}, bf16[1,1,1,1,48,768]{5,4,3,2,1,0:T(8,128)(2,1)S(1)}, u32[]{:S(2)}, u32[]{:S(2)}) collective-permute-start(bf16[1,1,1,1,48,768]{5,4,3,2,1,0:T(8,128)(2,1)} %maximum_bitcast_fusion.1), channel_id=1, source_target_pairs={{0,8},{2,10},{4,12},{6,14},{8,0},{10,2},{12,4},{14,6},{16,24},{18,... | collective-permute-start | bytes 221192 | tf_op jit(solution)/shard_map/ppermute | solution.py:352
  82.7 13.7 %collective-permute-start.41 = (bf16[2,2,1,1,48,512]{5,4,3,2,1,0:T(8,128)(2,1)S(1)}, bf16[2,2,1,1,48,512]{5,4,3,2,1,0:T(8,128)(2,1)S(1)}, u32[]{:S(2)}, u32[]{:S(2)}) collective-permute-start(bf16[2,2,1,1,48,512]{5,4,3,2,1,0:T(8,128)(2,1)S(1)} %pad_maximum_fusion.26), channel_id=1, source_target_pairs={{0,2},{2,0},{4,6},{6,4},{8,10},{10,8},{12,14},{14,12},{16,18},{18,... | collective-permute-start | bytes 589832 | tf_op jit(solution)/shard_map/ppermute | solution.py:352
  98.7 18.6 %collective-permute-start.42 = (bf16[2,2,1,2,48,512]{5,4,3,2,1,0:T(8,128)(2,1)S(1)}, bf16[2,2,1,2,48,512]{5,4,3,2,1,0:T(8,128)(2,1)S(1)}, u32[]{:S(2)}, u32[]{:S(2)}) collective-permute-start(bf16[2,2,1,2,48,512]{5,4,3,2,1,0:T(8,128)(2,1)S(1)} %pad_maximum_fusion.16), channel_id=1, source_target_pairs={{0,4},{2,6},{4,0},{6,2},{8,12},{10,14},{12,8},{14,10},{16,20},{18,... | collective-permute-start | bytes 1179656 | tf_op jit(solution)/shard_map/ppermute | solution.py:352
  100.3 19.5 %collective-permute-start.47 = (bf16[2,2,2,1,48,512]{5,4,3,2,1,0:T(8,128)(2,1)S(1)}, bf16[2,2,2,1,48,512]{5,4,3,2,1,0:T(8,128)(2,1)S(1)}, u32[]{:S(2)}, u32[]{:S(2)}) collective-permute-start(bf16[2,2,2,1,48,512]{5,4,3,2,1,0:T(8,128)(2,1)S(1)} %pad_maximum_fusion.17), channel_id=1, source_target_pairs={{0,2},{2,0},{4,6},{6,4},{8,10},{10,8},{12,14},{14,12},{16,18},{18,... | collective-permute-start | bytes 1179656 | tf_op jit(solution)/shard_map/ppermute | solution.py:352
  102.6 59.0 %collective-permute-start.32 = (bf16[2,2,1,2,48,512]{5,4,3,2,1,0:T(8,128)(2,1)S(1)}, bf16[2,2,1,2,48,512]{5,4,3,2,1,0:T(8,128)(2,1)S(1)}, u32[]{:S(2)}, u32[]{:S(2)}) collective-permute-start(bf16[2,2,1,2,48,512]{5,4,3,2,1,0:T(8,128)(2,1)S(1)} %pad_maximum_fusion.14), channel_id=1, source_target_pairs={{0,4},{2,6},{4,0},{6,2},{8,12},{10,14},{12,8},{14,10},{16,20},{18,... | collective-permute-start | bytes 1179656 | tf_op jit(solution)/shard_map/ppermute | solution.py:352
  106.4 72.4 %collective-permute-start.37 = (bf16[2,2,2,1,48,512]{5,4,3,2,1,0:T(8,128)(2,1)S(1)}, bf16[2,2,2,1,48,512]{5,4,3,2,1,0:T(8,128)(2,1)S(1)}, u32[]{:S(2)}, u32[]{:S(2)}) collective-permute-start(bf16[2,2,2,1,48,512]{5,4,3,2,1,0:T(8,128)(2,1)S(1)} %pad_maximum_fusion.15), channel_id=1, source_target_pairs={{0,2},{2,0},{4,6},{6,4},{8,10},{10,8},{12,14},{14,12},{16,18},{18,... | collective-permute-start | bytes 1179656 | tf_op jit(solution)/shard_map/ppermute | solution.py:352
  108.9 23.7 %collective-permute-start.10 = (bf16[2,2,1,2,48,768]{5,4,3,2,1,0:T(8,128)(2,1)S(1)}, bf16[2,2,1,2,48,768]{5,4,3,2,1,0:T(8,128)(2,1)S(1)}, u32[]{:S(2)}, u32[]{:S(2)}) collective-permute-start(bf16[2,2,1,2,48,768]{5,4,3,2,1,0:T(8,128)(2,1)S(1)} %pad_maximum_fusion.10), channel_id=1, source_target_pairs={{0,4},{2,6},{4,0},{6,2},{8,12},{10,14},{12,8},{14,10},{16,20},{18,... | collective-permute-start | bytes 1769480 | tf_op jit(solution)/shard_map/ppermute | solution.py:352
  117.3 15.9 %collective-permute-start.15 = (bf16[2,2,2,1,48,768]{5,4,3,2,1,0:T(8,128)(2,1)S(1)}, bf16[2,2,2,1,48,768]{5,4,3,2,1,0:T(8,128)(2,1)S(1)}, u32[]{:S(2)}, u32[]{:S(2)}) collective-permute-start(bf16[2,2,2,1,48,768]{5,4,3,2,1,0:T(8,128)(2,1)S(1)} %pad_maximum_fusion.11), channel_id=1, source_target_pairs={{0,2},{2,0},{4,6},{6,4},{8,10},{10,8},{12,14},{14,12},{16,18},{18,... | collective-permute-start | bytes 1769480 | tf_op jit(solution)/shard_map/ppermute | solution.py:352
  119.9 60.0 %collective-permute-start.22 = (bf16[2,2,1,2,48,512]{5,4,3,2,1,0:T(8,128)(2,1)S(1)}, bf16[2,2,1,2,48,512]{5,4,3,2,1,0:T(8,128)(2,1)}, u32[]{:S(2)}, u32[]{:S(2)}) collective-permute-start(bf16[2,2,1,2,48,512]{5,4,3,2,1,0:T(8,128)(2,1)S(1)} %pad_maximum_fusion.12), channel_id=1, source_target_pairs={{0,4},{2,6},{4,0},{6,2},{8,12},{10,14},{12,8},{14,10},{16,20},{18,... | collective-permute-start | bytes 1179656 | tf_op jit(solution)/shard_map/ppermute | solution.py:352
  132.6 49.4 %collective-permute-start.27 = (bf16[2,2,2,1,48,512]{5,4,3,2,1,0:T(8,128)(2,1)S(1)}, bf16[2,2,2,1,48,512]{5,4,3,2,1,0:T(8,128)(2,1)S(1)}, u32[]{:S(2)}, u32[]{:S(2)}) collective-permute-start(bf16[2,2,2,1,48,512]{5,4,3,2,1,0:T(8,128)(2,1)S(1)} %pad_maximum_fusion.13), channel_id=1, source_target_pairs={{0,2},{2,0},{4,6},{6,4},{8,10},{10,8},{12,14},{14,12},{16,18},{18,... | collective-permute-start | bytes 1179656 | tf_op jit(solution)/shard_map/ppermute | solution.py:352
  160.5 22.5 %collective-permute-start.17 = (bf16[1024,768]{1,0:T(8,128)(2,1)}, bf16[1024,768]{1,0:T(8,128)(2,1)S(1)}, u32[]{:S(2)}, u32[]{:S(2)}) collective-permute-start(bf16[1024,768]{1,0:T(8,128)(2,1)} %get-tuple-element.59), channel_id=1, source_target_pairs={{0,1},{1,0},{2,3},{3,2},{4,5},{5,4},{6,7},{7,6},{8,9},{9,8},{10,11... | collective-permute-start | bytes 4718600 | tf_op jit(solution)/shard_map/ppermute | solution.py:357
  205.4 44.5 %collective-permute-start.77 = (bf16[2,2,2,1,48,512]{5,4,3,2,1,0:T(8,128)(2,1)}, bf16[2,2,2,1,48,512]{5,4,3,2,1,0:T(8,128)(2,1)}, u32[]{:S(2)}, u32[]{:S(2)}) collective-permute-start(bf16[2,2,2,1,48,512]{5,4,3,2,1,0:T(8,128)(2,1)} %dynamic-slice_convert_fusion.4), channel_id=1, source_target_pairs={{0,2},{2,0},{4,6},{6,4},{8,10},{10,8},{12,14},{14,12},{16,18},{18,... | collective-permute-start | bytes 1179656 | tf_op jit(solution)/shard_map/ppermute | solution.py:352
  208.8 44.8 %collective-permute-start.62 = (bf16[2,2,1,2,48,512]{5,4,3,2,1,0:T(8,128)(2,1)}, bf16[2,2,1,2,48,512]{5,4,3,2,1,0:T(8,128)(2,1)S(1)}, u32[]{:S(2)}, u32[]{:S(2)}) collective-permute-start(bf16[2,2,1,2,48,512]{5,4,3,2,1,0:T(8,128)(2,1)} %dynamic-slice_convert_fusion.7), channel_id=1, source_target_pairs={{0,4},{2,6},{4,0},{6,2},{8,12},{10,14},{12,8},{14,10},{16,20},{18,... | collective-permute-start | bytes 1179656 | tf_op jit(solution)/shard_map/ppermute | solution.py:352
  227.0 25.1 %collective-permute-start.82 = (bf16[2,2,2,1,48,512]{5,4,3,2,1,0:T(8,128)(2,1)}, bf16[2,2,2,1,48,512]{5,4,3,2,1,0:T(8,128)(2,1)}, u32[]{:S(2)}, u32[]{:S(2)}) collective-permute-start(bf16[2,2,2,1,48,512]{5,4,3,2,1,0:T(8,128)(2,1)} %dynamic-slice_convert_fusion.3), channel_id=1, source_target_pairs={{0,2},{2,0},{4,6},{6,4},{8,10},{10,8},{12,14},{14,12},{16,18},{18,... | collective-permute-start | bytes 1179656 | tf_op jit(solution)/shard_map/ppermute | solution.py:352
  247.4 19.7 %collective-permute-start.72 = (bf16[2,2,1,2,48,512]{5,4,3,2,1,0:T(8,128)(2,1)S(1)}, bf16[2,2,1,2,48,512]{5,4,3,2,1,0:T(8,128)(2,1)S(1)}, u32[]{:S(2)}, u32[]{:S(2)}) collective-permute-start(bf16[2,2,1,2,48,512]{5,4,3,2,1,0:T(8,128)(2,1)S(1)} %dynamic-slice_convert_fusion.5), channel_id=1, source_target_pairs={{0,4},{2,6},{4,0},{6,2},{8,12},{10,14},{12,8},{14,10},{16,20},{18,... | collective-permute-start | bytes 1179656 | tf_op jit(solution)/shard_map/ppermute | solution.py:352
  249.9 18.1 %collective-permute-start.87 = (bf16[2,2,2,1,48,512]{5,4,3,2,1,0:T(8,128)(2,1)S(1)}, bf16[2,2,2,1,48,512]{5,4,3,2,1,0:T(8,128)(2,1)S(1)}, u32[]{:S(2)}, u32[]{:S(2)}) collective-permute-start(bf16[2,2,2,1,48,512]{5,4,3,2,1,0:T(8,128)(2,1)S(1)} %dynamic-slice_convert_fusion.2), channel_id=1, source_target_pairs={{0,2},{2,0},{4,6},{6,4},{8,10},{10,8},{12,14},{14,12},{16,18},{18,... | collective-permute-start | bytes 1179656 | tf_op jit(solution)/shard_map/ppermute | solution.py:352
  252.1 69.8 %collective-permute-start.48 = (bf16[2048,768]{1,0:T(8,128)(2,1)S(1)}, bf16[2048,768]{1,0:T(8,128)(2,1)}, u32[]{:S(2)}, u32[]{:S(2)}) collective-permute-start(bf16[2048,768]{1,0:T(8,128)(2,1)S(1)} %copy-done.10), channel_id=1, source_target_pairs={{0,1},{1,0},{2,3},{3,2},{4,5},{5,4},{6,7},{7,6},{8,9},{9,8},{10,11... | collective-permute-start | bytes 9437192 | tf_op jit(solution)/shard_map/ppermute | solution.py:357
  253.7 65.1 %collective-permute-start.49 = (bf16[2048,768]{1,0:T(8,128)(2,1)S(1)}, bf16[2048,768]{1,0:T(8,128)(2,1)S(1)}, u32[]{:S(2)}, u32[]{:S(2)}) collective-permute-start(bf16[2048,768]{1,0:T(8,128)(2,1)S(1)} %copy-done.4), channel_id=1, source_target_pairs={{0,1},{1,0},{2,3},{3,2},{4,5},{5,4},{6,7},{7,6},{8,9},{9,8},{10,11... | collective-permute-start | bytes 9437192 | tf_op jit(solution)/shard_map/ppermute | solution.py:357
  394.8 14.9 %collective-permute-start.52 = (bf16[2,2,1,2,48,768]{5,4,3,2,1,0:T(8,128)(2,1)}, bf16[2,2,1,2,48,768]{5,4,3,2,1,0:T(8,128)(2,1)}, u32[]{:S(2)}, u32[]{:S(2)}) collective-permute-start(bf16[2,2,1,2,48,768]{5,4,3,2,1,0:T(8,128)(2,1)} %dynamic-slice_convert_fusion.1), channel_id=1, source_target_pairs={{0,4},{2,6},{4,0},{6,2},{8,12},{10,14},{12,8},{14,10},{16,20},{18,... | collective-permute-start | bytes 1769480 | tf_op jit(solution)/shard_map/ppermute | solution.py:352
  405.3 32.8 %collective-permute-start.51 = (bf16[1024,768]{1,0:T(8,128)(2,1)}, bf16[1024,768]{1,0:T(8,128)(2,1)S(1)}, u32[]{:S(2)}, u32[]{:S(2)}) collective-permute-start(bf16[1024,768]{1,0:T(8,128)(2,1)} %get-tuple-element.79), channel_id=1, source_target_pairs={{0,1},{1,0},{2,3},{3,2},{4,5},{5,4},{6,7},{7,6},{8,9},{9,8},{10,11... | collective-permute-start | bytes 4718600 | tf_op jit(solution)/shard_map/ppermute | solution.py:357
  405.3 32.8 %collective-permute-start.50 = (bf16[1024,768]{1,0:T(8,128)(2,1)S(1)}, bf16[1024,768]{1,0:T(8,128)(2,1)S(1)}, u32[]{:S(2)}, u32[]{:S(2)}) collective-permute-start(bf16[1024,768]{1,0:T(8,128)(2,1)S(1)} %copy-done.8), channel_id=1, source_target_pairs={{0,1},{1,0},{2,3},{3,2},{4,5},{5,4},{6,7},{7,6},{8,9},{9,8},{10,11... | collective-permute-start | bytes 4718600 | tf_op jit(solution)/shard_map/ppermute | solution.py:357
  (110 other events, 1033.9 us)

commit v2 on v0

v2 whole, which is shorter than its diff:
```python
import functools

import jax
import jax.numpy as jnp
from jax import lax
from jax.experimental import pallas as pl
from jax.experimental.pallas import tpu as pltpu
from jax.sharding import PartitionSpec as P

DH = 64
LANES = 128
EPS = 1e-06
NEG = -1000000000.0
VMEM_LIMIT = 56 * 1024 * 1024
BF = jnp.bfloat16
F32 = jnp.float32
ANY = pl.BlockSpec(memory_space=pl.ANY)
SMEM = pl.BlockSpec(memory_space=pltpu.SMEM)
VMEM = pl.BlockSpec(memory_space=pltpu.VMEM)


def dot(left, right):
    return jnp.dot(left, right, preferred_element_type=F32)


def dot_rows(left, right):
    return lax.dot_general(left, right, (((0,), (0,)), ((), ())), preferred_element_type=F32)


def dot_cols(left, right):
    return lax.dot_general(left, right, (((1,), (1,)), ((), ())), preferred_element_type=F32)


def tiles(array, rows):
    return pl.BlockSpec((rows,) + array.shape[1:], lambda i: (i,) + (0,) * (array.ndim - 1))


def fixed(array):
    return pl.BlockSpec(array.shape, lambda i: (0,) * array.ndim)


def pair_tiles(pair, rows):
    count = pair[0].shape[0] // rows
    rest = (0,) * (pair[0].ndim - 1)
    shape = (rows,) + pair[0].shape[1:]
    return [
        pl.BlockSpec(shape, lambda i: (jnp.minimum(i, count - 1),) + rest),
        pl.BlockSpec(shape, lambda i: (jnp.maximum(i - count, 0),) + rest),
    ]


def pick(count, first, second):
    return jnp.where(pl.program_id(0) < count, first[...], second[...])


def out_of(shape, kind):
    return jax.ShapeDtypeStruct(tuple(shape), kind)


def call(kernel, outs, args, *, ins=None, out_specs=None, grid=None, scratch=(), flops=0, after=()):
    ins = list(ins or [VMEM] * len(args))
    extra = {} if grid is None else {"grid": grid}

    def body(*refs):
        kernel(*refs[: len(args)], *refs[len(args) + len(after) :])

    moved = sum(o.size * o.dtype.itemsize for o in outs) + sum(a.size * a.dtype.itemsize for a in args)
    return pl.pallas_call(
        body,
        out_shape=list(outs),
        in_specs=ins + [ANY] * len(after),
        out_specs=list(out_specs or [VMEM] * len(outs)),
        scratch_shapes=list(scratch),
        compiler_params=pltpu.CompilerParams(vmem_limit_bytes=VMEM_LIMIT),
        cost_estimate=pl.CostEstimate(flops=int(flops), bytes_accessed=int(moved), transcendentals=0),
        **extra,
    )(*args, *after)


class Ring:
    def __init__(self, sizes):
        self.dp, self.mp = sizes
        self.me = lax.axis_index("dp")
        self.odd = lax.axis_index("mp") & 1
        self.quarter = self.dp // 4
        j = jnp.arange(self.dp, dtype=jnp.int32)
        first = (j // self.quarter) & 1
        last = j // (2 * self.quarter)
        low = jnp.where(self.odd == 0, first + 2 * last, 2 * first + last)
        self.places = self.me ^ (4 * (j % self.quarter) + low)
        rel = self.me ^ j
        bit0, bit1 = rel & 1, (rel >> 1) & 1
        first, last = jnp.where(self.odd == 0, bit0, bit1), jnp.where(self.odd == 0, bit1, bit0)
        self.spots = (rel >> 2) + self.quarter * (first + 2 * last)

    def far(self, array, step):
        return lax.ppermute(array, "dp", [(i, i ^ (4 * step)) for i in range(self.dp)])

    def near(self, array, masks):
        pairs = [
            (i * self.mp + c, (i ^ masks[c & 1]) * self.mp + c)
            for i in range(self.dp)
            for c in range(self.mp)
        ]
        return lax.ppermute(array, ("dp", "mp"), pairs)

    def exchange(self, array):
        return [
            lax.ppermute(array, "mp", [(i, i ^ k) for i in range(self.mp)])
            for k in range(1, self.mp)
        ]


def join_kernel(*refs):
    sources, out = refs[:-1], refs[-1]
    at = 0
    for ref in sources:
        out[at : at + ref.shape[0]] = ref[...]
        at += ref.shape[0]


def join(parts, after=()):
    count = sum(p.shape[0] for p in parts)
    shape = (count,) + parts[0].shape[1:]
    return call(join_kernel, [out_of(shape, parts[0].dtype)], parts, after=after)[0]


def aligned(rows):
    return rows % 16 == 0


def blocks_of(ring, held, got):
    if aligned(held.shape[1]):
        return (held, got)
    blocks = jnp.take(jnp.concatenate([held, got], 0), ring.spots, axis=0)
    return (blocks.reshape((-1,) + held.shape[2:]),)


def load_start(places, sources, to, sem, cols):
    copies = []
    if len(sources) == 2:
        half, rows, _ = sources[0].shape
        for j in range(2 * half):
            at = pl.multiple_of(places[j] * rows, 16)
            block = sources[j // half].at[j % half, :, cols]
            copies.append(pltpu.make_async_copy(block, to.at[pl.ds(at, rows)], sem.at[j]))
    else:
        copies.append(pltpu.make_async_copy(sources[0].at[:, cols], to, sem.at[0]))
    for c in copies:
        c.start()
    return copies


def load(places, sources, to, sem, cols):
    for c in load_start(places, sources, to, sem, cols):
        c.wait()


def emit(places, total, keep, send, extra=None):
    half, rows, _ = keep.shape
    for j in range(2 * half):
        at = pl.multiple_of(places[j] * rows, 16)
        block = total[pl.ds(at, rows), :]
        if extra is not None:
            block = block + extra
        if j < half:
            keep[j] = block
        else:
            send[j - half] = block.astype(BF)


def emitted(ring, rows, cols):
    share = rows // ring.dp
    if aligned(share):
        shape = (ring.dp // 2, share, cols)
        return [out_of(shape, F32), out_of(shape, BF)]
    return [out_of((rows, cols), F32)]


def halves(ring, outs, extra=None):
    if len(outs) == 2:
        return outs
    blocks = outs[0].reshape(ring.dp, -1, outs[0].shape[1])
    if extra is not None:
        blocks = blocks + extra
    blocks = jnp.take(blocks, ring.places, axis=0)
    return blocks[: ring.dp // 2], blocks[ring.dp // 2 :].astype(BF)


def fold_kernel(keep_ref, got_ref, *refs):
    quarter = got_ref.shape[0] // 2
    keep, sends = refs[0], refs[1:]
    for j in range(quarter):
        keep[j] = keep_ref[j] + got_ref[j].astype(F32)
    for j in range(quarter):
        total = (keep_ref[quarter + j] + got_ref[quarter + j].astype(F32)).astype(BF)
        sends[0][j] = total


def fold(keep, got, after=()):
    quarter = keep.shape[0] // 2
    shape = (quarter,) + keep.shape[1:]
    return call(fold_kernel, [out_of(shape, F32), out_of(shape, BF)], [keep, got], after=after)


def part_kernel(keep_ref, got_ref, keep, *sends):
    keep[...] = keep_ref[0] + got_ref[0].astype(F32)
    for j, send in enumerate(sends):
        send[...] = (keep_ref[j + 1] + got_ref[j + 1].astype(F32)).astype(BF)


def part(keep, got, after=()):
    shape = keep.shape[1:]
    outs = [out_of(shape, F32)] + [out_of(shape, BF)] * (keep.shape[0] - 1)
    return call(part_kernel, outs, [keep, got], after=after)


def final_kernel(spans, groups, keep, *refs):
    got, outs = refs[:groups], refs[groups:]
    for out, span in zip(outs, spans):
        at = 0
        for start, stop in span:
            total = keep[:, start:stop]
            for g in got:
                total = total + g[:, start:stop].astype(F32)
            out[:, at : at + stop - start] = total
            at += stop - start


def final(keep, got, spans, after=()):
    outs = [out_of((keep.shape[0], sum(b - a for a, b in span)), F32) for span in spans]
    return call(functools.partial(final_kernel, spans, len(got)), outs, [keep, *got], after=after)


def distance_buckets(bounds_ref, dist, buckets):
    size = jnp.abs(dist)
    half = jnp.zeros(dist.shape, jnp.int32)
    for b in range(bounds_ref.shape[0]):
        half += (size >= bounds_ref[b]).astype(jnp.int32)
    return half + jnp.where(dist > 0, buckets // 2, 0)


def bases_kernel(bounds_ref, table_ref, near_ref, far_ref):
    heads, _, width = near_ref.shape
    buckets = table_ref.shape[1]
    for ref, sign in ((near_ref, 1), (far_ref, -1)):
        dist = sign * (lax.broadcasted_iota(jnp.int32, (8, width), 1) - width // 2)
        marks = distance_buckets(bounds_ref, dist, buckets)
        marks = jnp.concatenate([marks] * (buckets // 8), 0)
        onehot = (marks == lax.broadcasted_iota(jnp.int32, (buckets, width), 0)).astype(F32)
        line = dot(table_ref[...], onehot.astype(BF))
        row = lax.broadcasted_iota(jnp.int32, (8, width), 0)
        for h in range(heads):
            field = jnp.broadcast_to(line[h : h + 1], (8, width))
            for k in (1, 2, 4):
                field = jnp.where((row & k) != 0, pltpu.roll(field, k, 1), field)
            while field.shape[0] < LANES:
                field = jnp.concatenate([field, pltpu.roll(field, field.shape[0], 1)], 0)
            ref[h] = field


def bias_bases(boundaries, table, heads, width):
    rows = jnp.zeros((8, table.shape[0]), table.dtype).at[: table.shape[1]].set(table.T)
    shape = out_of((heads, LANES, width), F32)
    return call(bases_kernel, [shape, shape], [boundaries, rows], ins=[SMEM, VMEM])


def bucket_field(bounds_ref, fields, buckets, first):
    width = fields[0].shape[-1]
    dist = width // 2 - lax.broadcasted_iota(jnp.int32, (8, width), 1)
    marks = distance_buckets(bounds_ref, dist, buckets)
    row = lax.broadcasted_iota(jnp.int32, (8, width), 0)
    line = jnp.zeros((8, width), F32)
    for h, field in enumerate(fields):
        while field.shape[0] > 8:
            half = field.shape[0] // 2
            field = field[:half] + pltpu.roll(field[half:], width - half, 1)
        for k in (4, 2, 1):
            field = jnp.where((row & k) != 0, pltpu.roll(field, width - k, 1), field)
        line = jnp.where(row == h, jnp.sum(field, 0, keepdims=True), line)
    lane = lax.broadcasted_iota(jnp.int32, (8, LANES), 1)
    out = jnp.zeros((8, LANES), F32)
    for b in range(buckets):
        total = jnp.sum(jnp.where(marks == b, line, 0.0), 1, keepdims=True)
        out = jnp.where(lane == first + b, total, out)
    return out


def split_low(values, lane, off, rest):
    high = values.astype(BF).astype(F32)
    mid = (values - high).astype(BF).astype(F32)
    low = values - high - mid
    return jnp.where(
        lane == off,
        high,
        jnp.where(lane == off + 1, mid, jnp.where(lane == off + 2, low, rest)),
    )


def three_ones(lane, off):
    return jnp.where((lane >= off) & (lane < off + 3), 1.0, 0.0)


def slots_of(batches):
    at = 0
    for b, (slots, length) in enumerate(batches):
        for s in range(slots):
            yield b, s, length, slice(at, at + length)
            at += length


def attend_kernel(batches, pair, halves, *refs):
    places, lens = refs[0], refs[1 : 1 + len(batches)]
    refs = refs[1 + len(batches) :]
    normed_ref, near_ref = refs[:2]
    sources = refs[2 : 2 + halves]
    aug_ref, k_ref, v_ref, o_ref, w_scr, sem = refs[2 + halves :]
    width = near_ref.shape[-1]
    load(places, sources, w_scr, sem, pl.ds(pair * 3 * LANES, 3 * LANES))
    for b, s, length, span in slots_of(batches):
        valid = lens[b][s]
        lane = lax.broadcasted_iota(jnp.int32, (length, LANES), 1)
        place = lax.broadcasted_iota(jnp.int32, (length, LANES), 0)
        masked = jnp.where(place >= valid, NEG, 0.0)
        qkv = dot(normed_ref[span, :], w_scr[...])
        q, k, v = (qkv[:, i * LANES : (i + 1) * LANES] for i in range(3))
        k_ref[span, :] = k.astype(BF)
        v_ref[span, :] = v.astype(BF)
        mixed = []
        for e in range(2):
            own = (lane >= DH) == (e == 1)
            off = DH * (1 - e)
            marker = jnp.where(lane == off + 3, 1.0, 0.0)
            q_own = jnp.where(own, q, marker).astype(BF)
            k_own = jnp.where(own, k, jnp.where(lane == off + 3, masked, 0.0)).astype(BF)
            v_own = jnp.where(own, v, 1.0).astype(BF)
            tops = []
            sums = []
            for a in range(length // LANES):
                rows = slice(a * LANES, (a + 1) * LANES)
                start = width // 2 - a * LANES
                scores = dot_cols(q_own[rows], k_own) + near_ref[e, :, start : start + length]
                top = jnp.max(scores, 1, keepdims=True)
                expo = jnp.exp(scores - top)
                tops.append(jnp.broadcast_to(top, (LANES, LANES)))
                sums.append(dot(expo.astype(BF), v_own))
            sums = jnp.concatenate(sums, 0)
            total = jnp.where(own, pltpu.roll(sums, DH, 1), sums)
            logsum = jnp.concatenate(tops, 0) + jnp.log(total)
            extra = split_low(-logsum, lane, off, marker)
            aug_ref[span, e * LANES : (e + 1) * LANES] = jnp.where(own, q, extra).astype(BF)
            mixed.append(sums / total)
        o_ref[span, :] = jnp.where(lane < DH, mixed[0], mixed[1]).astype(BF)


def pair_of(near, pair):
    return pl.BlockSpec((2,) + near.shape[1:], lambda i: (pair, 0, 0))


def attend(ring, batches, lens, normed, weights, near, pair, after=()):
    rows, width = normed.shape
    shapes = [out_of((rows, c * LANES), BF) for c in (2, 1, 1, 1)]
    return call(
        functools.partial(attend_kernel, batches, pair, len(weights)),
        shapes,
        [ring.places, *lens, normed, near, *weights],
        ins=[SMEM] * (1 + len(lens)) + [fixed(normed), pair_of(near, pair)] + [ANY] * len(weights),
        out_specs=[fixed(s) for s in shapes],
        grid=(1,),
        scratch=[pltpu.VMEM((width, 3 * LANES), BF), pltpu.SemaphoreType.DMA((ring.dp,))],
        flops=1e10,
        after=after,
    )


def attend_back_kernel(batches, *refs):
    lens = refs[: len(batches)]
    go_ref, aug_ref, k_ref, v_ref, o_ref, far_ref, grads_ref, gbase_ref, ds_scr = refs[len(batches) :]
    width = far_ref.shape[-1]
    gbase_ref[...] = jnp.zeros_like(gbase_ref)
    for b, s, length, span in slots_of(batches):
        valid = lens[b][s]
        lane = lax.broadcasted_iota(jnp.int32, (length, LANES), 1)
        place = lax.broadcasted_iota(jnp.int32, (length, LANES), 0)
        masked = jnp.where(place >= valid, NEG, 0.0)
        k = k_ref[span, :].astype(F32)
        v = v_ref[span, :].astype(F32)
        go = go_ref[span, :].astype(F32)
        both = go * o_ref[span, :].astype(F32)
        grads = []
        for e in range(2):
            own = (lane >= DH) == (e == 1)
            off = DH * (1 - e)
            q_own = aug_ref[span, e * LANES : (e + 1) * LANES]
            ones = three_ones(lane, off)
            k_own = jnp.where(own, k, jnp.where(lane == off + 3, masked, ones)).astype(BF)
            v_own = jnp.where(own, v, ones).astype(BF)
            delta = jnp.sum(jnp.where(own, both, 0.0), 1, keepdims=True)
            g_own = jnp.where(own, go, split_low(-delta, lane, off, 0.0)).astype(BF)
            gks = []
            gvs = []
            for a in range(length // LANES):
                rows = slice(a * LANES, (a + 1) * LANES)
                start = width // 2 - a * LANES
                cols = slice(start, start + length)
                probs = jnp.exp(dot_cols(k_own[rows], q_own) + far_ref[e, :, cols])
                ds = probs * dot_cols(v_own[rows], g_own)
                gbase_ref[e, :, cols] += ds
                ds = ds.astype(BF)
                ds_scr[e, rows, :length] = ds
                gvs.append(dot(probs.astype(BF), g_own))
                gks.append(dot(ds, q_own))
            gq = dot_rows(ds_scr[e, :length, :length], k_own)
            grads.append((gq, jnp.concatenate(gks, 0), jnp.concatenate(gvs, 0)))
        first = lane < DH
        for i, (a, b) in enumerate(zip(*grads)):
            grads_ref[span, i * LANES : (i + 1) * LANES] = jnp.where(first, a, b).astype(BF)


def attend_back(batches, lens, go, aug, k, v, o, far, pair, after=()):
    rows = go.shape[0]
    longest = max(length for _, length in batches)
    outs = [out_of((rows, 3 * LANES), BF), out_of((2,) + far.shape[1:], F32)]
    go_spec = pl.BlockSpec((rows, LANES), lambda i: (0, pair))
    return call(
        functools.partial(attend_back_kernel, batches),
        outs,
        [*lens, go, aug, k, v, o, far],
        ins=[SMEM] * len(lens) + [go_spec] + [fixed(a) for a in (aug, k, v, o)] + [pair_of(far, pair)],
        out_specs=[fixed(o) for o in outs],
        grid=(1,),
        scratch=[pltpu.VMEM((2, longest, longest), BF)],
        flops=2e10,
        after=after,
    )


def project_out_kernel(halves, pairs, places, *refs):
    o_refs, refs = refs[:pairs], refs[pairs:]
    sources, (attn_ref, w_scr, sem) = refs[:halves], refs[halves:]
    cols = pairs * LANES

    @pl.when(pl.program_id(0) == 0)
    def _():
        load(places, sources, w_scr, sem, pl.ds(3 * cols, cols))

    o = jnp.concatenate([r[...] for r in o_refs], 1)
    attn_ref[...] = dot_cols(o, w_scr[...]).astype(BF)


def project_out(ring, mixed, weights, width, tile=512):
    rows = mixed[0].shape[0]
    pairs = len(mixed)
    out = out_of((rows, width), BF)
    return call(
        functools.partial(project_out_kernel, len(weights), pairs),
        [out],
        [ring.places, *mixed, *weights],
        ins=[SMEM] + [tiles(m, tile) for m in mixed] + [ANY] * len(weights),
        out_specs=[tiles(out, tile)],
        grid=(rows // tile,),
        scratch=[pltpu.VMEM((width, pairs * LANES), BF), pltpu.SemaphoreType.DMA((ring.dp,))],
        flops=2 * rows * width * pairs * LANES,
    )[0]


def rms_parts(field):
    scale = lax.rsqrt(jnp.mean(field * field, -1, keepdims=True) + EPS)
    return (scale, field * scale)


def norm_back(grad_unit, unit, scale):
    return scale * (grad_unit - unit * jnp.mean(grad_unit * unit, -1, keepdims=True))


def total_of(count, refs):
    total = pick(count, *refs[:2]).astype(F32)
    for r in refs[2:]:
        total = total + r[...].astype(F32)
    return total


def norm_kernel(count, gain_ref, short_ref, long_ref, normed_ref):
    unit = rms_parts(pick(count, short_ref, long_ref).astype(F32))[1]
    normed_ref[...] = (unit * gain_ref[0:1, :]).astype(BF)


def norm(gains, xs, tile=512, after=()):
    out = out_of((xs[0].shape[0] + xs[1].shape[0], xs[0].shape[1]), BF)
    return call(
        functools.partial(norm_kernel, xs[0].shape[0] // tile),
        [out],
        [gains, *xs],
        ins=[fixed(gains)] + pair_tiles(xs, tile),
        out_specs=[tiles(out, tile)],
        grid=(out.shape[0] // tile,),
        after=after,
    )[0]


def store_pair(count, first, second, value):
    @pl.when(pl.program_id(0) < count)
    def _():
        first[...] = value

    @pl.when(pl.program_id(0) >= count)
    def _():
        second[...] = value


def add_kernel(count, addends, *refs):
    store_pair(count, *refs[addends:], total_of(count, refs[:addends]).astype(BF))


def add_all(xs, fields, tile=512, after=()):
    outs = [out_of(x.shape, BF) for x in xs]
    return call(
        functools.partial(add_kernel, xs[0].shape[0] // tile, 2 + len(fields)),
        outs,
        [*xs, *fields],
        ins=pair_tiles(xs, tile) + [tiles(f, tile) for f in fields],
        out_specs=pair_tiles(outs, tile),
        grid=((xs[0].shape[0] + xs[1].shape[0]) // tile,),
        after=after,
    )


def input_grad_kernel(count, gain_ref, short_ref, long_ref, mid_ref, *refs):
    scale, unit = rms_parts(pick(count, short_ref, long_ref).astype(F32))
    grad = refs[0][...].astype(F32)
    for r in refs[1:-2]:
        grad = grad + r[...].astype(F32)
    value = mid_ref[...] + norm_back(grad * gain_ref[0:1, :], unit, scale)
    store_pair(count, *refs[-2:], value.astype(BF))


def input_grad(gains, xs, mid, fields, tile=512, after=()):
    outs = [out_of(x.shape, BF) for x in xs]
    return call(
        functools.partial(input_grad_kernel, xs[0].shape[0] // tile),
        outs,
        [gains, *xs, mid, *fields],
        ins=[fixed(gains)] + pair_tiles(xs, tile) + [tiles(f, tile) for f in (mid, *fields)],
        out_specs=pair_tiles(outs, tile),
        grid=(mid.shape[0] // tile,),
        after=after,
    )


def gelu_parts(x):
    c = 0.7978845608028654
    d = c * 0.044715
    square = x * x
    t = jnp.tanh(x * (c + d * square))
    half = 0.5 + 0.5 * t
    slope = half + (0.5 * x) * (1.0 - t * t) * (c + 3.0 * d * square)
    return x * half, slope


def ffn_first_kernel(halves, addends, emits, count, places, gain_ref, *refs):
    g_refs, refs = refs[:2], refs[2:]
    x_refs, refs = refs[:addends], refs[addends:]
    sources, refs = refs[:halves], refs[halves:]
    normed_ref, out_ref, gn_ref = refs[:3]
    grads, (w_scr, total, sem) = refs[3 : 3 + emits], refs[3 + emits :]
    units = w_scr.shape[1] // 2
    step = pl.program_id(0)

    @pl.when(step == 0)
    def _():
        total[...] = jnp.zeros_like(total)
        load(places, sources, w_scr, sem, pl.ds(0, 2 * units))

    normed = (rms_parts(total_of(count, x_refs))[1] * gain_ref[1:2, :]).astype(BF)
    normed_ref[...] = normed
    g = pick(count, *g_refs)
    win, wout = w_scr[:, :units], w_scr[:, units:]
    act, slope = gelu_parts(dot(normed, win))
    act = act.astype(BF)
    gpre = (dot(g, wout) * slope).astype(BF)
    out_ref[...] = dot_cols(act, wout)
    gn_ref[...] = dot_cols(gpre, win)
    total[:, :units] += dot_rows(normed, gpre)
    total[:, units:] += dot_rows(g, act)

    @pl.when(step == pl.num_programs(0) - 1)
    def _():
        if emits == 2:
            emit(places, total, *grads)
        else:
            grads[0][...] = total[...]


def ffn_first(ring, gains, gs, xs, fields, weights, units, tile=512, after=()):
    rows, width = fields[0].shape
    normed, field = out_of((rows, width), BF), out_of((rows, width), F32)
    grads = emitted(ring, width, 2 * units)
    addends = 2 + len(fields)
    count = xs[0].shape[0] // tile
    return call(
        functools.partial(ffn_first_kernel, len(weights), addends, len(grads), count),
        [normed, field, field] + grads,
        [ring.places, gains, *gs, *xs, *fields, *weights],
        ins=[SMEM, fixed(gains)]
        + pair_tiles(gs, tile)
        + pair_tiles(xs, tile)
        + [tiles(a, tile) for a in fields]
        + [ANY] * len(weights),
        out_specs=[tiles(normed, tile), tiles(field, tile), tiles(field, tile)]
        + [fixed(o) for o in grads],
        grid=(rows // tile,),
        scratch=[
            pltpu.VMEM((width, 2 * units), BF),
            pltpu.VMEM((width, 2 * units), F32),
            pltpu.SemaphoreType.DMA((ring.dp,)),
        ],
        flops=12 * rows * width * units,
        after=after,
    )


def ffn_next_kernel(halves, count, places, normed_ref, *refs):
    g_refs, (out_in, gn_in), refs = refs[:2], refs[2:4], refs[4:]
    sources, refs = refs[:halves], refs[halves:]
    out_ref, gn_ref, act_ref, gpre_ref, w_scr, sem = refs
    units = w_scr.shape[1] // 2

    @pl.when(pl.program_id(0) == 0)
    def _():
        load(places, sources, w_scr, sem, pl.ds(0, 2 * units))

    win, wout = w_scr[:, :units], w_scr[:, units:]
    act, slope = gelu_parts(dot(normed_ref[...], win))
    act = act.astype(BF)
    gpre = (dot(pick(count, *g_refs), wout) * slope).astype(BF)
    act_ref[...] = act
    gpre_ref[...] = gpre
    out_ref[...] = (out_in[...] + dot_cols(act, wout)).astype(BF)
    gn_ref[...] = (gn_in[...] + dot_cols(gpre, win)).astype(BF)


def ffn_next(ring, normed, gs, out, gn, weights, units, tile=512, after=()):
    rows, width = normed.shape
    outs = [out_of((rows, width), BF)] * 2 + [out_of((rows, units), BF)] * 2
    return call(
        functools.partial(ffn_next_kernel, len(weights), gs[0].shape[0] // tile),
        outs,
        [ring.places, normed, *gs, out, gn, *weights],
        ins=[SMEM, tiles(normed, tile)]
        + pair_tiles(gs, tile)
        + [tiles(out, tile), tiles(gn, tile)]
        + [ANY] * len(weights),
        out_specs=[tiles(o, tile) for o in outs],
        grid=(rows // tile,),
        scratch=[pltpu.VMEM((width, 2 * units), BF), pltpu.SemaphoreType.DMA((ring.dp,))],
        flops=8 * rows * width * units,
        after=after,
    )


def ffn_grads_kernel(emits, count, places, normed_ref, *refs):
    g_refs, (gpre_ref, act_ref) = refs[:2], refs[2:4]
    grads, total = refs[4:-1], refs[-1]
    step = pl.program_id(0)
    units = act_ref.shape[1]

    @pl.when(step == 0)
    def _():
        total[...] = jnp.zeros_like(total)

    total[:, :units] += dot_rows(normed_ref[...], gpre_ref[...])
    total[:, units:] += dot_rows(pick(count, *g_refs), act_ref[...])

    @pl.when(step == pl.num_programs(0) - 1)
    def _():
        if emits == 2:
            emit(places, total, *grads)
        else:
            grads[0][...] = total[...]


def ffn_grads(ring, normed, gs, gpre, act, tile=512, after=()):
    rows, width = normed.shape
    cols = 2 * act.shape[1]
    outs = emitted(ring, width, cols)
    return call(
        functools.partial(ffn_grads_kernel, len(outs), gs[0].shape[0] // tile),
        outs,
        [ring.places, normed, *gs, gpre, act],
        ins=[SMEM, tiles(normed, tile)]
        + pair_tiles(gs, tile)
        + [tiles(gpre, tile), tiles(act, tile)],
        out_specs=[fixed(o) for o in outs],
        grid=(rows // tile,),
        scratch=[pltpu.VMEM((width, cols), F32)],
        flops=2 * rows * width * cols,
        after=after,
    )


def middle_back_kernel(halves, groups, pairs, count, places, gain_ref, *refs):
    g_refs, refs = refs[:2], refs[2:]
    x_refs, refs = refs[: groups + 2], refs[groups + 2 :]
    gn_refs, refs = refs[:groups], refs[groups:]
    sources, (mid_ref, attn_ref, go_ref, gain_out, w_scr, sem) = refs[:halves], refs[halves:]
    cols = pairs * LANES

    @pl.when(pl.program_id(0) == 0)
    def _():
        gain_out[...] = jnp.zeros_like(gain_out)
        load(places, sources, w_scr, sem, pl.ds(3 * cols, cols))

    scale, unit = rms_parts(total_of(count, x_refs))
    gn = gn_refs[0][...].astype(F32)
    for r in gn_refs[1:]:
        gn = gn + r[...].astype(F32)
    gain_out[...] += jnp.sum((gn * unit).reshape(-1, 8, unit.shape[1]), 0)
    mid = pick(count, *g_refs).astype(F32) + norm_back(gn * gain_ref[1:2, :], unit, scale)
    mid_ref[...] = mid
    grad = mid.astype(BF)
    attn_ref[...] = grad
    go_ref[...] = dot(grad, w_scr[...]).astype(BF)


def middle_back(ring, gains, gs, xs, fields, gns, weights, pairs, tile=512, after=()):
    rows, width = fields[0].shape
    cols = pairs * LANES
    outs = [out_of((rows, width), F32), out_of((rows, width), BF), out_of((rows, cols), BF)]
    gain = out_of((8, width), F32)
    return call(
        functools.partial(
            middle_back_kernel, len(weights), len(gns), pairs, xs[0].shape[0] // tile
        ),
        outs + [gain],
        [ring.places, gains, *gs, *xs, *fields, *gns, *weights],
        ins=[SMEM, fixed(gains)]
        + pair_tiles(gs, tile)
        + pair_tiles(xs, tile)
        + [tiles(a, tile) for a in (*fields, *gns)]
        + [ANY] * len(weights),
        out_specs=[tiles(o, tile) for o in outs] + [fixed(gain)],
        grid=(rows // tile,),
        scratch=[pltpu.VMEM((width, cols), BF), pltpu.SemaphoreType.DMA((ring.dp,))],
        flops=2 * rows * width * cols,
        after=after,
    )


def input_back_kernel(halves, pairs, count, places, short_ref, long_ref, *refs):
    g_refs, refs = refs[:pairs], refs[pairs:]
    sources, (part_ref, gain_out, w_scr, sem) = refs[:halves], refs[halves:]

    @pl.when(pl.program_id(0) == 0)
    def _():
        gain_out[...] = jnp.zeros_like(gain_out)
        load(places, sources, w_scr, sem, pl.ds(0, 3 * pairs * LANES))

    part = dot_cols(jnp.concatenate([r[...] for r in g_refs], 1), w_scr[...])
    unit = rms_parts(pick(count, short_ref, long_ref).astype(F32))[1]
    gain_out[...] += jnp.sum((part * unit).reshape(-1, 8, unit.shape[1]), 0)
    part_ref[...] = part.astype(BF)


def input_back(ring, xs, grads, weights, tile=512, after=()):
    rows, width = grads[0].shape[0], xs[0].shape[1]
    pairs = len(grads)
    out, gain = out_of((rows, width), BF), out_of((8, width), F32)
    return call(
        functools.partial(input_back_kernel, len(weights), pairs, xs[0].shape[0] // tile),
        [out, gain],
        [ring.places, *xs, *grads, *weights],
        ins=[SMEM] + pair_tiles(xs, tile) + [tiles(a, tile) for a in grads] + [ANY] * len(weights),
        out_specs=[tiles(out, tile), fixed(gain)],
        grid=(rows // tile,),
        scratch=[pltpu.VMEM((width, 3 * pairs * LANES), BF), pltpu.SemaphoreType.DMA((ring.dp,))],
        flops=2 * rows * width * 3 * pairs * LANES,
        after=after,
    )


def last_kernel(emits, pairs, buckets, places, bounds, normed_ref, grad_ref, gain_f, gain_a, *refs):
    g_refs, refs = refs[:pairs], refs[pairs:]
    o_refs, refs = refs[:pairs], refs[pairs:]
    bases, refs = refs[:pairs], refs[pairs:]
    grads, refs = refs[:emits], refs[emits:]
    table_ref, total = refs
    step = pl.program_id(0)
    cols = pairs * LANES

    @pl.when(step == 0)
    def _():
        total[...] = jnp.zeros_like(total)

    normed = normed_ref[...]
    grad = grad_ref[...]
    total[:, : 3 * cols] += dot_rows(normed, jnp.concatenate([r[...] for r in g_refs], 1))
    total[:, 3 * cols : 4 * cols] += dot_rows(grad, jnp.concatenate([r[...] for r in o_refs], 1))

    @pl.when(step == pl.num_programs(0) - 1)
    def _():
        row = lax.broadcasted_iota(jnp.int32, (LANES, total.shape[0]), 0)
        both = jnp.where(
            row == 0,
            jnp.sum(gain_a[...], 0, keepdims=True),
            jnp.where(row == 1, jnp.sum(gain_f[...], 0, keepdims=True), 0.0),
        )
        total[:, 4 * cols :] = jnp.transpose(both)
        fields = [ref[e] for ref in bases for e in range(2)]
        table = bucket_field(bounds, fields, buckets, 8)
        table_ref[...] = table
        if emits == 2:
            rows = grads[0].shape[1]
            table = jnp.concatenate([table, jnp.zeros((rows - 8, LANES), F32)], 0)
            table = jnp.concatenate([jnp.zeros((rows, 4 * cols), F32), table], 1)
            emit(places, total, *grads, extra=table)
        else:
            grads[0][...] = total[...]


def last_grads(ring, boundaries, buckets, normed, grad, gain_f, gain_a, grads, mixed, bases, tile=512):
    rows, width = normed.shape
    pairs = len(grads)
    cols = 4 * pairs * LANES + LANES
    outs = emitted(ring, width, cols)
    table = out_of((8, LANES), F32)
    *outs, table = call(
        functools.partial(last_kernel, len(outs), pairs, buckets),
        outs + [table],
        [ring.places, boundaries, normed, grad, gain_f, gain_a, *grads, *mixed, *bases],
        ins=[SMEM, SMEM, tiles(normed, tile), tiles(grad, tile), fixed(gain_f), fixed(gain_a)]
        + [tiles(a, tile) for a in (*grads, *mixed)]
        + [fixed(b) for b in bases],
        out_specs=[fixed(o) for o in outs] + [fixed(table)],
        grid=(rows // tile,),
        scratch=[pltpu.VMEM((width, cols), F32)],
        flops=2 * rows * width * cols,
    )
    share = width // ring.dp
    table = jnp.pad(table, ((0, share - 8), (cols - LANES, 0)))
    return halves(ring, outs, table)


def pad_cols(array, cols):
    return jnp.pad(array, ((0, 0), (0, cols - array.shape[1]))) if cols > array.shape[1] else array


def small_sum(array, size):
    bits = [1 << b for b in range(size.bit_length() - 1)]
    for i in range(0, len(bits), 2):
        masks = [0]
        for b in bits[i : i + 2]:
            masks = masks + [m | b for m in masks]
        total = array
        for m in masks[1:]:
            total = total + lax.ppermute(array, "dp", [(i, i ^ m) for i in range(size)])
        array = total
    return array


def small_gather(part, size, me):
    rows, share = part.shape
    wide = jnp.zeros((rows, share * size), part.dtype)
    return small_sum(lax.dynamic_update_slice_in_dim(wide, part, me * share, 1), size)


def on_device(
    sizes,
    x_short,
    x_long,
    len_short,
    len_long,
    boundaries,
    q_weight,
    k_weight,
    v_weight,
    out_weight,
    in_weight,
    ff_out_weight,
    attn_gain,
    ffn_gain,
    bias_table,
    cot_short,
    cot_long,
):
    ring = Ring(sizes)
    quarter = ring.quarter
    width = x_short.shape[2]
    buckets, heads = bias_table.shape
    real = heads * DH
    cols = -(-real // LANES) * LANES
    pairs = cols // LANES
    units = in_weight.shape[1] // 2
    span = 2 * max(x_short.shape[1], x_long.shape[1])
    batches = [x.shape[:2] for x in (x_short, x_long)]
    lens = (len_short, len_long)

    xs = [x.reshape(-1, width) for x in (x_short, x_long)]
    gs = [g.reshape(-1, width) for g in (cot_short, cot_long)]

    padded = [pad_cols(w, cols) for w in (q_weight, k_weight, v_weight, out_weight)]
    pieces = [w[:, p * LANES : (p + 1) * LANES] for p in range(pairs) for w in padded[:3]]
    own = jnp.concatenate(pieces + [padded[3]], 1)[None]
    got = [ring.far(own, s) for s in range(1, quarter)]
    gains = small_gather(jnp.stack([attn_gain, ffn_gain]).astype(F32), ring.dp, ring.me)
    near, far = bias_bases(boundaries, bias_table, cols // DH, span)
    normed = norm(gains, xs)
    held = join([own] + got, after=[near, normed])
    got = ring.near(held, (1, 2))
    ffn_own = [
        jnp.concatenate([w[:, at : at + units] for w in (in_weight, ff_out_weight)], 1)[None]
        for at in (0, units)
    ]
    own1 = join([ffn_own[0]], after=[held])
    got1 = [ring.far(own1, s) for s in range(1, quarter)]
    held = join([held, got])
    qkvo = blocks_of(ring, held, ring.near(held, (2, 1)))

    fwd = []
    after = ()
    for p in range(pairs):
        if p == 1:
            held1 = join([own1] + got1, after=[fwd[-1][0]])
            got1 = ring.near(held1, (1, 2))
            own2 = join([ffn_own[1]], after=[held1])
            got2 = [ring.far(own2, s) for s in range(1, quarter)]
            after = [held1, own2]
        if p == pairs - 1:
            held1 = join([held1, got1], after=[fwd[-1][0]])
            got1 = ring.near(held1, (2, 1))
            held2 = join([own2] + got2, after=[held1])
            got2 = ring.near(held2, (1, 2))
            after = [held1, held2]
        fwd.append(attend(ring, batches, lens, normed, qkvo, near, p, after=after))
    attn = project_out(ring, [f[3] for f in fwd], qkvo, width)
    fields = [attn] + ring.exchange(attn)
    held2 = join([held2, got2], after=[attn])
    got2 = ring.near(held2, (2, 1))
    first, second = blocks_of(ring, held1, got1), blocks_of(ring, held2, got2)

    normed_f, out, gn, *grad1 = ffn_first(
        ring, gains, gs, xs, fields, first, units, after=[held2]
    )
    keep1, send = halves(ring, grad1)
    got1 = ring.near(send, (2, 1))
    out, gn, act, gpre = ffn_next(ring, normed_f, gs, out, gn, second, units)
    gns = [gn] + ring.exchange(gn)
    outs = [out] + ring.exchange(out)
    keep1, send = fold(keep1, got1, after=[gn])
    got1 = ring.near(send, (1, 2))
    keep2, send = halves(ring, ffn_grads(ring, normed_f, gs, gpre, act, after=[keep1]))
    got2 = ring.near(send, (2, 1))
    mid, grad_attn, go, gain_f = middle_back(
        ring, gains, gs, xs, fields, gns, qkvo, pairs, after=[keep2]
    )

    back = []
    for p in range(pairs):
        if p == 0:
            keep1, *sends = part(keep1, got1, after=[go])
            got1 = [ring.far(s, i + 1) for i, s in enumerate(sends)]
            keep2, send = fold(keep2, got2, after=[keep1])
            got2 = ring.near(send, (1, 2))
            after = [keep2]
        if p == 1:
            keep2, *sends = part(keep2, got2, after=[back[-1][0]])
            got2 = [ring.far(s, i + 1) for i, s in enumerate(sends)]
            in1, out1 = final(keep1, got1, [[(0, units)], [(units, 2 * units)]])
            after = [keep2, in1]
        aug, k, v, o = fwd[p]
        back.append(attend_back(batches, lens, go, aug, k, v, o, far, p, after=after))

    grads = [b[0] for b in back]
    gna, gain_a = input_back(ring, xs, grads, qkvo)
    gnas = [gna] + ring.exchange(gna)
    keep, send = last_grads(
        ring,
        boundaries,
        buckets,
        normed,
        grad_attn,
        gain_f,
        gain_a,
        grads,
        [f[3] for f in fwd],
        [b[1] for b in back],
    )
    got = ring.near(send, (2, 1))
    grad_xs = input_grad(gains, xs, mid, gnas, after=[keep])
    keep, send = fold(keep, got, after=[grad_xs[0]])
    got = ring.near(send, (1, 2))
    ys = add_all(xs, [*fields, *outs], after=[keep])
    keep, *sends = part(keep, got, after=[ys[0]])
    got = [ring.far(s, i + 1) for i, s in enumerate(sends)]
    in2, out2 = final(keep2, got2, [[(0, units)], [(units, 2 * units)]], after=[keep])
    step = 3 * LANES
    at = [
        [(p * step + i * LANES, p * step + (i + 1) * LANES) for p in range(pairs)] for i in range(3)
    ]
    at += [[(3 * cols, 4 * cols)], [(4 * cols, 4 * cols + LANES)]]
    gq, gk, gv, go, small = final(keep, got, at)
    gain_a_grad = small[:, 0]
    for other in ring.exchange(gain_a_grad):
        gain_a_grad = gain_a_grad + other
    table_grad = small[:8, 8 : 8 + buckets].T[:, :heads]
    return (
        ys[0].reshape(x_short.shape),
        ys[1].reshape(x_long.shape),
        grad_xs[0].reshape(x_short.shape),
        grad_xs[1].reshape(x_long.shape),
        gq[:, :real],
        gk[:, :real],
        gv[:, :real],
        go[:, :real],
        jnp.concatenate([in1, in2], 1),
        jnp.concatenate([out1, out2], 1),
        gain_a_grad,
        small[:, 1],
        table_grad,
    )


def solution(mesh):
    sizes = (mesh.shape["dp"], mesh.shape["mp"])
    return jax.shard_map(
        functools.partial(on_device, sizes),
        mesh=mesh,
        in_specs=(
            P("dp", None, None),
            P("dp", None, None),
            P("dp"),
            P("dp"),
            P(),
            P("dp", "mp"),
            P("dp", "mp"),
            P("dp", "mp"),
            P("dp", "mp"),
            P("dp", "mp"),
            P("dp", "mp"),
            P("dp"),
            P("dp"),
            P(None, "mp"),
            P("dp", None, None),
            P("dp", None, None),
        ),
        out_specs=(
            P("dp", None, None),
            P("dp", None, None),
            P("dp", None, None),
            P("dp", None, None),
            P("dp", "mp"),
            P("dp", "mp"),
            P("dp", "mp"),
            P("dp", "mp"),
            P("dp", "mp"),
            P("dp", "mp"),
            P("dp"),
            P("dp"),
            P(None, "mp"),
        ),
        check_vma=False,
    )
```

time: 1490 us -> 402 us (0.27)
  waiting for transfers between devices: 767 us -> 63.2 us
  blocking collectives: 282 us -> 0 us
  Pallas kernels: 0 us -> 240 us
  matrix products: 208 us -> 0 us
  local copies, waits for them, and re-layouts: 148 us -> 33.3 us
  starting transfers between devices: 1.34 us -> 50.7 us
  other arithmetic: 50.7 us -> 7.7 us
  between operations: 18 us -> 1.38 us
    reduce_scatter x5 -> x0, waiting for transfers between devices: 513 us -> none  [the longest x1 142 us: on_device(): lax.psum_scatter(total[4], 'dp', scatter_dimension=0, tiled=True)]
    pallas_call x0 -> x34, Pallas kernels: none -> 240 us  [call(): pl.pallas_call(body, out_shape=list(outs), in_specs=ins + [ANY] * len(aft...]
    dot_general x74 -> x0, matrix products: 208 us -> none  [the longest x12 43.3 us: contract_rows(): lax.dot_general(left, right, (((0,), (0,)), ((), ())), preferred_element_...]
    all_gather x4 -> x0, blocking collectives: 162 us -> none  [the longest x1 42.5 us: on_device(): lax.all_gather(out_weight, 'dp', axis=0, tiled=True)]
    unnamed x12 -> x0, waiting for transfers between devices: 143 us -> none
    unnamed x2 -> x0, blocking collectives: 121 us -> none
    all_gather x2 -> x0, waiting for transfers between devices: 88.7 us -> none  [the longest x1 51.7 us: on_device(): lax.all_gather(in_weight, 'dp', axis=0, tiled=True)]
    ppermute x0 -> x41, waiting for transfers between devices: none -> 63.2 us  [the longest x12 54.6 us: near(): return lax.ppermute(array, ('dp', 'mp'), pairs)]
  transfers between devices with their start and end apart: 11 -> 41, of which waited for: 9 -> 7; matrix products, arithmetic and copies ran while one was open for 7% -> 4% of each run, Pallas kernels for 0% -> 39%
where the time goes in v2:
time: 402 us; the launch traced here: 397 us
  Pallas kernels  240 us (60%)
  waiting for transfers between devices  63.2 us (16%)
  starting transfers between devices  50.7 us (13%)
  local copies, waits for them, and re-layouts  33.3 us (8%)
  other arithmetic  7.7 us (2%)
    pallas_call x34, Pallas kernels, call(): pl.pallas_call(body, out_shape=list(outs), in_specs=ins + [ANY] * len(aft...  240 us
    ppermute x12, waiting for transfers between devices, near(): return lax.ppermute(array, ('dp', 'mp'), pairs)  54.6 us
    unnamed x107, local copies, waits for them, and re-layouts  28.1 us
    ppermute x18, starting transfers between devices, far(): lax.ppermute(array, 'dp', [(i, i ^ 4 * step) for i in range(self.dp)])  26.4 us
    ppermute x12, starting transfers between devices, near(): return lax.ppermute(array, ('dp', 'mp'), pairs)  14.2 us
    ppermute x6, starting transfers between devices, small_sum(): total = total + lax.ppermute(array, 'dp', [(i, i ^ m) for i in range(size)])  9.47 us
    ppermute x18, waiting for transfers between devices, far(): lax.ppermute(array, 'dp', [(i, i ^ 4 * step) for i in range(self.dp)])  8.55 us
  transfers between devices with their start and end apart: 41, of which 7 were waited for; matrix products, arithmetic and copies ran while one was open for 4% of the time, Pallas kernels for 39%

profile of v2, /device:TPU:0, one launch (start us, length us, event | category | flops | bytes accessed | tf_op | source)
XLA Modules:
  0.0 396.6 jit_solution(18028416319787341393)
XLA Ops:
  13.5 4.2 %collective-permute-start.5 = (f32[2,768]{1,0:T(2,128)S(1)}, f32[2,768]{1,0:T(2,128)S(1)}, u32[]{:S(2)}, u32[]{:S(2)}) collective-permute-start(f32[2,768]{1,0:T(2,128)S(1)} %add_add_fusion.1), channel_id=1, source_target_pairs={{0,24},{2,26},{4,28},{6,30},{8,16},{10,18},{12,20},{14,22},{16,8},... | collective-permute-start | bytes 18440 | tf_op jit(solution)/shard_map/ppermute | solution.py:855
  24.2 7.8 %shard_map.256 = (f32[6,128,1024]{2,1,0:T(8,128)}, f32[6,128,1024]{2,1,0:T(8,128)}) custom-call(s32[15]{0:T(128)} %refs_1_.13, bf16[8,32]{1,0:T(8,128)(2,1)} %scatter.4.refs_1_), custom_call_target="tpu_custom_call" | custom-call | bytes 6292028 | tf_op jit(solution)/shard_map/pallas_call | solution.py:68
  33.2 5.2 %shard_map.255.refs_5_.refs_3_.refs_2_ = bf16[2048,768]{1,0:T(8,128)(2,1)} custom-call(f32[2,768]{1,0:T(2,128)} %add_add_fusion.refs_0_.refs_1_, bf16[1024,768]{1,0:T(8,128)(2,1)} %bitcast.19, bf16[1024,768]{1,0:T(8,128)(2,1)} %bitcast.25), custom_call_target="tpu_custom_call" | custom-call | bytes 6297600 | tf_op jit(solution)/shard_map/pallas_call | solution.py:68
  42.8 8.5 %collective-permute-done.9.refs_1_ = bf16[4,48,1536]{2,1,0:T(8,128)(2,1)S(1)} collective-permute-done((bf16[4,48,1536]{2,1,0:T(8,128)(2,1)}, bf16[4,48,1536]{2,1,0:T(8,128)(2,1)S(1)}, u32[]{:S(2)}, u32[]{:S(2)}) %collective-permute-start.9) | collective-permute-done | bytes 589856 | tf_op jit(solution)/shard_map/ppermute | solution.py:105
  63.9 6.9 %collective-permute-done.10.refs_6_.refs_5_.refs_11_.refs_7_ = bf16[8,48,1536]{2,1,0:T(8,128)(2,1)S(1)} collective-permute-done((bf16[8,48,1536]{2,1,0:T(8,128)(2,1)}, bf16[8,48,1536]{2,1,0:T(8,128)(2,1)S(1)}, u32[]{:S(2)}, u32[]{:S(2)}) %collective-permute-start.10) | collective-permute-done | bytes 1179680 | tf_op jit(solution)/shard_map/ppermute | solution.py:105
  71.9 12.7 %shard_map.259 = (bf16[2048,256]{1,0:T(8,128)(2,1)}, bf16[2048,128]{1,0:T(8,128)(2,1)}, bf16[2048,128]{1,0:T(8,128)(2,1)}, bf16[2048,128]{1,0:T(8,128)(2,1)}) custom-call(s32[16]{0:T(128)} %fusion.1.refs_0_, s32[4]{0:T(128)} %refs_0_.7, s32[2]{0:T(128)} %refs_1_.12, bf16[2048,768]{1,0:T(8,128)(2,1)} %shard_map.255.refs_5_.refs_3_.refs_2_, ...), custom_call_target="tpu_custom_call" | custom-call | flops 10000000000 | bytes 11272280 | tf_op jit(solution)/shard_map/pallas_call | solution.py:68
  94.9 13.2 %shard_map.263 = (bf16[2048,256]{1,0:T(8,128)(2,1)}, bf16[2048,128]{1,0:T(8,128)(2,1)}, bf16[2048,128]{1,0:T(8,128)(2,1)}, bf16[2048,128]{1,0:T(8,128)(2,1)}) custom-call(s32[16]{0:T(128)} %fusion.1.refs_0_, s32[4]{0:T(128)} %refs_0_.7, s32[2]{0:T(128)} %refs_1_.12, bf16[2048,768]{1,0:T(8,128)(2,1)} %shard_map.255.refs_5_.refs_3_.refs_2_, ...), custom_call_target="tpu_custom_call" | custom-call | flops 10000000000 | bytes 11272280 | tf_op jit(solution)/shard_map/pallas_call | solution.py:68
  114.7 12.7 %shard_map.266 = (bf16[2048,256]{1,0:T(8,128)(2,1)}, bf16[2048,128]{1,0:T(8,128)(2,1)}, bf16[2048,128]{1,0:T(8,128)(2,1)}, bf16[2048,128]{1,0:T(8,128)(2,1)}) custom-call(s32[16]{0:T(128)} %fusion.1.refs_0_, s32[4]{0:T(128)} %refs_0_.7, s32[2]{0:T(128)} %refs_1_.12, bf16[2048,768]{1,0:T(8,128)(2,1)} %shard_map.255.refs_5_.refs_3_.refs_2_, ...), custom_call_target="tpu_custom_call" | custom-call | flops 10000000000 | bytes 11272280 | tf_op jit(solution)/shard_map/pallas_call | solution.py:68
  127.4 6.4 %shard_map.267.refs_2_.refs_6_ = bf16[2048,768]{1,0:T(8,128)(2,1)} custom-call(s32[16]{0:T(128)} %fusion.1.refs_0_, bf16[2048,128]{1,0:T(8,128)(2,1)} %get-tuple-element.96.refs_1_.refs_6_.refs_9_, bf16[2048,128]{1,0:T(8,128)(2,1)} %get-tuple-element.98.refs_2_.refs_6_.refs_10_, bf16[2048,128]{1,0:T(8,128)(2,1)} %get-tuple-element.100.refs_3_.refs_6_.refs_11_, ...), custom_call_target="tpu_custom_call" | custom-call | flops 1207959552 | bytes 7077952 | tf_op jit(solution)/shard_map/pallas_call | solution.py:68
  136.1 15.7 %collective-permute-done.20.refs_1_ = bf16[4,48,1536]{2,1,0:T(8,128)(2,1)S(1)} collective-permute-done((bf16[4,48,1536]{2,1,0:T(8,128)(2,1)S(1)}, bf16[4,48,1536]{2,1,0:T(8,128)(2,1)S(1)}, u32[]{:S(2)}, u32[]{:S(2)}) %collective-permute-start.20) | collective-permute-done | bytes 589856 | tf_op jit(solution)/shard_map/ppermute | solution.py:105
  158.1 25.3 %shard_map.269 = (bf16[2048,768]{1,0:T(8,128)(2,1)}, f32[2048,768]{1,0:T(8,128)}, f32[2048,768]{1,0:T(8,128)}, f32[8,48,1536]{2,1,0:T(8,128)}, bf16[8,48,1536]{2,1,0:T(8,128)(2,1)}) custom-call(s32[16]{0:T(128)} %fusion.1.refs_0_, f32[2,768]{1,0:T(2,128)} %add_add_fusion.refs_0_.refs_1_, bf16[1024,768]{1,0:T(8,128)(2,1)} %bitcast.31, ...), custom_call_target="tpu_custom_call" | custom-call | flops 14495514624 | bytes 34216000 | tf_op jit(solution)/shard_map/pallas_call | solution.py:68
  184.4 17.6 %shard_map.270 = (bf16[2048,768]{1,0:T(8,128)(2,1)}, bf16[2048,768]{1,0:T(8,128)(2,1)}, bf16[2048,768]{1,0:T(8,128)(2,1)}, bf16[2048,768]{1,0:T(8,128)(2,1)}) custom-call(s32[16]{0:T(128)} %fusion.1.refs_0_, bf16[2048,768]{1,0:T(8,128)(2,1)} %get-tuple-element.101.refs_1_, bf16[1024,768]{1,0:T(8,128)(2,1)} %bitcast.32, bf16[1024,768]{1,0:T(8,128)(2,1)} %bitcast.36, ...), custom_call_target="tpu_custom_call" | custom-call | flops 9663676416 | bytes 33816640 | tf_op jit(solution)/shard_map/pallas_call | solution.py:68
  203.9 14.5 %collective-permute-done.24.refs_1_ = bf16[8,48,1536]{2,1,0:T(8,128)(2,1)S(1)} collective-permute-done((bf16[8,48,1536]{2,1,0:T(8,128)(2,1)S(1)}, bf16[8,48,1536]{2,1,0:T(8,128)(2,1)S(1)}, u32[]{:S(2)}, u32[]{:S(2)}) %collective-permute-start.24) | collective-permute-done | bytes 1179680 | tf_op jit(solution)/shard_map/ppermute | solution.py:105
  222.7 10.7 %shard_map.272 = (f32[8,48,1536]{2,1,0:T(8,128)}, bf16[8,48,1536]{2,1,0:T(8,128)(2,1)}) custom-call(s32[16]{0:T(128)} %fusion.1.refs_0_, bf16[2048,768]{1,0:T(8,128)(2,1)} %get-tuple-element.101.refs_1_, bf16[1024,768]{1,0:T(8,128)(2,1)} %bitcast.33, bf16[1024,768]{1,0:T(8,128)(2,1)} %bitcast.37, bf16[2048,768]{1,0:T(8,128)(2,1)} %get-tuple-element.106.refs_4_, ...), custom_call_target="tpu_custom_call" | custom-call | flops 4831838208 | bytes 16121920 | tf_op jit(solution)/shard_map/pallas_call | solution.py:68
  237.7 14.5 %shard_map.273 = (f32[2048,768]{1,0:T(8,128)}, bf16[2048,768]{1,0:T(8,128)(2,1)}, bf16[2048,384]{1,0:T(8,128)(2,1)}, f32[8,768]{1,0:T(8,128)}) custom-call(s32[16]{0:T(128)} %fusion.1.refs_0_, f32[2,768]{1,0:T(2,128)} %add_add_fusion.refs_0_.refs_1_, bf16[1024,768]{1,0:T(8,128)(2,1)} %bitcast.34, bf16[1024,768]{1,0:T(8,128)(2,1)} %bitcast.38, ...), custom_call_target="tpu_custom_call" | custom-call | flops 1207959552 | bytes 32274496 | tf_op jit(solution)/shard_map/pallas_call | solution.py:68
  265.2 10.5 %shard_map.276 = (bf16[2048,384]{1,0:T(8,128)(2,1)}, f32[2,128,1024]{2,1,0:T(8,128)}) custom-call(s32[4]{0:T(128)} %refs_0_.7, s32[2]{0:T(128)} %refs_1_.12, bf16[2048,384]{1,0:T(8,128)(2,1)} %get-tuple-element.114.refs_2_, bf16[2048,256]{1,0:T(8,128)(2,1)} %get-tuple-element.97.refs_4_.refs_3_, bf16[2048,128]{1,0:T(8,128)(2,1)} %get-tuple-element.115.refs_4_, ...), custom_call_target="tpu_custom_call" | custom-call | flops 20000000000 | bytes 9961496 | tf_op jit(solution)/shard_map/pallas_call | solution.py:68
  282.1 11.0 %shard_map.279 = (bf16[2048,384]{1,0:T(8,128)(2,1)}, f32[2,128,1024]{2,1,0:T(8,128)}) custom-call(s32[4]{0:T(128)} %refs_0_.7, s32[2]{0:T(128)} %refs_1_.12, bf16[2048,384]{1,0:T(8,128)(2,1)} %get-tuple-element.114.refs_2_, bf16[2048,256]{1,0:T(8,128)(2,1)} %get-tuple-element.99.refs_2_.refs_3_, bf16[2048,128]{1,0:T(8,128)(2,1)} %get-tuple-element.123.refs_4_, ...), custom_call_target="tpu_custom_call" | custom-call | flops 20000000000 | bytes 9961496 | tf_op jit(solution)/shard_map/pallas_call | solution.py:68
  293.1 10.5 %shard_map.280 = (bf16[2048,384]{1,0:T(8,128)(2,1)}, f32[2,128,1024]{2,1,0:T(8,128)}) custom-call(s32[4]{0:T(128)} %refs_0_.7, s32[2]{0:T(128)} %refs_1_.12, bf16[2048,384]{1,0:T(8,128)(2,1)} %get-tuple-element.114.refs_2_, bf16[2048,256]{1,0:T(8,128)(2,1)} %get-tuple-element.132.refs_3_, bf16[2048,128]{1,0:T(8,128)(2,1)} %get-tuple-element.133.refs_4_, ...), custom_call_target="tpu_custom_call" | custom-call | flops 20000000000 | bytes 9961496 | tf_op jit(solution)/shard_map/pallas_call | solution.py:68
  303.7 10.0 %shard_map.281 = (bf16[2048,768]{1,0:T(8,128)(2,1)}, f32[8,768]{1,0:T(8,128)}) custom-call(s32[16]{0:T(128)} %fusion.1.refs_0_, bf16[1024,768]{1,0:T(8,128)(2,1)} %bitcast.22, bf16[1024,768]{1,0:T(8,128)(2,1)} %bitcast.28, bf16[2048,384]{1,0:T(8,128)(2,1)} %get-tuple-element.122.refs_2_.refs_3_.refs_6_, ...), custom_call_target="tpu_custom_call" | custom-call | flops 3623878656 | bytes 13393984 | tf_op jit(solution)/shard_map/pallas_call | solution.py:68
  314.3 15.4 %shard_map.282 = (f32[8,48,1664]{2,1,0:T(8,128)}, bf16[8,48,1664]{2,1,0:T(8,128)(2,1)}, f32[8,128]{1,0:T(8,128)}) custom-call(s32[16]{0:T(128)} %fusion.1.refs_0_, s32[15]{0:T(128)} %refs_1_.13, bf16[2048,768]{1,0:T(8,128)(2,1)} %shard_map.255.refs_5_.refs_3_.refs_2_, bf16[2048,768]{1,0:T(8,128)(2,1)} %get-tuple-element.112.refs_3_, ...), custom_call_target="tpu_custom_call" | custom-call | flops 5234491392 | bytes 19615868 | tf_op jit(solution)/shard_map/pallas_call | solution.py:68
  330.2 8.8 %shard_map.283 = (bf16[1024,768]{1,0:T(8,128)(2,1)}, bf16[1024,768]{1,0:T(8,128)(2,1)}) custom-call(f32[2,768]{1,0:T(2,128)} %add_add_fusion.refs_0_.refs_1_, bf16[1024,768]{1,0:T(8,128)(2,1)} %bitcast.23, bf16[1024,768]{1,0:T(8,128)(2,1)} %bitcast.29, f32[2048,768]{1,0:T(8,128)} %get-tuple-element.142.refs_3_, ...), custom_call_target="tpu_custom_call" | custom-call | bytes 18880512 | tf_op jit(solution)/shard_map/pallas_call | solution.py:68
  339.0 8.3 %collective-permute-done.31.refs_1_ = bf16[8,48,1664]{2,1,0:T(8,128)(2,1)S(1)} collective-permute-done((bf16[8,48,1664]{2,1,0:T(8,128)(2,1)}, bf16[8,48,1664]{2,1,0:T(8,128)(2,1)S(1)}, u32[]{:S(2)}, u32[]{:S(2)}) %collective-permute-start.31) | collective-permute-done | bytes 1277984 | tf_op jit(solution)/shard_map/ppermute | solution.py:105
  358.7 9.0 %shard_map.285 = (bf16[1024,768]{1,0:T(8,128)(2,1)}, bf16[1024,768]{1,0:T(8,128)(2,1)}) custom-call(bf16[1024,768]{1,0:T(8,128)(2,1)} %bitcast.24, bf16[1024,768]{1,0:T(8,128)(2,1)} %bitcast.30, bf16[2048,768]{1,0:T(8,128)(2,1)} %shard_map.267.refs_2_.refs_6_, bf16[2048,768]{1,0:T(8,128)(2,1)} %copy-done, bf16[2048,768]{1,0:T(8,128)(2,1)} %get-tuple-element.104.refs_4_, ...), custom_call_target="tpu_custom_call" | custom-call | bytes 18874368 | tf_op jit(solution)/shard_map/pallas_call | solution.py:68
  381.3 8.5 %collective-permute-done.35.refs_2_ = bf16[48,1664]{1,0:T(8,128)(2,1)S(1)} collective-permute-done((bf16[48,1664]{1,0:T(8,128)(2,1)S(1)}, bf16[48,1664]{1,0:T(8,128)(2,1)S(1)}, u32[]{:S(2)}, u32[]{:S(2)}) %collective-permute-start.35) | collective-permute-done | bytes 159776 | tf_op jit(solution)/shard_map/ppermute | solution.py:97
  (217 shorter events, 127.2 us)
Async XLA Ops:
  13.5 18.4 %collective-permute-start.5 = (f32[2,768]{1,0:T(2,128)S(1)}, f32[2,768]{1,0:T(2,128)S(1)}, u32[]{:S(2)}, u32[]{:S(2)}) collective-permute-start(f32[2,768]{1,0:T(2,128)S(1)} %add_add_fusion.1), channel_id=1, source_target_pairs={{0,24},{2,26},{4,28},{6,30},{8,16},{10,18},{12,20},{14,22},{16,8},... | collective-permute-start | bytes 18440 | tf_op jit(solution)/shard_map/ppermute | solution.py:855
  19.1 19.3 %collective-permute-start.8 = (bf16[1,48,1536]{2,1,0:T(8,128)(2,1)S(1)}, bf16[1,48,1536]{2,1,0:T(8,128)(2,1)S(1)}, u32[]{:S(2)}, u32[]{:S(2)}) collective-permute-start(bf16[1,48,1536]{2,1,0:T(8,128)(2,1)S(1)} %bitcast.41), channel_id=1, source_target_pairs={{0,24},{2,26},{4,28},{6,30},{8,16},{10,18},{12,20},{14,22},{16,8},... | collective-permute-start | bytes 442376 | tf_op jit(solution)/shard_map/ppermute | solution.py:97
  54.4 16.4 %collective-permute-start.10 = (bf16[8,48,1536]{2,1,0:T(8,128)(2,1)}, bf16[8,48,1536]{2,1,0:T(8,128)(2,1)S(1)}, u32[]{:S(2)}, u32[]{:S(2)}) collective-permute-start(bf16[8,48,1536]{2,1,0:T(8,128)(2,1)} %shard_map.258.refs_5_.refs_4_.refs_10_.refs_6_), channel_id=1, source_target_pairs={{0,4},{1,3},{2,6},{3,1},{4,0},{5,7},{6,2},{7,5},{8,12},{9,11},{10,... | collective-permute-start | bytes 3538952 | tf_op jit(solution)/shard_map/ppermute | solution.py:105
  59.5 25.0 %collective-permute-start.13 = (bf16[1,48,1536]{2,1,0:T(8,128)(2,1)}, bf16[1,48,1536]{2,1,0:T(8,128)(2,1)S(1)}, u32[]{:S(2)}, u32[]{:S(2)}) collective-permute-start(bf16[1,48,1536]{2,1,0:T(8,128)(2,1)} %shard_map.260.refs_0_), channel_id=1, source_target_pairs={{0,24},{2,26},{4,28},{6,30},{8,16},{10,18},{12,20},{14,22},{16,8},... | collective-permute-start | bytes 442376 | tf_op jit(solution)/shard_map/ppermute | solution.py:97
  63.1 21.5 %collective-permute-start.12 = (bf16[1,48,1536]{2,1,0:T(8,128)(2,1)}, bf16[1,48,1536]{2,1,0:T(8,128)(2,1)S(1)}, u32[]{:S(2)}, u32[]{:S(2)}) collective-permute-start(bf16[1,48,1536]{2,1,0:T(8,128)(2,1)} %shard_map.260.refs_0_), channel_id=1, source_target_pairs={{0,16},{2,18},{4,20},{6,22},{8,24},{10,26},{12,28},{14,30},{16,0},... | collective-permute-start | bytes 442376 | tf_op jit(solution)/shard_map/ppermute | solution.py:97
  63.1 21.5 %collective-permute-start.11 = (bf16[1,48,1536]{2,1,0:T(8,128)(2,1)}, bf16[1,48,1536]{2,1,0:T(8,128)(2,1)S(1)}, u32[]{:S(2)}, u32[]{:S(2)}) collective-permute-start(bf16[1,48,1536]{2,1,0:T(8,128)(2,1)} %shard_map.260.refs_0_), channel_id=1, source_target_pairs={{0,8},{2,10},{4,12},{6,14},{8,0},{10,2},{12,4},{14,6},{16,24},{18,... | collective-permute-start | bytes 442376 | tf_op jit(solution)/shard_map/ppermute | solution.py:97
  88.9 22.4 %collective-permute-start.17 = (bf16[1,48,1536]{2,1,0:T(8,128)(2,1)}, bf16[1,48,1536]{2,1,0:T(8,128)(2,1)S(1)}, u32[]{:S(2)}, u32[]{:S(2)}) collective-permute-start(bf16[1,48,1536]{2,1,0:T(8,128)(2,1)} %shard_map.262.refs_8_.refs_0_), channel_id=1, source_target_pairs={{0,24},{2,26},{4,28},{6,30},{8,16},{10,18},{12,20},{14,22},{16,8},... | collective-permute-start | bytes 442376 | tf_op jit(solution)/shard_map/ppermute | solution.py:97
  92.6 18.7 %collective-permute-start.16 = (bf16[1,48,1536]{2,1,0:T(8,128)(2,1)}, bf16[1,48,1536]{2,1,0:T(8,128)(2,1)S(1)}, u32[]{:S(2)}, u32[]{:S(2)}) collective-permute-start(bf16[1,48,1536]{2,1,0:T(8,128)(2,1)} %shard_map.262.refs_8_.refs_0_), channel_id=1, source_target_pairs={{0,16},{2,18},{4,20},{6,22},{8,24},{10,26},{12,28},{14,30},{16,0},... | collective-permute-start | bytes 442376 | tf_op jit(solution)/shard_map/ppermute | solution.py:97
  92.6 18.7 %collective-permute-start.15 = (bf16[1,48,1536]{2,1,0:T(8,128)(2,1)}, bf16[1,48,1536]{2,1,0:T(8,128)(2,1)S(1)}, u32[]{:S(2)}, u32[]{:S(2)}) collective-permute-start(bf16[1,48,1536]{2,1,0:T(8,128)(2,1)} %shard_map.262.refs_8_.refs_0_), channel_id=1, source_target_pairs={{0,8},{2,10},{4,12},{6,14},{8,0},{10,2},{12,4},{14,6},{16,24},{18,... | collective-permute-start | bytes 442376 | tf_op jit(solution)/shard_map/ppermute | solution.py:97
  133.8 22.3 %collective-permute-start.18 = (bf16[2048,768]{1,0:T(8,128)(2,1)}, bf16[2048,768]{1,0:T(8,128)(2,1)S(1)}, u32[]{:S(2)}, u32[]{:S(2)}) collective-permute-start(bf16[2048,768]{1,0:T(8,128)(2,1)} %shard_map.267.refs_2_.refs_6_), channel_id=1, source_target_pairs={{0,1},{1,0},{2,3},{3,2},{4,5},{5,4},{6,7},{7,6},{8,9},{9,8},{10,11... | collective-permute-start | bytes 9437192 | tf_op jit(solution)/shard_map/ppermute | solution.py:109
  133.9 22.2 %collective-permute-start.19 = (bf16[8,48,1536]{2,1,0:T(8,128)(2,1)S(1)}, bf16[8,48,1536]{2,1,0:T(8,128)(2,1)S(1)}, u32[]{:S(2)}, u32[]{:S(2)}) collective-permute-start(bf16[8,48,1536]{2,1,0:T(8,128)(2,1)S(1)} %copy-done.2), channel_id=1, source_target_pairs={{0,4},{1,3},{2,6},{3,1},{4,0},{5,7},{6,2},{7,5},{8,12},{9,11},{10,... | collective-permute-start | bytes 3538952 | tf_op jit(solution)/shard_map/ppermute | solution.py:105
  154.9 28.5 %collective-permute-start.21 = (bf16[8,48,1536]{2,1,0:T(8,128)(2,1)}, bf16[8,48,1536]{2,1,0:T(8,128)(2,1)S(1)}, u32[]{:S(2)}, u32[]{:S(2)}) collective-permute-start(bf16[8,48,1536]{2,1,0:T(8,128)(2,1)} %shard_map.268.refs_10_.refs_6_), channel_id=1, source_target_pairs={{0,4},{1,3},{2,6},{3,1},{4,0},{5,7},{6,2},{7,5},{8,12},{9,11},{10,... | collective-permute-start | bytes 3538952 | tf_op jit(solution)/shard_map/ppermute | solution.py:105
  202.0 33.9 %collective-permute-start.23 = (bf16[2048,768]{1,0:T(8,128)(2,1)}, bf16[2048,768]{1,0:T(8,128)(2,1)S(1)}, u32[]{:S(2)}, u32[]{:S(2)}) collective-permute-start(bf16[2048,768]{1,0:T(8,128)(2,1)} %get-tuple-element.105.refs_2_.refs_8_), channel_id=1, source_target_pairs={{0,1},{1,0},{2,3},{3,2},{4,5},{5,4},{6,7},{7,6},{8,9},{9,8},{10,11... | collective-permute-start | bytes 9437192 | tf_op jit(solution)/shard_map/ppermute | solution.py:109
  202.1 16.3 %collective-permute-start.24 = (bf16[8,48,1536]{2,1,0:T(8,128)(2,1)S(1)}, bf16[8,48,1536]{2,1,0:T(8,128)(2,1)S(1)}, u32[]{:S(2)}, u32[]{:S(2)}) collective-permute-start(bf16[8,48,1536]{2,1,0:T(8,128)(2,1)S(1)} %copy-done.40), channel_id=1, source_target_pairs={{0,4},{1,3},{2,6},{3,1},{4,0},{5,7},{6,2},{7,5},{8,12},{9,11},{10,... | collective-permute-start | bytes 3538952 | tf_op jit(solution)/shard_map/ppermute | solution.py:105
  233.4 26.2 %collective-permute-start.25 = (bf16[8,48,1536]{2,1,0:T(8,128)(2,1)}, bf16[8,48,1536]{2,1,0:T(8,128)(2,1)S(1)}, u32[]{:S(2)}, u32[]{:S(2)}) collective-permute-start(bf16[8,48,1536]{2,1,0:T(8,128)(2,1)} %get-tuple-element.118), channel_id=1, source_target_pairs={{0,4},{1,3},{2,6},{3,1},{4,0},{5,7},{6,2},{7,5},{8,12},{9,11},{10,... | collective-permute-start | bytes 3538952 | tf_op jit(solution)/shard_map/ppermute | solution.py:105
  235.1 17.0 %collective-permute-start.26 = (bf16[4,48,1536]{2,1,0:T(8,128)(2,1)S(1)}, bf16[4,48,1536]{2,1,0:T(8,128)(2,1)S(1)}, u32[]{:S(2)}, u32[]{:S(2)}) collective-permute-start(bf16[4,48,1536]{2,1,0:T(8,128)(2,1)S(1)} %copy-done.42), channel_id=1, source_target_pairs={{0,2},{1,5},{2,0},{3,7},{4,6},{5,1},{6,4},{7,3},{8,10},{9,13},{10,... | collective-permute-start | bytes 1769480 | tf_op jit(solution)/shard_map/ppermute | solution.py:105
  255.3 20.5 %collective-permute-start.28 = (bf16[48,1536]{1,0:T(8,128)(2,1)}, bf16[48,1536]{1,0:T(8,128)(2,1)S(1)}, u32[]{:S(2)}, u32[]{:S(2)}) collective-permute-start(bf16[48,1536]{1,0:T(8,128)(2,1)} %get-tuple-element.127), channel_id=1, source_target_pairs={{0,8},{2,10},{4,12},{6,14},{8,0},{10,2},{12,4},{14,6},{16,24},{18,... | collective-permute-start | bytes 442376 | tf_op jit(solution)/shard_map/ppermute | solution.py:97
  256.5 19.2 %collective-permute-start.29 = (bf16[48,1536]{1,0:T(8,128)(2,1)}, bf16[48,1536]{1,0:T(8,128)(2,1)S(1)}, u32[]{:S(2)}, u32[]{:S(2)}) collective-permute-start(bf16[48,1536]{1,0:T(8,128)(2,1)} %get-tuple-element.128), channel_id=1, source_target_pairs={{0,16},{2,18},{4,20},{6,22},{8,24},{10,26},{12,28},{14,30},{16,0},... | collective-permute-start | bytes 442376 | tf_op jit(solution)/shard_map/ppermute | solution.py:97
  259.4 16.3 %collective-permute-start.30 = (bf16[48,1536]{1,0:T(8,128)(2,1)}, bf16[48,1536]{1,0:T(8,128)(2,1)S(1)}, u32[]{:S(2)}, u32[]{:S(2)}) collective-permute-start(bf16[48,1536]{1,0:T(8,128)(2,1)} %get-tuple-element.129), channel_id=1, source_target_pairs={{0,24},{2,26},{4,28},{6,30},{8,16},{10,18},{12,20},{14,22},{16,8},... | collective-permute-start | bytes 442376 | tf_op jit(solution)/shard_map/ppermute | solution.py:97
  313.7 16.4 %collective-permute-start.32 = (bf16[2048,768]{1,0:T(8,128)(2,1)}, bf16[2048,768]{1,0:T(8,128)(2,1)}, u32[]{:S(2)}, u32[]{:S(2)}) collective-permute-start(bf16[2048,768]{1,0:T(8,128)(2,1)} %get-tuple-element.143.refs_4_), channel_id=1, source_target_pairs={{0,1},{1,0},{2,3},{3,2},{4,5},{5,4},{6,7},{7,6},{8,9},{9,8},{10,11... | collective-permute-start | bytes 9437192 | tf_op jit(solution)/shard_map/ppermute | solution.py:109
  313.8 43.2 %collective-permute-start.22 = (bf16[2048,768]{1,0:T(8,128)(2,1)S(1)}, bf16[2048,768]{1,0:T(8,128)(2,1)S(1)}, u32[]{:S(2)}, u32[]{:S(2)}) collective-permute-start(bf16[2048,768]{1,0:T(8,128)(2,1)S(1)} %copy-done.3), channel_id=1, source_target_pairs={{0,1},{1,0},{2,3},{3,2},{4,5},{5,4},{6,7},{7,6},{8,9},{9,8},{10,11... | collective-permute-start | bytes 9437192 | tf_op jit(solution)/shard_map/ppermute | solution.py:109
  329.7 17.5 %collective-permute-start.31 = (bf16[8,48,1664]{2,1,0:T(8,128)(2,1)}, bf16[8,48,1664]{2,1,0:T(8,128)(2,1)S(1)}, u32[]{:S(2)}, u32[]{:S(2)}) collective-permute-start(bf16[8,48,1664]{2,1,0:T(8,128)(2,1)} %get-tuple-element.141), channel_id=1, source_target_pairs={{0,4},{1,3},{2,6},{3,1},{4,0},{5,7},{6,2},{7,5},{8,12},{9,11},{10,... | collective-permute-start | bytes 3833864 | tf_op jit(solution)/shard_map/ppermute | solution.py:105
  352.6 18.4 %collective-permute-start.37 = (bf16[48,1536]{1,0:T(8,128)(2,1)S(1)}, bf16[48,1536]{1,0:T(8,128)(2,1)S(1)}, u32[]{:S(2)}, u32[]{:S(2)}) collective-permute-start(bf16[48,1536]{1,0:T(8,128)(2,1)S(1)} %copy-done.48), channel_id=1, source_target_pairs={{0,8},{2,10},{4,12},{6,14},{8,0},{10,2},{12,4},{14,6},{16,24},{18,... | collective-permute-start | bytes 442376 | tf_op jit(solution)/shard_map/ppermute | solution.py:97
  352.9 18.1 %collective-permute-start.38 = (bf16[48,1536]{1,0:T(8,128)(2,1)S(1)}, bf16[48,1536]{1,0:T(8,128)(2,1)S(1)}, u32[]{:S(2)}, u32[]{:S(2)}) collective-permute-start(bf16[48,1536]{1,0:T(8,128)(2,1)S(1)} %copy-done.47), channel_id=1, source_target_pairs={{0,16},{2,18},{4,20},{6,22},{8,24},{10,26},{12,28},{14,30},{16,0},... | collective-permute-start | bytes 442376 | tf_op jit(solution)/shard_map/ppermute | solution.py:97
  (66 other events, 387.2 us)

commit v3 on v2

v3 whole, which is shorter than its diff:
```python
import functools

import jax
import jax.numpy as jnp
from jax import lax
from jax.experimental import pallas as pl
from jax.experimental.pallas import tpu as pltpu
from jax.sharding import PartitionSpec as P

DH = 64
LANES = 128
EPS = 1e-06
NEG = -1000000000.0
VMEM_LIMIT = 56 * 1024 * 1024
BF = jnp.bfloat16
F32 = jnp.float32
ANY = pl.BlockSpec(memory_space=pl.ANY)
SMEM = pl.BlockSpec(memory_space=pltpu.SMEM)
VMEM = pl.BlockSpec(memory_space=pltpu.VMEM)


def dot(left, right):
    return jnp.dot(left, right, preferred_element_type=F32)


def dot_rows(left, right):
    return lax.dot_general(left, right, (((0,), (0,)), ((), ())), preferred_element_type=F32)


def dot_cols(left, right):
    return lax.dot_general(left, right, (((1,), (1,)), ((), ())), preferred_element_type=F32)


def tiles(array, rows):
    return pl.BlockSpec((rows,) + array.shape[1:], lambda i: (i,) + (0,) * (array.ndim - 1))


def fixed(array):
    return pl.BlockSpec(array.shape, lambda i: (0,) * array.ndim)


def pair_tiles(pair, rows):
    count = pair[0].shape[0] // rows
    rest = (0,) * (pair[0].ndim - 1)
    shape = (rows,) + pair[0].shape[1:]
    return [
        pl.BlockSpec(shape, lambda i: (jnp.minimum(i, count - 1),) + rest),
        pl.BlockSpec(shape, lambda i: (jnp.maximum(i - count, 0),) + rest),
    ]


def pick(count, first, second):
    return jnp.where(pl.program_id(0) < count, first[...], second[...])


def out_of(shape, kind):
    return jax.ShapeDtypeStruct(tuple(shape), kind)


def call(kernel, outs, args, *, ins=None, out_specs=None, grid=None, scratch=(), us=2, after=(), through=()):
    ins = list(ins or [VMEM] * len(args))
    out_specs = list(out_specs or [VMEM] * len(outs))
    extra = {} if grid is None else {"grid": grid}
    idle = len(after) + len(through)

    def body(*refs):
        given, made = refs[: len(args)], refs[len(args) + idle :]
        kernel(*given, *made[: len(outs)], *made[len(outs) + len(through) :])

    return pl.pallas_call(
        body,
        out_shape=list(outs) + [out_of(t.shape, t.dtype) for t in through],
        in_specs=ins + [ANY] * idle,
        out_specs=out_specs + [ANY] * len(through),
        scratch_shapes=list(scratch),
        compiler_params=pltpu.CompilerParams(vmem_limit_bytes=VMEM_LIMIT),
        input_output_aliases={len(args) + len(after) + i: len(outs) + i for i in range(len(through))},
        cost_estimate=pl.CostEstimate(flops=int(us * 1e9), bytes_accessed=1000, transcendentals=0),
        **extra,
    )(*args, *after, *through)


class Ring:
    def __init__(self, sizes):
        self.dp, self.mp = sizes
        self.me = lax.axis_index("dp")
        self.odd = lax.axis_index("mp") & 1
        self.quarter = self.dp // 4
        j = jnp.arange(self.dp, dtype=jnp.int32)
        first = (j // self.quarter) & 1
        last = j // (2 * self.quarter)
        low = jnp.where(self.odd == 0, first + 2 * last, 2 * first + last)
        self.order = self.me ^ (4 * (j % self.quarter) + low)
        rel = self.me ^ j
        bit0, bit1 = rel & 1, (rel >> 1) & 1
        first, last = jnp.where(self.odd == 0, bit0, bit1), jnp.where(self.odd == 0, bit1, bit0)
        self.spots = (rel >> 2) + self.quarter * (first + 2 * last)
        lead = (lax.axis_index("mp") == 0).astype(jnp.int32)
        self.places = jnp.concatenate([self.order, lead[None]])

    def far(self, array):
        return [
            lax.ppermute(array, "dp", [(i, i ^ (4 * step)) for i in range(self.dp)])
            for step in range(1, self.quarter)
        ]

    def far_all(self, arrays):
        return [
            lax.ppermute(a, "dp", [(i, i ^ (4 * (step + 1))) for i in range(self.dp)])
            for step, a in enumerate(arrays)
        ]

    def near(self, array, masks):
        pairs = [
            (i * self.mp + c, (i ^ masks[c & 1]) * self.mp + c)
            for i in range(self.dp)
            for c in range(self.mp)
        ]
        return lax.ppermute(array, ("dp", "mp"), pairs)

    def first(self, array):
        return self.near(array, (1, 2))

    def last(self, array):
        return self.near(array, (2, 1))

    def exchange(self, array):
        return [
            lax.ppermute(array, "mp", [(i, i ^ k) for i in range(self.mp)])
            for k in range(1, self.mp)
        ]


def join_kernel(plan, *refs):
    sources, outs = refs[: -len(plan)], refs[-len(plan) :]
    for (chosen, start, stop), out in zip(plan, outs):
        at = 0
        for i in chosen:
            count = sources[i].shape[0]
            out[at : at + count] = sources[i][:, :, start:stop]
            at += count


def join(arrays, plan, after=(), through=()):
    outs = []
    for chosen, start, stop in plan:
        count = sum(arrays[i].shape[0] for i in chosen)
        outs.append(out_of((count, arrays[0].shape[1], stop - start), arrays[0].dtype))
    return call(functools.partial(join_kernel, plan), outs, arrays, after=after, through=through)


def aligned(rows):
    return rows % 16 == 0


def blocks_of(ring, held, got):
    if aligned(held.shape[1]):
        return (held, got)
    blocks = jnp.take(jnp.concatenate([held, got], 0), ring.spots, axis=0)
    return (blocks.reshape((-1,) + held.shape[2:]),)


def load_start(places, sources, to, sem, cols):
    copies = []
    if len(sources) == 2:
        half, rows, _ = sources[0].shape
        for j in range(2 * half):
            at = pl.multiple_of(places[j] * rows, 16)
            block = sources[j // half].at[j % half, :, cols]
            copies.append(pltpu.make_async_copy(block, to.at[pl.ds(at, rows)], sem.at[j]))
    else:
        copies.append(pltpu.make_async_copy(sources[0].at[:, cols], to, sem.at[0]))
    for c in copies:
        c.start()
    return copies


def load(places, sources, to, sem, cols):
    for c in load_start(places, sources, to, sem, cols):
        c.wait()


def load_all(places, refs, to, sem, plan):
    step = len(refs) // len(plan)
    copies = []
    to_at = 0
    for i, (at, count) in enumerate(plan):
        there = to.at[:, pl.ds(to_at, count)]
        copies += load_start(places, refs[i * step : (i + 1) * step], there, sem.at[i], pl.ds(at, count))
        to_at += count
    for c in copies:
        c.wait()


def emit(places, total, keep, send, extra=None):
    half, rows, _ = keep.shape
    for j in range(2 * half):
        at = pl.multiple_of(places[j] * rows, 16)
        block = total[pl.ds(at, rows), :]
        if extra is not None:
            block = block + extra
        if j < half:
            keep[j] = block
        else:
            send[j - half] = block.astype(BF)


def emitted(ring, rows, cols):
    share = rows // ring.dp
    if aligned(share):
        shape = (ring.dp // 2, share, cols)
        return [out_of(shape, F32), out_of(shape, BF)]
    return [out_of((rows, cols), F32)]


def halves(ring, outs, extra=None):
    if len(outs) == 2:
        return outs
    blocks = outs[0].reshape(ring.dp, -1, outs[0].shape[1])
    if extra is not None:
        blocks = blocks + extra
    blocks = jnp.take(blocks, ring.order, axis=0)
    return blocks[: ring.dp // 2], blocks[ring.dp // 2 :].astype(BF)


def fold_kernel(modes, *refs):
    ins, outs = refs[: 2 * len(modes)], refs[2 * len(modes) :]
    for mode in modes:
        keep, got = ins[:2]
        ins = ins[2:]
        count = got.shape[0] if mode else got.shape[0] // 2
        if mode:
            outs[0][...] = keep[0] + got[0].astype(F32)
            for j in range(1, count):
                outs[j][...] = (keep[j] + got[j].astype(F32)).astype(BF)
            outs = outs[count:]
        else:
            outs[0][...] = keep[:count] + got[:count].astype(F32)
            outs[1][...] = (keep[count:] + got[count:].astype(F32)).astype(BF)
            outs = outs[2:]


def fold(*items, after=(), through=()):
    outs = []
    args = []
    for keep, got, mode in items:
        args += [keep, got]
        if mode:
            shape = keep.shape[1:]
            outs += [out_of(shape, F32)] + [out_of(shape, BF)] * (keep.shape[0] - 1)
        else:
            shape = (keep.shape[0] // 2,) + keep.shape[1:]
            outs += [out_of(shape, F32), out_of(shape, BF)]
    kernel = functools.partial(fold_kernel, [m for *_, m in items])
    return call(kernel, outs, args, after=after, through=through)


def final_kernel(counts, plan, scaled, gain_ref, *refs):
    weights, refs = refs[: len(scaled)], refs[len(scaled) :]
    fields = []
    for count in counts:
        total = refs[0][...]
        for r in refs[1:count]:
            total = total + r[...].astype(F32)
        fields.append(total)
        refs = refs[count:]
    outs, gain_out = refs[:-1], refs[-1]
    sums = jnp.zeros(gain_out.shape, F32)
    for i, (out, spans) in enumerate(zip(outs, plan)):
        at = 0
        for f, start, stop in spans:
            value = fields[f][:, start:stop]
            there = slice(at, at + stop - start)
            if i in scaled:
                kept = weights[scaled.index(i)][:, there].astype(F32)
                sums += jnp.sum(value * kept, 1, keepdims=True)
                value = value * gain_ref[...]
            out[:, there] = value
            at += stop - start
    gain_out[...] = sums


def final(items, plan, scaled, gain, weights, after=()):
    rows = gain.shape[0]
    outs = [out_of((rows, sum(b - a for _, a, b in spans)), F32) for spans in plan]
    outs.append(out_of((rows, LANES), F32))
    kernel = functools.partial(final_kernel, [len(i) for i in items], plan, scaled)
    return call(kernel, outs, [gain, *weights, *[a for i in items for a in i]], after=after)


def distance_buckets(bounds_ref, dist, buckets):
    size = jnp.abs(dist)
    half = jnp.zeros(dist.shape, jnp.int32)
    for b in range(bounds_ref.shape[0]):
        half += (size >= bounds_ref[b]).astype(jnp.int32)
    return half + jnp.where(dist > 0, buckets // 2, 0)


def bases_kernel(bounds_ref, table_ref, near_ref, far_ref):
    heads, _, width = near_ref.shape
    buckets = table_ref.shape[1]
    for ref, sign in ((near_ref, 1), (far_ref, -1)):
        dist = sign * (lax.broadcasted_iota(jnp.int32, (8, width), 1) - width // 2)
        marks = distance_buckets(bounds_ref, dist, buckets)
        marks = jnp.concatenate([marks] * (buckets // 8), 0)
        onehot = (marks == lax.broadcasted_iota(jnp.int32, (buckets, width), 0)).astype(F32)
        line = dot(table_ref[...], onehot.astype(BF))
        row = lax.broadcasted_iota(jnp.int32, (8, width), 0)
        for h in range(heads):
            field = jnp.broadcast_to(line[h : h + 1], (8, width))
            for k in (1, 2, 4):
                field = jnp.where((row & k) != 0, pltpu.roll(field, k, 1), field)
            while field.shape[0] < LANES:
                field = jnp.concatenate([field, pltpu.roll(field, field.shape[0], 1)], 0)
            ref[h] = field


def bias_bases(boundaries, table, heads, width):
    rows = jnp.zeros((8, table.shape[0]), table.dtype).at[: table.shape[1]].set(table.T)
    shape = out_of((heads, LANES, width), F32)
    return call(bases_kernel, [shape, shape], [boundaries, rows], ins=[SMEM, VMEM])


def bucket_field(bounds_ref, fields, buckets, first):
    width = fields[0].shape[-1]
    dist = width // 2 - lax.broadcasted_iota(jnp.int32, (8, width), 1)
    marks = distance_buckets(bounds_ref, dist, buckets)
    row = lax.broadcasted_iota(jnp.int32, (8, width), 0)
    line = jnp.zeros((8, width), F32)
    for h, field in enumerate(fields):
        while field.shape[0] > 8:
            half = field.shape[0] // 2
            field = field[:half] + pltpu.roll(field[half:], width - half, 1)
        for k in (4, 2, 1):
            field = jnp.where((row & k) != 0, pltpu.roll(field, width - k, 1), field)
        line = jnp.where(row == h, jnp.sum(field, 0, keepdims=True), line)
    lane = lax.broadcasted_iota(jnp.int32, (8, LANES), 1)
    out = jnp.zeros((8, LANES), F32)
    for b in range(buckets):
        total = jnp.sum(jnp.where(marks == b, line, 0.0), 1, keepdims=True)
        out = jnp.where(lane == first + b, total, out)
    return out


def split_low(values, lane, off, rest):
    high = values.astype(BF).astype(F32)
    mid = (values - high).astype(BF).astype(F32)
    low = values - high - mid
    return jnp.where(
        lane == off,
        high,
        jnp.where(lane == off + 1, mid, jnp.where(lane == off + 2, low, rest)),
    )


def three_ones(lane, off):
    return jnp.where((lane >= off) & (lane < off + 3), 1.0, 0.0)


def slots_of(batches):
    at = 0
    for b, (slots, length) in enumerate(batches):
        for s in range(slots):
            yield b, s, length, slice(at, at + length)
            at += length


def attend_kernel(batches, at, halves, *refs):
    places, lens = refs[0], refs[1 : 1 + len(batches)]
    refs = refs[1 + len(batches) :]
    normed_ref, near_ref = refs[:2]
    sources = refs[2 : 2 + halves]
    aug_ref, k_ref, v_ref, o_ref, w_scr, sem = refs[2 + halves :]
    width = near_ref.shape[-1]
    load(places, sources, w_scr, sem, pl.ds(at, 3 * LANES))
    for b, s, length, span in slots_of(batches):
        valid = lens[b][s]
        lane = lax.broadcasted_iota(jnp.int32, (length, LANES), 1)
        place = lax.broadcasted_iota(jnp.int32, (length, LANES), 0)
        masked = jnp.where(place >= valid, NEG, 0.0)
        qkv = dot(normed_ref[span, :], w_scr[...])
        q, k, v = (qkv[:, i * LANES : (i + 1) * LANES] for i in range(3))
        k_ref[span, :] = k.astype(BF)
        v_ref[span, :] = v.astype(BF)
        mixed = []
        for e in range(2):
            own = (lane >= DH) == (e == 1)
            off = DH * (1 - e)
            marker = jnp.where(lane == off + 3, 1.0, 0.0)
            q_own = jnp.where(own, q, marker).astype(BF)
            k_own = jnp.where(own, k, jnp.where(lane == off + 3, masked, 0.0)).astype(BF)
            v_own = jnp.where(own, v, 1.0).astype(BF)
            start = width // 2
            bias = [
                near_ref[e, :, start - a * LANES : start - a * LANES + length]
                for a in range(length // LANES)
            ]
            scores = dot_cols(q_own, k_own) + jnp.concatenate(bias, 0)
            top = jnp.max(scores, 1, keepdims=True)
            expo = jnp.exp(scores - top)
            sums = dot(expo.astype(BF), v_own)
            total = jnp.where(own, pltpu.roll(sums, DH, 1), sums)
            logsum = top + jnp.log(total)
            extra = split_low(-logsum, lane, off, marker)
            aug_ref[span, e * LANES : (e + 1) * LANES] = jnp.where(own, q, extra).astype(BF)
            mixed.append(sums / total)
        o_ref[span, :] = jnp.where(lane < DH, mixed[0], mixed[1]).astype(BF)


def pair_of(near, pair):
    return pl.BlockSpec((2,) + near.shape[1:], lambda i: (pair, 0, 0))


def attend(ring, batches, lens, normed, weights, at, near, pair, after=()):
    rows, width = normed.shape
    shapes = [out_of((rows, c * LANES), BF) for c in (2, 1, 1, 1)]
    return call(
        functools.partial(attend_kernel, batches, at, len(weights)),
        shapes,
        [ring.places, *lens, normed, near, *weights],
        ins=[SMEM] * (1 + len(lens)) + [fixed(normed), pair_of(near, pair)] + [ANY] * len(weights),
        out_specs=[fixed(s) for s in shapes],
        grid=(1,),
        scratch=[pltpu.VMEM((width, 3 * LANES), BF), pltpu.SemaphoreType.DMA((ring.dp,))],
        us=10,
        after=after,
    )


def attend_back_kernel(batches, *refs):
    lens = refs[: len(batches)]
    go_ref, aug_ref, k_ref, v_ref, o_ref, far_ref, grads_ref, gbase_ref = refs[len(batches) :]
    width = far_ref.shape[-1]
    gbase_ref[...] = jnp.zeros_like(gbase_ref)
    for b, s, length, span in slots_of(batches):
        valid = lens[b][s]
        lane = lax.broadcasted_iota(jnp.int32, (length, LANES), 1)
        place = lax.broadcasted_iota(jnp.int32, (length, LANES), 0)
        masked = jnp.where(place >= valid, NEG, 0.0)
        k = k_ref[span, :].astype(F32)
        v = v_ref[span, :].astype(F32)
        go = go_ref[span, :].astype(F32)
        both = go * o_ref[span, :].astype(F32)
        grads = []
        for e in range(2):
            own = (lane >= DH) == (e == 1)
            off = DH * (1 - e)
            q_own = aug_ref[span, e * LANES : (e + 1) * LANES]
            ones = three_ones(lane, off)
            k_own = jnp.where(own, k, jnp.where(lane == off + 3, masked, ones)).astype(BF)
            v_own = jnp.where(own, v, ones).astype(BF)
            delta = jnp.sum(jnp.where(own, both, 0.0), 1, keepdims=True)
            g_own = jnp.where(own, go, split_low(-delta, lane, off, 0.0)).astype(BF)
            cols = [
                slice(width // 2 - a * LANES, width // 2 - a * LANES + length)
                for a in range(length // LANES)
            ]
            bias = jnp.concatenate([far_ref[e, :, c] for c in cols], 0)
            probs = jnp.exp(dot_cols(k_own, q_own) + bias)
            ds = probs * dot_cols(v_own, g_own)
            for a, c in enumerate(cols):
                gbase_ref[e, :, c] += ds[a * LANES : (a + 1) * LANES]
            ds = ds.astype(BF)
            gv = dot(probs.astype(BF), g_own)
            grads.append((dot_rows(ds, k_own), dot(ds, q_own), gv))
        first = lane < DH
        for i, (a, b) in enumerate(zip(*grads)):
            grads_ref[span, i * LANES : (i + 1) * LANES] = jnp.where(first, a, b).astype(BF)


def attend_back(batches, lens, go, aug, k, v, o, far, pair, after=()):
    rows = go.shape[0]
    outs = [out_of((rows, 3 * LANES), BF), out_of((2,) + far.shape[1:], F32)]
    go_spec = pl.BlockSpec((rows, LANES), lambda i: (0, pair))
    return call(
        functools.partial(attend_back_kernel, batches),
        outs,
        [*lens, go, aug, k, v, o, far],
        ins=[SMEM] * len(lens) + [go_spec] + [fixed(a) for a in (aug, k, v, o)] + [pair_of(far, pair)],
        out_specs=[fixed(o) for o in outs],
        grid=(1,),
        us=10,
        after=after,
    )


def project_out_kernel(halves, pairs, at, places, *refs):
    o_refs, refs = refs[:pairs], refs[pairs:]
    sources, (attn_ref, w_scr, sem) = refs[:halves], refs[halves:]
    cols = pairs * LANES

    @pl.when(pl.program_id(0) == 0)
    def _():
        load(places, sources, w_scr, sem, pl.ds(at, cols))

    o = jnp.concatenate([r[...] for r in o_refs], 1)
    attn_ref[...] = dot_cols(o, w_scr[...]).astype(BF)


def project_out(ring, mixed, weights, at, width, tile=512, after=()):
    rows = mixed[0].shape[0]
    pairs = len(mixed)
    out = out_of((rows, width), BF)
    return call(
        functools.partial(project_out_kernel, len(weights), pairs, at),
        [out],
        [ring.places, *mixed, *weights],
        ins=[SMEM] + [tiles(m, tile) for m in mixed] + [ANY] * len(weights),
        out_specs=[tiles(out, tile)],
        grid=(rows // tile,),
        scratch=[pltpu.VMEM((width, pairs * LANES), BF), pltpu.SemaphoreType.DMA((ring.dp,))],
        us=6,
        after=after,
    )[0]


def rms_parts(field):
    scale = lax.rsqrt(jnp.mean(field * field, -1, keepdims=True) + EPS)
    return (scale, field * scale)


def norm_back(grad_unit, unit, scale):
    return scale * (grad_unit - unit * jnp.mean(grad_unit * unit, -1, keepdims=True))


def norm_kernel(count, short_ref, long_ref, unit_ref):
    unit_ref[...] = rms_parts(pick(count, short_ref, long_ref).astype(F32))[1].astype(BF)


def norm(xs, tile=512, after=()):
    out = out_of((xs[0].shape[0] + xs[1].shape[0], xs[0].shape[1]), BF)
    return call(
        functools.partial(norm_kernel, xs[0].shape[0] // tile),
        [out],
        xs,
        ins=pair_tiles(xs, tile),
        out_specs=[tiles(out, tile)],
        grid=(out.shape[0] // tile,),
        us=5,
        after=after,
    )[0]


def sum_of(refs):
    total = refs[0][...].astype(F32)
    for r in refs[1:]:
        total = total + r[...].astype(F32)
    return total


def add_kernel(count, addends, *refs):
    value = sum_of(refs[:addends]).astype(BF)

    @pl.when(pl.program_id(0) < count)
    def _():
        refs[-2][...] = value

    @pl.when(pl.program_id(0) >= count)
    def _():
        refs[-1][...] = value


def add_all(shapes, fields, tile=512, after=()):
    outs = [out_of(s, BF) for s in shapes]
    return call(
        functools.partial(add_kernel, shapes[0][0] // tile, len(fields)),
        outs,
        fields,
        ins=[tiles(f, tile) for f in fields],
        out_specs=pair_tiles(outs, tile),
        grid=((shapes[0][0] + shapes[1][0]) // tile,),
        us=5,
        after=after,
    )


def gelu_parts(x):
    c = 0.7978845608028654
    d = c * 0.044715
    square = x * x
    t = jnp.tanh(x * (c + d * square))
    half = 0.5 + 0.5 * t
    slope = half + (0.5 * x) * (1.0 - t * t) * (c + 3.0 * d * square)
    return x * half, slope


def ffn_first_kernel(halves, groups, emits, count, places, *refs):
    g_refs, x_refs, refs = refs[:2], refs[2:4], refs[4:]
    attn_refs, refs = refs[:groups], refs[groups:]
    sources, refs = refs[:halves], refs[halves:]
    unit_ref, scale_ref, out_ref, gn_ref = refs[:4]
    grads, (w_scr, total, sem) = refs[4 : 4 + emits], refs[4 + emits :]
    units = w_scr.shape[1] // 2
    step = pl.program_id(0)

    @pl.when(step == 0)
    def _():
        total[...] = jnp.zeros_like(total)
        load_all(places, sources, w_scr, sem, [(0, units), (0, units)])

    middle = pick(count, *x_refs).astype(F32) + sum_of(attn_refs)
    scale, unit = rms_parts(middle)
    unit = unit.astype(BF)
    unit_ref[...] = unit
    scale_ref[...] = jnp.broadcast_to(scale, scale_ref.shape)
    g = pick(count, *g_refs)
    win, wout = w_scr[:, :units], w_scr[:, units:]
    act, slope = gelu_parts(dot(unit, win))
    act = act.astype(BF)
    gpre = (dot(g, wout) * slope).astype(BF)
    lead = places[places.shape[0] - 1].astype(F32)
    out_ref[...] = dot_cols(act, wout) + lead * middle
    gn_ref[...] = dot_cols(gpre, win)
    total[:, :units] += dot_rows(unit, gpre)
    total[:, units:] += dot_rows(g, act)

    @pl.when(step == pl.num_programs(0) - 1)
    def _():
        if emits == 2:
            emit(places, total, *grads)
        else:
            grads[0][...] = total[...]


def ffn_first(ring, gs, xs, fields, weights, units, tile=512, after=()):
    rows, width = fields[0].shape
    unit, field = out_of((rows, width), BF), out_of((rows, width), F32)
    outs = [unit, out_of((rows, LANES), F32), field, field]
    grads = emitted(ring, width, 2 * units)
    return call(
        functools.partial(
            ffn_first_kernel, len(weights), len(fields), len(grads), xs[0].shape[0] // tile
        ),
        outs + grads,
        [ring.places, *gs, *xs, *fields, *weights],
        ins=[SMEM]
        + pair_tiles(gs, tile)
        + pair_tiles(xs, tile)
        + [tiles(a, tile) for a in fields]
        + [ANY] * len(weights),
        out_specs=[tiles(o, tile) for o in outs] + [fixed(o) for o in grads],
        grid=(rows // tile,),
        scratch=[
            pltpu.VMEM((width, 2 * units), BF),
            pltpu.VMEM((width, 2 * units), F32),
            pltpu.SemaphoreType.DMA((2, ring.dp)),
        ],
        us=25,
        after=after,
    )


def ffn_next_kernel(halves, count, places, unit_ref, scale_ref, *refs):
    g_refs, (out_in, gn_in), refs = refs[:2], refs[2:4], refs[4:]
    sources, refs = refs[:halves], refs[halves:]
    out_ref, mid_ref, act_ref, gpre_ref, w_scr, sem = refs
    units = w_scr.shape[1] // 2

    @pl.when(pl.program_id(0) == 0)
    def _():
        load(places, sources, w_scr, sem, pl.ds(0, 2 * units))

    win, wout = w_scr[:, :units], w_scr[:, units:]
    unit = unit_ref[...]
    g = pick(count, *g_refs)
    act, slope = gelu_parts(dot(unit, win))
    act = act.astype(BF)
    gpre = (dot(g, wout) * slope).astype(BF)
    act_ref[...] = act
    gpre_ref[...] = gpre
    out_ref[...] = (out_in[...] + dot_cols(act, wout)).astype(BF)
    lead = places[places.shape[0] - 1].astype(F32)
    back = norm_back(gn_in[...] + dot_cols(gpre, win), unit.astype(F32), scale_ref[:, :1])
    mid_ref[...] = (back + lead * g.astype(F32)).astype(BF)


def ffn_next(ring, unit, scale, gs, out, gn, weights, units, tile=512, after=()):
    rows, width = unit.shape
    outs = [out_of((rows, width), BF)] * 2 + [out_of((rows, units), BF)] * 2
    return call(
        functools.partial(ffn_next_kernel, len(weights), gs[0].shape[0] // tile),
        outs,
        [ring.places, unit, scale, *gs, out, gn, *weights],
        ins=[SMEM, tiles(unit, tile), tiles(scale, tile)]
        + pair_tiles(gs, tile)
        + [tiles(out, tile), tiles(gn, tile)]
        + [ANY] * len(weights),
        out_specs=[tiles(o, tile) for o in outs],
        grid=(rows // tile,),
        scratch=[pltpu.VMEM((width, 2 * units), BF), pltpu.SemaphoreType.DMA((ring.dp,))],
        us=17,
        after=after,
    )


def in_grad_kernel(unit_ref, gpre_ref, total_ref):
    part = dot_rows(unit_ref[...], gpre_ref[...])

    @pl.when(pl.program_id(0) == 0)
    def _():
        total_ref[...] = part

    @pl.when(pl.program_id(0) > 0)
    def _():
        total_ref[...] += part


def in_grad(unit, gpre, tile=1024, after=()):
    rows, width = unit.shape
    out = out_of((width, gpre.shape[1]), F32)
    return call(
        in_grad_kernel,
        [out],
        [unit, gpre],
        ins=[tiles(unit, tile), tiles(gpre, tile)],
        out_specs=[fixed(out)],
        grid=(rows // tile,),
        us=6,
        after=after,
    )[0]


def middle_kernel(halves, groups, pairs, emits, count, at, places, *refs):
    g_refs, mid_refs, refs = refs[:2], refs[2 : 2 + groups], refs[2 + groups :]
    act_ref, in_ref, refs = refs[0], refs[1], refs[2:]
    o_refs, refs = refs[:pairs], refs[pairs:]
    sources, refs = refs[:halves], refs[halves:]
    go_ref, grads, (w_scr, total, sem) = refs[0], refs[1 : 1 + emits], refs[1 + emits :]
    units = act_ref.shape[1]
    cols = pairs * LANES
    step = pl.program_id(0)

    @pl.when(step == 0)
    def _():
        total[:, units:] = jnp.zeros((total.shape[0], total.shape[1] - units), F32)
        total[:, :units] = in_ref[...]
        load(places, sources, w_scr, sem, pl.ds(at, cols))

    grad = sum_of(mid_refs).astype(BF)
    go_ref[...] = dot(grad, w_scr[...]).astype(BF)
    o = jnp.concatenate([r[...] for r in o_refs], 1)
    total[:, 2 * units :] += dot_rows(grad, o)
    total[:, units : 2 * units] += dot_rows(pick(count, *g_refs), act_ref[...])

    @pl.when(step == pl.num_programs(0) - 1)
    def _():
        if emits == 2:
            emit(places, total, *grads)
        else:
            grads[0][...] = total[...]


def middle_back(ring, gs, mids, act, grad_in, mixed, weights, at, tile=512, after=()):
    rows, width = mids[0].shape
    pairs = len(mixed)
    cols = pairs * LANES
    units = act.shape[1]
    go = out_of((rows, cols), BF)
    grads = emitted(ring, width, 2 * units + cols)
    return call(
        functools.partial(
            middle_kernel, len(weights), len(mids), pairs, len(grads), gs[0].shape[0] // tile, at
        ),
        [go] + grads,
        [ring.places, *gs, *mids, act, grad_in, *mixed, *weights],
        ins=[SMEM]
        + pair_tiles(gs, tile)
        + [tiles(a, tile) for a in (*mids, act)]
        + [fixed(grad_in)]
        + [tiles(a, tile) for a in mixed]
        + [ANY] * len(weights),
        out_specs=[tiles(go, tile)] + [fixed(g) for g in grads],
        grid=(rows // tile,),
        scratch=[
            pltpu.VMEM((width, cols), BF),
            pltpu.VMEM((width, 2 * units + cols), F32),
            pltpu.SemaphoreType.DMA((ring.dp,)),
        ],
        us=9,
        after=after,
    )


def input_back_kernel(plan, groups, pairs, count, places, short_ref, long_ref, *refs):
    mid_refs, refs = refs[:groups], refs[groups:]
    g_refs, refs = refs[:pairs], refs[pairs:]
    sources, (part_ref, w_scr, sem) = refs[:-3], refs[-3:]

    @pl.when(pl.program_id(0) == 0)
    def _():
        load_all(places, sources, w_scr, sem, plan)

    part = dot_cols(jnp.concatenate([r[...] for r in g_refs], 1), w_scr[...])
    scale, unit = rms_parts(pick(count, short_ref, long_ref).astype(F32))
    lead = places[places.shape[0] - 1].astype(F32)
    part_ref[...] = (norm_back(part, unit, scale) + lead * sum_of(mid_refs)).astype(BF)


def input_back(ring, xs, mids, grads, weights, plan, tile=512, after=()):
    rows, width = grads[0].shape[0], xs[0].shape[1]
    pairs = len(grads)
    out = out_of((rows, width), BF)
    return call(
        functools.partial(input_back_kernel, plan, len(mids), pairs, xs[0].shape[0] // tile),
        [out],
        [ring.places, *xs, *mids, *grads, *weights],
        ins=[SMEM]
        + pair_tiles(xs, tile)
        + [tiles(a, tile) for a in (*mids, *grads)]
        + [ANY] * len(weights),
        out_specs=[tiles(out, tile)],
        grid=(rows // tile,),
        scratch=[
            pltpu.VMEM((width, 3 * pairs * LANES), BF),
            pltpu.SemaphoreType.DMA((len(plan), ring.dp)),
        ],
        us=9,
        after=after,
    )[0]


def last_kernel(emits, pairs, buckets, places, bounds, unit_ref, *refs):
    g_refs, refs = refs[:pairs], refs[pairs:]
    bases, refs = refs[:pairs], refs[pairs:]
    grads, refs = refs[:emits], refs[emits:]
    table_ref, total = refs
    step = pl.program_id(0)
    cols = 3 * pairs * LANES

    @pl.when(step == 0)
    def _():
        total[...] = jnp.zeros_like(total)

    total[:, :cols] += dot_rows(unit_ref[...], jnp.concatenate([r[...] for r in g_refs], 1))

    @pl.when(step == pl.num_programs(0) - 1)
    def _():
        fields = [ref[e] for ref in bases for e in range(2)]
        table = bucket_field(bounds, fields, buckets, 0)
        table_ref[...] = table
        if emits == 2:
            rows = grads[0].shape[1]
            table = jnp.concatenate([table, jnp.zeros((rows - 8, LANES), F32)], 0)
            table = jnp.concatenate([jnp.zeros((rows, cols), F32), table], 1)
            emit(places, total, *grads, extra=table)
        else:
            grads[0][...] = total[...]


def last_grads(ring, boundaries, buckets, unit, grads, bases, tile=512, after=()):
    rows, width = unit.shape
    pairs = len(grads)
    cols = 3 * pairs * LANES + LANES
    outs = emitted(ring, width, cols)
    table = out_of((8, LANES), F32)
    *outs, table = call(
        functools.partial(last_kernel, len(outs), pairs, buckets),
        outs + [table],
        [ring.places, boundaries, unit, *grads, *bases],
        ins=[SMEM, SMEM, tiles(unit, tile)]
        + [tiles(a, tile) for a in grads]
        + [fixed(b) for b in bases],
        out_specs=[fixed(o) for o in outs] + [fixed(table)],
        grid=(rows // tile,),
        scratch=[pltpu.VMEM((width, cols), F32)],
        us=9,
        after=after,
    )
    share = width // ring.dp
    table = jnp.pad(table, ((0, share - 8), (cols - LANES, 0)))
    return halves(ring, outs, table)


def pad_cols(array, cols):
    return jnp.pad(array, ((0, 0), (0, cols - array.shape[1]))) if cols > array.shape[1] else array


def on_device(
    sizes,
    x_short,
    x_long,
    len_short,
    len_long,
    boundaries,
    q_weight,
    k_weight,
    v_weight,
    out_weight,
    in_weight,
    ff_out_weight,
    attn_gain,
    ffn_gain,
    bias_table,
    cot_short,
    cot_long,
):
    ring = Ring(sizes)
    quarter = ring.quarter
    width = x_short.shape[2]
    buckets, heads = bias_table.shape
    real = heads * DH
    cols = -(-real // LANES) * LANES
    pairs = cols // LANES
    units = in_weight.shape[1] // 2
    span = 2 * max(x_short.shape[1], x_long.shape[1])
    batches = [x.shape[:2] for x in (x_short, x_long)]
    lens = (len_short, len_long)

    xs = [x.reshape(-1, width) for x in (x_short, x_long)]
    gs = [g.reshape(-1, width) for g in (cot_short, cot_long)]

    col_a, col_f = (v.astype(F32)[:, None] for v in (attn_gain, ffn_gain))
    padded = [pad_cols(w, cols) for w in (q_weight, k_weight, v_weight, out_weight)]
    scaled = [(w.astype(F32) * col_a).astype(BF) for w in padded[:3]]
    pieces = [w[:, p * LANES : (p + 1) * LANES] for p in range(pairs) for w in scaled]
    own = jnp.concatenate(pieces + [padded[3]], 1)[None]
    win = (in_weight.astype(F32) * col_f).astype(BF)
    own1, own2 = (
        jnp.concatenate([w[:, at : at + units] for w in (win, ff_out_weight)], 1)[None]
        for at in (0, units)
    )

    step = 3 * LANES
    both = list(range(quarter))
    wide = own.shape[2]

    got = ring.far(own)
    near, far = bias_bases(boundaries, bias_table, cols // DH, span)
    held, own1 = join([own, *got], [(both, 0, wide)], after=[near], through=[own1])
    got = ring.first(held)
    got1 = ring.far(own1)
    unit = norm(xs, after=[held])
    head, rest = join([held, got], [((0, 1), 0, step), ((0, 1), step, wide)], after=[unit])
    qkv = blocks_of(ring, head, ring.last(head))
    rest = blocks_of(ring, rest, ring.last(rest))
    held1, own2 = join([own1, *got1], [(both, 0, 2 * units)], after=[head], through=[own2])
    got1 = ring.first(held1)
    got2 = ring.far(own2)

    fwd = []
    after = [held1]
    for p in range(pairs):
        weights, at = (rest, (p - 1) * step) if p else (qkv, 0)
        fwd.append(attend(ring, batches, lens, unit, weights, at, near, p, after=after))
        if p == 0:
            plan = [((0, 1), 0, units), ((0, 1), units, 2 * units)]
            helds = join([held1, got1], plan, after=[fwd[0][0]])
            gots = [ring.last(h) for h in helds]
            after = helds
        if p == min(1, pairs - 1):
            held2 = join([own2, *got2], [(both, 0, 2 * units)], after=[fwd[p][0]])[0]
            got2 = ring.first(held2)
            after = [held2]
    (held2,) = join([held2, got2], [((0, 1), 0, 2 * units)], after=[fwd[-1][0], *gots])
    got2 = ring.last(held2)
    mixed = [f[3] for f in fwd]
    out_at = (pairs - 1) * step
    attn = project_out(ring, mixed, rest, out_at, width, after=[held2])
    fields = [attn] + ring.exchange(attn)
    first = [b for h, g in zip(helds, gots) for b in blocks_of(ring, h, g)]
    second = blocks_of(ring, held2, got2)

    unit_f, scale, out, gn, *grad1 = ffn_first(ring, gs, xs, fields, first, units)
    keep1, send = halves(ring, grad1)
    got1 = ring.last(send)
    out, mid, act, gpre = ffn_next(ring, unit_f, scale, gs, out, gn, second, units)
    keep1, send, mid, out = fold((keep1, got1, 0), through=[mid, out])
    mids = [mid] + ring.exchange(mid)
    outs = [out] + ring.exchange(out)
    got1 = ring.first(send)
    grad_in = in_grad(unit_f, gpre, after=[keep1])
    go, *grad2 = middle_back(ring, gs, mids, act, grad_in, mixed, rest, out_at)
    keep2, send = halves(ring, grad2)
    got2 = ring.last(send)
    keep1, *sends = fold((keep1, got1, 1), after=[go])
    got1 = ring.far_all(sends)

    back = []
    after = [keep1]
    for p in range(pairs):
        aug, k, v, o = fwd[p]
        back.append(attend_back(batches, lens, go, aug, k, v, o, far, p, after=after))
        if p == min(1, pairs - 1):
            keep2, send = fold((keep2, got2, 0), after=[back[-1][0], *got1])
            got2 = ring.first(send)
            after = [keep2]
    keep2, *sends = fold((keep2, got2, 1), after=[back[-1][0]])
    got2 = ring.far_all(sends)

    grads = [b[0] for b in back]
    keep, send = last_grads(
        ring, boundaries, buckets, unit, grads, [b[1] for b in back], after=[keep2]
    )
    got = ring.last(send)
    plan = [(0, step), (0, (pairs - 1) * step)][: 2 if pairs > 1 else 1]
    weights = [*qkv, *rest][: len(plan) * len(qkv)]
    part = input_back(ring, xs, mids, grads, weights, plan, after=[keep])
    keep, send, part = fold((keep, got, 0), through=[part])
    got = ring.first(send)
    parts = [part] + ring.exchange(part)
    shapes = [x.shape for x in xs]
    ys = add_all(shapes, outs, after=[keep])
    keep, *sends = fold((keep, got, 1), after=[ys[0]])
    got = ring.far_all(sends)
    grad_xs = add_all(shapes, parts, after=[keep])
    plan = [
        [(0, 0, units), (1, 0, units)],
        [(0, units, 2 * units), (1, units, 2 * units)],
        [(1, 2 * units, 2 * units + cols)],
    ]
    grad_in, grad_ff, grad_o, gain_f = final(
        [[keep1, *got1], [keep2, *got2]], plan, [0], col_f, [in_weight], after=[keep]
    )
    plan = [
        [(0, p * step + i * LANES, p * step + (i + 1) * LANES) for p in range(pairs)]
        for i in range(3)
    ]
    plan.append([(0, pairs * step, pairs * step + LANES)])
    gq, gk, gv, table, gain_a = final([[keep, *got]], plan, [0, 1, 2], col_a, padded[:3])
    gain = jnp.stack([gain_a[:, 0], gain_f[:, 0]])
    for other in ring.exchange(gain):
        gain = gain + other
    return (
        ys[0].reshape(x_short.shape),
        ys[1].reshape(x_long.shape),
        grad_xs[0].reshape(x_short.shape),
        grad_xs[1].reshape(x_long.shape),
        gq[:, :real],
        gk[:, :real],
        gv[:, :real],
        grad_o[:, :real],
        grad_in,
        grad_ff,
        gain[0],
        gain[1],
        table[:heads, :buckets].T,
    )


def solution(mesh):
    sizes = (mesh.shape["dp"], mesh.shape["mp"])
    return jax.shard_map(
        functools.partial(on_device, sizes),
        mesh=mesh,
        in_specs=(
            P("dp", None, None),
            P("dp", None, None),
            P("dp"),
            P("dp"),
            P(),
            P("dp", "mp"),
            P("dp", "mp"),
            P("dp", "mp"),
            P("dp", "mp"),
            P("dp", "mp"),
            P("dp", "mp"),
            P("dp"),
            P("dp"),
            P(None, "mp"),
            P("dp", None, None),
            P("dp", None, None),
        ),
        out_specs=(
            P("dp", None, None),
            P("dp", None, None),
            P("dp", None, None),
            P("dp", None, None),
            P("dp", "mp"),
            P("dp", "mp"),
            P("dp", "mp"),
            P("dp", "mp"),
            P("dp", "mp"),
            P("dp", "mp"),
            P("dp"),
            P("dp"),
            P(None, "mp"),
        ),
        check_vma=False,
    )
```

time: 402 us -> 314 us (0.78)
  waiting for transfers between devices: 63.2 us -> 16.9 us
  Pallas kernels: 240 us -> 213 us
  local copies, waits for them, and re-layouts: 33.3 us -> 24.9 us
  starting transfers between devices: 50.7 us -> 46.2 us
    ppermute x12 -> x14, waiting for transfers between devices: 54.6 us -> 5.73 us  [near(): return lax.ppermute(array, ('dp', 'mp'), pairs)]
    pallas_call x34 -> x31, Pallas kernels: 240 us -> 213 us  [call(): pl.pallas_call(body, out_shape=list(outs) + [out_of(t.shape, t.dtype) for...]
    ppermute x18 -> x9, starting transfers between devices: 26.4 us -> 14.5 us  [far(): lax.ppermute(array, 'dp', [(i, i ^ 4 * step) for i in range(self.dp)])]
    unnamed x107 -> x91, local copies, waits for them, and re-layouts: 28.1 us -> 17.1 us
    ppermute x18 -> x9, waiting for transfers between devices: 8.55 us -> 0.12 us  [far(): lax.ppermute(array, 'dp', [(i, i ^ 4 * step) for i in range(self.dp)])]
    ppermute x6 -> x9, waiting for transfers between devices: 0.02 us -> 6.18 us  [far_all(): lax.ppermute(a, 'dp', [(i, i ^ 4 * (step + 1)) for i in range(self.dp)])]
    ppermute x5, waiting for transfers between devices: 0.01 us -> 4.85 us  [exchange(): lax.ppermute(array, 'mp', [(i, i ^ k) for i in range(self.mp)])]
    ppermute x6 -> x9, starting transfers between devices: 9.47 us -> 14.1 us  [far_all(): lax.ppermute(a, 'dp', [(i, i ^ 4 * (step + 1)) for i in range(self.dp)])]
  transfers between devices with their start and end apart: 41 -> 37, of which waited for: 7 -> 7; matrix products, arithmetic and copies ran while one was open for 4% -> 4% of each run, Pallas kernels for 39% -> 63%
where the time goes in v3:
time: 314 us; the launch traced here: 308 us
  Pallas kernels  213 us (68%)
  starting transfers between devices  46.2 us (15%)
  local copies, waits for them, and re-layouts  24.9 us (8%)
  waiting for transfers between devices  16.9 us (5%)
  other arithmetic  6.19 us (2%)
    pallas_call x31, Pallas kernels, call(): pl.pallas_call(body, out_shape=list(outs) + [out_of(t.shape, t.dtype) for...  213 us
    unnamed x91, local copies, waits for them, and re-layouts  17.1 us
    ppermute x14, starting transfers between devices, near(): return lax.ppermute(array, ('dp', 'mp'), pairs)  17.1 us
    ppermute x9, starting transfers between devices, far(): lax.ppermute(array, 'dp', [(i, i ^ 4 * step) for i in range(self.dp)])  14.5 us
    ppermute x9, starting transfers between devices, far_all(): lax.ppermute(a, 'dp', [(i, i ^ 4 * (step + 1)) for i in range(self.dp)])  14.1 us
  transfers between devices with their start and end apart: 37, of which 7 were waited for; matrix products, arithmetic and copies ran while one was open for 4% of the time, Pallas kernels for 63%

profile of v3, /device:TPU:0, one launch (start us, length us, event | category | flops | bytes accessed | tf_op | source)
XLA Modules:
  0.0 308.2 jit_solution(10417590648007875547)
XLA Ops:
  3.6 3.1 %collective-permute-start = (bf16[1,48,1536]{2,1,0:T(8,128)(2,1)S(1)}, bf16[1,48,1536]{2,1,0:T(8,128)(2,1)S(1)}, u32[]{:S(2)}, u32[]{:S(2)}) collective-permute-start(bf16[1,48,1536]{2,1,0:T(8,128)(2,1)S(1)} %bitcast.32), channel_id=1, source_target_pairs={{0,8},{2,10},{4,12},{6,14},{8,0},{10,2},{12,4},{14,6},{16,24},{18,... | collective-permute-start | bytes 442376 | tf_op jit(solution)/shard_map/ppermute | solution.py:103
  14.3 7.7 %shard_map.255 = (f32[6,128,1024]{2,1,0:T(8,128)}, f32[6,128,1024]{2,1,0:T(8,128)}) custom-call(s32[15]{0:T(128)} %refs_1_.15, bf16[8,32]{1,0:T(8,128)(2,1)} %scatter.4.refs_1_), custom_call_target="tpu_custom_call" | custom-call | flops 2000000000 | bytes 1000 | tf_op jit(solution)/shard_map/pallas_call | solution.py:70
  27.8 3.5 %collective-permute-start.6 = (bf16[1,48,1536]{2,1,0:T(8,128)(2,1)}, bf16[1,48,1536]{2,1,0:T(8,128)(2,1)S(1)}, u32[]{:S(2)}, u32[]{:S(2)}) collective-permute-start(bf16[1,48,1536]{2,1,0:T(8,128)(2,1)} %get-tuple-element.105.refs_0_), channel_id=1, source_target_pairs={{0,16},{2,18},{4,20},{6,22},{8,24},{10,26},{12,28},{14,30},{16,0},... | collective-permute-start | bytes 442376 | tf_op jit(solution)/shard_map/ppermute | solution.py:103
  31.6 5.0 %shard_map.257.refs_2_.refs_3_ = bf16[2048,768]{1,0:T(8,128)(2,1)} custom-call(bf16[1024,768]{1,0:T(8,128)(2,1)} %bitcast.42, bf16[1024,768]{1,0:T(8,128)(2,1)} %bitcast.45, bf16[4,48,1536]{2,1,0:T(8,128)(2,1)} %get-tuple-element.103.refs_2_.refs_0_), custom_call_target="tpu_custom_call" | custom-call | flops 5000000000 | bytes 1000 | tf_op jit(solution)/shard_map/pallas_call | solution.py:70
  51.6 9.8 %shard_map.260 = (bf16[2048,256]{1,0:T(8,128)(2,1)}, bf16[2048,128]{1,0:T(8,128)(2,1)}, bf16[2048,128]{1,0:T(8,128)(2,1)}, bf16[2048,128]{1,0:T(8,128)(2,1)}) custom-call(s32[17]{0:T(128)} %pad_add_fusion.refs_0_, s32[4]{0:T(128)} %refs_0_.7, s32[2]{0:T(128)} %refs_1_.14, bf16[2048,768]{1,0:T(8,128)(2,1)} %shard_map.257.refs_2_.refs_3_, ...), custom_call_target="tpu_custom_call" | custom-call | flops 10000000000 | bytes 1000 | tf_op jit(solution)/shard_map/pallas_call | solution.py:70
  61.4 4.2 %collective-permute-done.9.refs_1_ = bf16[4,48,1536]{2,1,0:T(8,128)(2,1)S(1)} collective-permute-done((bf16[4,48,1536]{2,1,0:T(8,128)(2,1)}, bf16[4,48,1536]{2,1,0:T(8,128)(2,1)S(1)}, u32[]{:S(2)}, u32[]{:S(2)}) %collective-permute-start.9) | collective-permute-done | bytes 589856 | tf_op jit(solution)/shard_map/ppermute | solution.py:119
  70.8 9.8 %shard_map.262 = (bf16[2048,256]{1,0:T(8,128)(2,1)}, bf16[2048,128]{1,0:T(8,128)(2,1)}, bf16[2048,128]{1,0:T(8,128)(2,1)}, bf16[2048,128]{1,0:T(8,128)(2,1)}) custom-call(s32[17]{0:T(128)} %pad_add_fusion.refs_0_, s32[4]{0:T(128)} %refs_0_.7, s32[2]{0:T(128)} %refs_1_.14, bf16[2048,768]{1,0:T(8,128)(2,1)} %shard_map.257.refs_2_.refs_3_, ...), custom_call_target="tpu_custom_call" | custom-call | flops 10000000000 | bytes 1000 | tf_op jit(solution)/shard_map/pallas_call | solution.py:70
  85.1 10.2 %shard_map.264 = (bf16[2048,256]{1,0:T(8,128)(2,1)}, bf16[2048,128]{1,0:T(8,128)(2,1)}, bf16[2048,128]{1,0:T(8,128)(2,1)}, bf16[2048,128]{1,0:T(8,128)(2,1)}) custom-call(s32[17]{0:T(128)} %pad_add_fusion.refs_0_, s32[4]{0:T(128)} %refs_0_.7, s32[2]{0:T(128)} %refs_1_.14, bf16[2048,768]{1,0:T(8,128)(2,1)} %shard_map.257.refs_2_.refs_3_, ...), custom_call_target="tpu_custom_call" | custom-call | flops 10000000000 | bytes 1000 | tf_op jit(solution)/shard_map/pallas_call | solution.py:70
  99.0 6.3 %shard_map.266.refs_5_ = bf16[2048,768]{1,0:T(8,128)(2,1)} custom-call(s32[17]{0:T(128)} %pad_add_fusion.refs_0_, bf16[2048,128]{1,0:T(8,128)(2,1)} %get-tuple-element.107.refs_1_.refs_7_.refs_6_, bf16[2048,128]{1,0:T(8,128)(2,1)} %get-tuple-element.112.refs_2_.refs_8_.refs_6_, bf16[2048,128]{1,0:T(8,128)(2,1)} %get-tuple-element.115.refs_3_.refs_9_.refs_6_, ...), custom_call_target="tpu_custom_call" | custom-call | flops 6000000000 | bytes 1000 | tf_op jit(solution)/shard_map/pallas_call | solution.py:70
  106.4 4.8 %collective-permute-done.16.refs_6_ = bf16[2048,768]{1,0:T(8,128)(2,1)S(1)} collective-permute-done((bf16[2048,768]{1,0:T(8,128)(2,1)}, bf16[2048,768]{1,0:T(8,128)(2,1)S(1)}, u32[]{:S(2)}, u32[]{:S(2)}) %collective-permute-start.16) | collective-permute-done | bytes 3145760 | tf_op jit(solution)/shard_map/ppermute | solution.py:129
  112.9 25.2 %shard_map.267 = (bf16[2048,768]{1,0:T(8,128)(2,1)}, f32[2048,128]{1,0:T(8,128)}, f32[2048,768]{1,0:T(8,128)}, f32[2048,768]{1,0:T(8,128)}, f32[8,48,1536]{2,1,0:T(8,128)}, /*index=5*/bf16[8,48,1536]{2,1,0:T(8,128)(2,1)}) custom-call(s32[17]{0:T(128)} %pad_add_fusion.refs_0_, bf16[1024,768]{1,0:T(8,128)(2,1)} %bitcast.36, bf16[1024,768]{1,0:T(8,128)(2,1)} %bitcast.39, ...), custom_call_target="tpu_custom_call" | custom-call | flops 24999999488 | bytes 1000 | tf_op jit(solution)/shard_map/pallas_call | solution.py:70
  140.2 19.4 %shard_map.268 = (bf16[2048,768]{1,0:T(8,128)(2,1)}, bf16[2048,768]{1,0:T(8,128)(2,1)}, bf16[2048,768]{1,0:T(8,128)(2,1)}, bf16[2048,768]{1,0:T(8,128)(2,1)}) custom-call(s32[17]{0:T(128)} %pad_add_fusion.refs_0_, bf16[2048,768]{1,0:T(8,128)(2,1)} %get-tuple-element.119.refs_1_.refs_0_, f32[2048,128]{1,0:T(8,128)} %get-tuple-element.120.refs_2_, ...), custom_call_target="tpu_custom_call" | custom-call | flops 16999999488 | bytes 1000 | tf_op jit(solution)/shard_map/pallas_call | solution.py:70
  160.6 3.3 %shard_map.269 = (f32[4,48,1536]{2,1,0:T(8,128)}, bf16[4,48,1536]{2,1,0:T(8,128)(2,1)}, bf16[2048,768]{1,0:T(8,128)(2,1)}, bf16[2048,768]{1,0:T(8,128)(2,1)}) custom-call(f32[8,48,1536]{2,1,0:T(8,128)} %get-tuple-element.117.refs_0_, bf16[8,48,1536]{2,1,0:T(8,128)(2,1)} %copy-done, ...), custom_call_target="tpu_custom_call", output_to_operand_aliasing={{2}: (2, {}), {3}: (3, {})} | custom-call | flops 2000000000 | bytes 1000 | tf_op jit(solution)/shard_map/pallas_call | solution.py:70
  164.8 6.6 %shard_map.270.refs_6_ = f32[768,768]{1,0:T(8,128)} custom-call(bf16[2048,768]{1,0:T(8,128)(2,1)} %get-tuple-element.119.refs_1_.refs_0_, bf16[2048,768]{1,0:T(8,128)(2,1)} %get-tuple-element.128.refs_1_, f32[4,48,1536]{2,1,0:T(8,128)} %get-tuple-element.129.refs_2_.refs_0_), custom_call_target="tpu_custom_call" | custom-call | flops 6000000000 | bytes 1000 | tf_op jit(solution)/shard_map/pallas_call | solution.py:70
  173.0 14.3 %shard_map.271 = (bf16[2048,384]{1,0:T(8,128)(2,1)}, f32[8,48,1920]{2,1,0:T(8,128)}, bf16[8,48,1920]{2,1,0:T(8,128)(2,1)}) custom-call(s32[17]{0:T(128)} %pad_add_fusion.refs_0_, bf16[1024,768]{1,0:T(8,128)(2,1)} %bitcast.38, bf16[1024,768]{1,0:T(8,128)(2,1)} %bitcast.41, bf16[2048,768]{1,0:T(8,128)(2,1)} %get-tuple-element.126.refs_3_, ...), custom_call_target="tpu_custom_call" | custom-call | flops 8999999488 | bytes 1000 | tf_op jit(solution)/shard_map/pallas_call | solution.py:70
  195.9 9.2 %shard_map.273 = (bf16[2048,384]{1,0:T(8,128)(2,1)}, f32[2,128,1024]{2,1,0:T(8,128)}) custom-call(s32[4]{0:T(128)} %refs_0_.7, s32[2]{0:T(128)} %refs_1_.14, bf16[2048,384]{1,0:T(8,128)(2,1)} %get-tuple-element.130.refs_2_, bf16[2048,256]{1,0:T(8,128)(2,1)} %get-tuple-element.109.refs_2_.refs_3_, bf16[2048,128]{1,0:T(8,128)(2,1)} %get-tuple-element.131.refs_4_, ...), custom_call_target="tpu_custom_call" | custom-call | flops 10000000000 | bytes 1000 | tf_op jit(solution)/shard_map/pallas_call | solution.py:70
  205.1 9.2 %shard_map.274 = (bf16[2048,384]{1,0:T(8,128)(2,1)}, f32[2,128,1024]{2,1,0:T(8,128)}) custom-call(s32[4]{0:T(128)} %refs_0_.7, s32[2]{0:T(128)} %refs_1_.14, bf16[2048,384]{1,0:T(8,128)(2,1)} %get-tuple-element.130.refs_2_, bf16[2048,256]{1,0:T(8,128)(2,1)} %get-tuple-element.114.refs_4_.refs_3_, bf16[2048,128]{1,0:T(8,128)(2,1)} %get-tuple-element.137.refs_4_, ...), custom_call_target="tpu_custom_call" | custom-call | flops 10000000000 | bytes 1000 | tf_op jit(solution)/shard_map/pallas_call | solution.py:70
  215.5 3.7 %shard_map.275 = (f32[4,48,1920]{2,1,0:T(8,128)}, bf16[4,48,1920]{2,1,0:T(8,128)(2,1)}) custom-call(f32[8,48,1920]{2,1,0:T(8,128)} %get-tuple-element.142.refs_0_, bf16[8,48,1920]{2,1,0:T(8,128)(2,1)} %copy-done.7, bf16[2048,384]{1,0:T(8,128)(2,1)} %get-tuple-element.139.refs_2_.refs_4_.refs_6_, bf16[48,1536]{1,0:T(8,128)(2,1)} %copy-done.26, ...), custom_call_target="tpu_custom_call" | custom-call | flops 2000000000 | bytes 1000 | tf_op jit(solution)/shard_map/pallas_call | solution.py:70
  220.9 9.2 %shard_map.276 = (bf16[2048,384]{1,0:T(8,128)(2,1)}, f32[2,128,1024]{2,1,0:T(8,128)}) custom-call(s32[4]{0:T(128)} %refs_0_.7, s32[2]{0:T(128)} %refs_1_.14, bf16[2048,384]{1,0:T(8,128)(2,1)} %get-tuple-element.130.refs_2_, bf16[2048,256]{1,0:T(8,128)(2,1)} %get-tuple-element.116.refs_2_.refs_3_, bf16[2048,128]{1,0:T(8,128)(2,1)} %get-tuple-element.140.refs_4_, ...), custom_call_target="tpu_custom_call" | custom-call | flops 10000000000 | bytes 1000 | tf_op jit(solution)/shard_map/pallas_call | solution.py:70
  234.3 12.2 %shard_map.278 = (f32[8,48,1280]{2,1,0:T(8,128)}, bf16[8,48,1280]{2,1,0:T(8,128)(2,1)}, f32[8,128]{1,0:T(8,128)}) custom-call(s32[17]{0:T(128)} %pad_add_fusion.refs_0_, s32[15]{0:T(128)} %refs_1_.15, bf16[2048,768]{1,0:T(8,128)(2,1)} %shard_map.257.refs_2_.refs_3_, bf16[2048,384]{1,0:T(8,128)(2,1)} %get-tuple-element.136.refs_3_.refs_5_, ...), custom_call_target="tpu_custom_call" | custom-call | flops 8999999488 | bytes 1000 | tf_op jit(solution)/shard_map/pallas_call | solution.py:70
  247.6 12.5 %shard_map.279.refs_2_ = bf16[2048,768]{1,0:T(8,128)(2,1)} custom-call(s32[17]{0:T(128)} %pad_add_fusion.refs_0_, bf16[1024,768]{1,0:T(8,128)(2,1)} %bitcast.44, bf16[1024,768]{1,0:T(8,128)(2,1)} %bitcast.47, bf16[2048,768]{1,0:T(8,128)(2,1)} %get-tuple-element.126.refs_3_, bf16[2048,768]{1,0:T(8,128)(2,1)} %copy-done.5, ...), custom_call_target="tpu_custom_call" | custom-call | flops 8999999488 | bytes 1000 | tf_op jit(solution)/shard_map/pallas_call | solution.py:70
  272.6 5.7 %shard_map.281 = (bf16[1024,768]{1,0:T(8,128)(2,1)}, bf16[1024,768]{1,0:T(8,128)(2,1)}) custom-call(bf16[2048,768]{1,0:T(8,128)(2,1)} %get-tuple-element.125.refs_0_, bf16[2048,768]{1,0:T(8,128)(2,1)} %copy-done.4, f32[4,48,1280]{2,1,0:T(8,128)} %get-tuple-element.156.refs_2_.refs_0_), custom_call_target="tpu_custom_call" | custom-call | flops 5000000000 | bytes 1000 | tf_op jit(solution)/shard_map/pallas_call | solution.py:70
  291.0 5.1 %collective-permute-done.31.refs_6_ = bf16[48,1280]{1,0:T(8,128)(2,1)S(1)} collective-permute-done((bf16[48,1280]{1,0:T(8,128)(2,1)}, bf16[48,1280]{1,0:T(8,128)(2,1)S(1)}, u32[]{:S(2)}, u32[]{:S(2)}) %collective-permute-start.31) | collective-permute-done | bytes 122912 | tf_op jit(solution)/shard_map/ppermute | solution.py:109
  302.3 5.7 %shard_map.283 = (bf16[1024,768]{1,0:T(8,128)(2,1)}, bf16[1024,768]{1,0:T(8,128)(2,1)}) custom-call(bf16[2048,768]{1,0:T(8,128)(2,1)} %get-tuple-element.159.refs_0_, bf16[2048,768]{1,0:T(8,128)(2,1)} %collective-permute-done.28.refs_1_, f32[48,1280]{1,0:T(8,128)} %get-tuple-element.161.refs_2_.refs_4_.refs_10_), custom_call_target="tpu_custom_call" | custom-call | flops 5000000000 | bytes 1000 | tf_op jit(solution)/shard_map/pallas_call | solution.py:70
  (191 shorter events, 101.2 us)
Async XLA Ops:
  3.6 18.4 %collective-permute-start = (bf16[1,48,1536]{2,1,0:T(8,128)(2,1)S(1)}, bf16[1,48,1536]{2,1,0:T(8,128)(2,1)S(1)}, u32[]{:S(2)}, u32[]{:S(2)}) collective-permute-start(bf16[1,48,1536]{2,1,0:T(8,128)(2,1)S(1)} %bitcast.32), channel_id=1, source_target_pairs={{0,8},{2,10},{4,12},{6,14},{8,0},{10,2},{12,4},{14,6},{16,24},{18,... | collective-permute-start | bytes 442376 | tf_op jit(solution)/shard_map/ppermute | solution.py:103
  6.7 15.3 %collective-permute-start.1 = (bf16[1,48,1536]{2,1,0:T(8,128)(2,1)S(1)}, bf16[1,48,1536]{2,1,0:T(8,128)(2,1)S(1)}, u32[]{:S(2)}, u32[]{:S(2)}) collective-permute-start(bf16[1,48,1536]{2,1,0:T(8,128)(2,1)S(1)} %bitcast.33), channel_id=1, source_target_pairs={{0,16},{2,18},{4,20},{6,22},{8,24},{10,26},{12,28},{14,30},{16,0},... | collective-permute-start | bytes 442376 | tf_op jit(solution)/shard_map/ppermute | solution.py:103
  27.2 14.7 %collective-permute-start.5 = (bf16[1,48,1536]{2,1,0:T(8,128)(2,1)}, bf16[1,48,1536]{2,1,0:T(8,128)(2,1)S(1)}, u32[]{:S(2)}, u32[]{:S(2)}) collective-permute-start(bf16[1,48,1536]{2,1,0:T(8,128)(2,1)} %get-tuple-element.105.refs_0_), channel_id=1, source_target_pairs={{0,8},{2,10},{4,12},{6,14},{8,0},{10,2},{12,4},{14,6},{16,24},{18,... | collective-permute-start | bytes 442376 | tf_op jit(solution)/shard_map/ppermute | solution.py:103
  27.8 14.1 %collective-permute-start.6 = (bf16[1,48,1536]{2,1,0:T(8,128)(2,1)}, bf16[1,48,1536]{2,1,0:T(8,128)(2,1)S(1)}, u32[]{:S(2)}, u32[]{:S(2)}) collective-permute-start(bf16[1,48,1536]{2,1,0:T(8,128)(2,1)} %get-tuple-element.105.refs_0_), channel_id=1, source_target_pairs={{0,16},{2,18},{4,20},{6,22},{8,24},{10,26},{12,28},{14,30},{16,0},... | collective-permute-start | bytes 442376 | tf_op jit(solution)/shard_map/ppermute | solution.py:103
  45.2 35.4 %collective-permute-start.10 = (bf16[1,48,1536]{2,1,0:T(8,128)(2,1)}, bf16[1,48,1536]{2,1,0:T(8,128)(2,1)S(1)}, u32[]{:S(2)}, u32[]{:S(2)}) collective-permute-start(bf16[1,48,1536]{2,1,0:T(8,128)(2,1)} %get-tuple-element.113.refs_0_), channel_id=1, source_target_pairs={{0,8},{2,10},{4,12},{6,14},{8,0},{10,2},{12,4},{14,6},{16,24},{18,... | collective-permute-start | bytes 442376 | tf_op jit(solution)/shard_map/ppermute | solution.py:103
  46.7 33.9 %collective-permute-start.11 = (bf16[1,48,1536]{2,1,0:T(8,128)(2,1)}, bf16[1,48,1536]{2,1,0:T(8,128)(2,1)S(1)}, u32[]{:S(2)}, u32[]{:S(2)}) collective-permute-start(bf16[1,48,1536]{2,1,0:T(8,128)(2,1)} %get-tuple-element.113.refs_0_), channel_id=1, source_target_pairs={{0,16},{2,18},{4,20},{6,22},{8,24},{10,26},{12,28},{14,30},{16,0},... | collective-permute-start | bytes 442376 | tf_op jit(solution)/shard_map/ppermute | solution.py:103
  49.4 31.3 %collective-permute-start.12 = (bf16[1,48,1536]{2,1,0:T(8,128)(2,1)}, bf16[1,48,1536]{2,1,0:T(8,128)(2,1)S(1)}, u32[]{:S(2)}, u32[]{:S(2)}) collective-permute-start(bf16[1,48,1536]{2,1,0:T(8,128)(2,1)} %get-tuple-element.113.refs_0_), channel_id=1, source_target_pairs={{0,24},{2,26},{4,28},{6,30},{8,16},{10,18},{12,20},{14,22},{16,8},... | collective-permute-start | bytes 442376 | tf_op jit(solution)/shard_map/ppermute | solution.py:103
  49.6 19.2 %collective-permute-start.8 = (bf16[8,48,1152]{2,1,0:T(8,128)(2,1)S(1)}, bf16[8,48,1152]{2,1,0:T(8,128)(2,1)S(1)}, u32[]{:S(2)}, u32[]{:S(2)}) collective-permute-start(bf16[8,48,1152]{2,1,0:T(8,128)(2,1)S(1)} %copy-done.11), channel_id=1, source_target_pairs={{0,4},{1,3},{2,6},{3,1},{4,0},{5,7},{6,2},{7,5},{8,12},{9,11},{10,... | collective-permute-start | bytes 2654216 | tf_op jit(solution)/shard_map/ppermute | solution.py:119
  50.1 15.5 %collective-permute-start.9 = (bf16[4,48,1536]{2,1,0:T(8,128)(2,1)}, bf16[4,48,1536]{2,1,0:T(8,128)(2,1)S(1)}, u32[]{:S(2)}, u32[]{:S(2)}) collective-permute-start(bf16[4,48,1536]{2,1,0:T(8,128)(2,1)} %get-tuple-element.106.refs_7_.refs_0_), channel_id=1, source_target_pairs={{0,2},{1,5},{2,0},{3,7},{4,6},{5,1},{6,4},{7,3},{8,10},{9,13},{10,... | collective-permute-start | bytes 1769480 | tf_op jit(solution)/shard_map/ppermute | solution.py:119
  68.8 26.5 %collective-permute-start.14 = (bf16[8,48,768]{2,1,0:T(8,128)(2,1)}, bf16[8,48,768]{2,1,0:T(8,128)(2,1)S(1)}, u32[]{:S(2)}, u32[]{:S(2)}) collective-permute-start(bf16[8,48,768]{2,1,0:T(8,128)(2,1)} %get-tuple-element.110.refs_7_), channel_id=1, source_target_pairs={{0,4},{1,3},{2,6},{3,1},{4,0},{5,7},{6,2},{7,5},{8,12},{9,11},{10,... | collective-permute-start | bytes 1769480 | tf_op jit(solution)/shard_map/ppermute | solution.py:119
  68.8 26.5 %collective-permute-start.15 = (bf16[8,48,768]{2,1,0:T(8,128)(2,1)}, bf16[8,48,768]{2,1,0:T(8,128)(2,1)S(1)}, u32[]{:S(2)}, u32[]{:S(2)}) collective-permute-start(bf16[8,48,768]{2,1,0:T(8,128)(2,1)} %get-tuple-element.111.refs_8_.refs_9_), channel_id=1, source_target_pairs={{0,4},{1,3},{2,6},{3,1},{4,0},{5,7},{6,2},{7,5},{8,12},{9,11},{10,... | collective-permute-start | bytes 1769480 | tf_op jit(solution)/shard_map/ppermute | solution.py:119
  105.4 33.8 %collective-permute-start.18 = (bf16[8,48,1536]{2,1,0:T(8,128)(2,1)S(1)}, bf16[8,48,1536]{2,1,0:T(8,128)(2,1)S(1)}, u32[]{:S(2)}, u32[]{:S(2)}) collective-permute-start(bf16[8,48,1536]{2,1,0:T(8,128)(2,1)S(1)} %copy-done.8), channel_id=1, source_target_pairs={{0,4},{1,3},{2,6},{3,1},{4,0},{5,7},{6,2},{7,5},{8,12},{9,11},{10,... | collective-permute-start | bytes 3538952 | tf_op jit(solution)/shard_map/ppermute | solution.py:119
  138.1 21.4 %collective-permute-start.17 = (bf16[8,48,1536]{2,1,0:T(8,128)(2,1)}, bf16[8,48,1536]{2,1,0:T(8,128)(2,1)S(1)}, u32[]{:S(2)}, u32[]{:S(2)}) collective-permute-start(bf16[8,48,1536]{2,1,0:T(8,128)(2,1)} %get-tuple-element.118), channel_id=1, source_target_pairs={{0,4},{1,3},{2,6},{3,1},{4,0},{5,7},{6,2},{7,5},{8,12},{9,11},{10,... | collective-permute-start | bytes 3538952 | tf_op jit(solution)/shard_map/ppermute | solution.py:119
  163.9 107.0 %collective-permute-start.19 = (bf16[2048,768]{1,0:T(8,128)(2,1)}, bf16[2048,768]{1,0:T(8,128)(2,1)S(1)}, u32[]{:S(2)}, u32[]{:S(2)}) collective-permute-start(bf16[2048,768]{1,0:T(8,128)(2,1)} %get-tuple-element.125.refs_0_), channel_id=1, source_target_pairs={{0,1},{1,0},{2,3},{3,2},{4,5},{5,4},{6,7},{7,6},{8,9},{9,8},{10,11... | collective-permute-start | bytes 9437192 | tf_op jit(solution)/shard_map/ppermute | solution.py:129
  164.4 24.0 %collective-permute-start.21 = (bf16[4,48,1536]{2,1,0:T(8,128)(2,1)}, bf16[4,48,1536]{2,1,0:T(8,128)(2,1)S(1)}, u32[]{:S(2)}, u32[]{:S(2)}) collective-permute-start(bf16[4,48,1536]{2,1,0:T(8,128)(2,1)} %get-tuple-element.134), channel_id=1, source_target_pairs={{0,2},{1,5},{2,0},{3,7},{4,6},{5,1},{6,4},{7,3},{8,10},{9,13},{10,... | collective-permute-start | bytes 1769480 | tf_op jit(solution)/shard_map/ppermute | solution.py:119
  187.4 26.9 %collective-permute-start.22 = (bf16[8,48,1920]{2,1,0:T(8,128)(2,1)}, bf16[8,48,1920]{2,1,0:T(8,128)(2,1)S(1)}, u32[]{:S(2)}, u32[]{:S(2)}) collective-permute-start(bf16[8,48,1920]{2,1,0:T(8,128)(2,1)} %get-tuple-element.143), channel_id=1, source_target_pairs={{0,4},{1,3},{2,6},{3,1},{4,0},{5,7},{6,2},{7,5},{8,12},{9,11},{10,... | collective-permute-start | bytes 4423688 | tf_op jit(solution)/shard_map/ppermute | solution.py:119
  191.5 22.7 %collective-permute-start.23 = (bf16[48,1536]{1,0:T(8,128)(2,1)}, bf16[48,1536]{1,0:T(8,128)(2,1)S(1)}, u32[]{:S(2)}, u32[]{:S(2)}) collective-permute-start(bf16[48,1536]{1,0:T(8,128)(2,1)} %get-tuple-element.144), channel_id=1, source_target_pairs={{0,8},{2,10},{4,12},{6,14},{8,0},{10,2},{12,4},{14,6},{16,24},{18,... | collective-permute-start | bytes 442376 | tf_op jit(solution)/shard_map/ppermute | solution.py:109
  192.3 22.0 %collective-permute-start.24 = (bf16[48,1536]{1,0:T(8,128)(2,1)}, bf16[48,1536]{1,0:T(8,128)(2,1)S(1)}, u32[]{:S(2)}, u32[]{:S(2)}) collective-permute-start(bf16[48,1536]{1,0:T(8,128)(2,1)} %get-tuple-element.145), channel_id=1, source_target_pairs={{0,16},{2,18},{4,20},{6,22},{8,24},{10,26},{12,28},{14,30},{16,0},... | collective-permute-start | bytes 442376 | tf_op jit(solution)/shard_map/ppermute | solution.py:109
  194.7 19.5 %collective-permute-start.25 = (bf16[48,1536]{1,0:T(8,128)(2,1)}, bf16[48,1536]{1,0:T(8,128)(2,1)S(1)}, u32[]{:S(2)}, u32[]{:S(2)}) collective-permute-start(bf16[48,1536]{1,0:T(8,128)(2,1)} %get-tuple-element.146), channel_id=1, source_target_pairs={{0,24},{2,26},{4,28},{6,30},{8,16},{10,18},{12,20},{14,22},{16,8},... | collective-permute-start | bytes 442376 | tf_op jit(solution)/shard_map/ppermute | solution.py:109
  246.5 14.4 %collective-permute-start.27 = (bf16[8,48,1280]{2,1,0:T(8,128)(2,1)}, bf16[8,48,1280]{2,1,0:T(8,128)(2,1)S(1)}, u32[]{:S(2)}, u32[]{:S(2)}) collective-permute-start(bf16[8,48,1280]{2,1,0:T(8,128)(2,1)} %get-tuple-element.155), channel_id=1, source_target_pairs={{0,4},{1,3},{2,6},{3,1},{4,0},{5,7},{6,2},{7,5},{8,12},{9,11},{10,... | collective-permute-start | bytes 2949128 | tf_op jit(solution)/shard_map/ppermute | solution.py:119
  264.8 37.5 %collective-permute-start.28 = (bf16[2048,768]{1,0:T(8,128)(2,1)}, bf16[2048,768]{1,0:T(8,128)(2,1)}, u32[]{:S(2)}, u32[]{:S(2)}) collective-permute-start(bf16[2048,768]{1,0:T(8,128)(2,1)} %get-tuple-element.159.refs_0_), channel_id=1, source_target_pairs={{0,1},{1,0},{2,3},{3,2},{4,5},{5,4},{6,7},{7,6},{8,9},{9,8},{10,11... | collective-permute-start | bytes 9437192 | tf_op jit(solution)/shard_map/ppermute | solution.py:129
  267.9 16.4 %collective-permute-start.34 = (bf16[48,1920]{1,0:T(8,128)(2,1)S(1)}, bf16[48,1920]{1,0:T(8,128)(2,1)S(1)}, u32[]{:S(2)}, u32[]{:S(2)}) collective-permute-start(bf16[48,1920]{1,0:T(8,128)(2,1)S(1)} %copy-done.22), channel_id=1, source_target_pairs={{0,16},{2,18},{4,20},{6,22},{8,24},{10,26},{12,28},{14,30},{16,0},... | collective-permute-start | bytes 552968 | tf_op jit(solution)/shard_map/ppermute | solution.py:109
  270.9 16.0 %collective-permute-start.35 = (bf16[48,1920]{1,0:T(8,128)(2,1)S(1)}, bf16[48,1920]{1,0:T(8,128)(2,1)S(1)}, u32[]{:S(2)}, u32[]{:S(2)}) collective-permute-start(bf16[48,1920]{1,0:T(8,128)(2,1)S(1)} %copy-done.21), channel_id=1, source_target_pairs={{0,24},{2,26},{4,28},{6,30},{8,16},{10,18},{12,20},{14,22},{16,8},... | collective-permute-start | bytes 552968 | tf_op jit(solution)/shard_map/ppermute | solution.py:109
  280.6 15.5 %collective-permute-start.31 = (bf16[48,1280]{1,0:T(8,128)(2,1)}, bf16[48,1280]{1,0:T(8,128)(2,1)S(1)}, u32[]{:S(2)}, u32[]{:S(2)}) collective-permute-start(bf16[48,1280]{1,0:T(8,128)(2,1)} %get-tuple-element.165), channel_id=1, source_target_pairs={{0,16},{2,18},{4,20},{6,22},{8,24},{10,26},{12,28},{14,30},{16,0},... | collective-permute-start | bytes 368648 | tf_op jit(solution)/shard_map/ppermute | solution.py:109
  (54 other events, 240.5 us)
